TPU v7x, 32 devices: a whole 2x2x4 slice. The times are simulated.
32 devices in a mesh: seq: 8 (over y, x, core), tp: 4 (over z).
Axes of the slice: x: 2, y: 2, z: 4, core: 2. Of those that a mesh axis runs over, the one named last changes fastest.
Arguments:
- short_inputs: bfloat16 [4, 2560, 1280], P(None, 'seq'), may hold values from -8 to 8
- long_inputs: bfloat16 [4, 12, 1280], replicated, may hold values from -8 to 8
- short_keys: bfloat16 [2560, 16, 1280], P('seq', None, 'tp'), may hold values from -6 to 6
- short_values: bfloat16 [2560, 16, 1280], P('seq', None, 'tp'), may hold values from -6 to 6
- long_keys: bfloat16 [12, 128, 1280], P(None, 'seq', 'tp'), may hold values from -6 to 6
- long_values: bfloat16 [12, 128, 1280], P(None, 'seq', 'tp'), may hold values from -6 to 6
- short_lengths: int32 [2560], P('seq'), may hold values from 1 to 16, as said below
- long_lengths: int32 [12], replicated, may hold values from 32 to 128, as said below
- attn_gain: float32 [1280], replicated, may hold values from 0.1 to 1.9
- mlp_gain: float32 [1280], replicated, may hold values from 0.1 to 1.9
- query_scale: float32 [16, 80], P('tp'), may hold values from 1 to 40, as said below
- q_weight: bfloat16 [1280, 1280], P(None, 'tp'), may hold values from -0.15625 to 0.15625
- k_weight: bfloat16 [1280, 1280], P(None, 'tp'), may hold values from -0.15625 to 0.15625
- v_weight: bfloat16 [1280, 1280], P(None, 'tp'), may hold values from -0.15625 to 0.15625
- o_weight: bfloat16 [1280, 1280], P('tp'), may hold values from -0.15625 to 0.15625
- up_weight: bfloat16 [1280, 1280], P(None, 'tp'), may hold values from -0.15625 to 0.15625
- down_weight: bfloat16 [1280, 1280], P('tp'), may hold values from -0.15625 to 0.15625
Outputs:
- short_outputs: bfloat16 [4, 2560, 1280], P(None, 'seq', 'tp')
- long_outputs: bfloat16 [4, 12, 1280], P(None, None, 'tp')
Inputs may be any that keep to these rules, and one draw needn't show every extreme that they name: `short_lengths`: some short request fills all 16 slots. `long_lengths`: some long request fills all 128 slots. `query_scale`: positive scales.
All inputs are finite; a program needn't handle non-finite values.
Results may differ from a plain program's by a relative error of at most 0.012.
The roundings to bfloat16 on the way count: a program that leaves them out, or rounds other values in their place, can miss the bound.
Values may be sent and summed in bfloat16 or wider, within the bound.
No kernel may reach another device: no remote copies, remote signals or barrier semaphores. Data moves between devices by JAX's collectives and lax.ppermute only.
A program may use at most 128 MiB of HBM per device.

v0:
```python
import jax
import jax.numpy as jnp
from jax import lax
from jax.sharding import PartitionSpec as P

norm_eps = 1e-06
masked_fill = -1e30


def rms_scale(matrix, gain_row):
    mean_square = jnp.sum(matrix * matrix, axis=-1, keepdims=True) / matrix.shape[-1]
    return matrix * lax.rsqrt(mean_square + norm_eps) * gain_row


def project_heads(flat_rows, weight, step_count, head_count):
    product = jnp.dot(flat_rows, weight, preferred_element_type=jnp.float32)
    return product.reshape(step_count, -1, head_count, product.shape[-1] // head_count)


def cache_partial(queries, cache_keys, cache_values, lengths, offset):
    request_count, slot_count = (cache_keys.shape[0], cache_keys.shape[1])
    head_count, head_dim = (queries.shape[2], queries.shape[3])
    keys_split = cache_keys.reshape(request_count, slot_count, head_count, head_dim)
    values_split = cache_values.reshape(request_count, slot_count, head_count, head_dim)
    scores = jnp.einsum("sbhd,bchd->sbhc", queries, keys_split, preferred_element_type=jnp.float32)
    slots = offset + jnp.arange(slot_count, dtype=jnp.int32)
    valid_slots = (slots[None, :] < lengths[:, None])[None, :, None, :]
    scores = jnp.where(valid_slots, scores, masked_fill)
    row_max = jnp.max(scores, axis=-1)
    probs = jnp.where(valid_slots, jnp.exp(scores - row_max[..., None]), 0.0)
    weight_sum = jnp.sum(probs, axis=-1)
    weighted = jnp.einsum(
        "sbhc,bchd->sbhd",
        probs.astype(jnp.bfloat16),
        values_split,
        preferred_element_type=jnp.float32,
    )
    return (row_max, weight_sum, weighted)


def add_fresh(queries, row_max, weight_sum, weighted, new_keys, new_values):
    step_count = queries.shape[0]
    causal = (jnp.arange(step_count)[None, :] <= jnp.arange(step_count)[:, None])[:, None, None, :]
    fresh_scores = jnp.einsum(
        "sbhd,tbhd->sbht", queries, new_keys, preferred_element_type=jnp.float32
    )
    fresh_scores = jnp.where(causal, fresh_scores, masked_fill)
    final_max = jnp.maximum(row_max, jnp.max(fresh_scores, axis=-1))
    rescale = jnp.exp(row_max - final_max)
    fresh_probs = jnp.where(causal, jnp.exp(fresh_scores - final_max[..., None]), 0.0)
    denominator = weight_sum * rescale + jnp.sum(fresh_probs, axis=-1)
    combined = weighted * rescale[..., None] + jnp.einsum(
        "sbht,tbhd->sbhd",
        fresh_probs.astype(jnp.bfloat16),
        new_values,
        preferred_element_type=jnp.float32,
    )
    return (combined / denominator[..., None]).astype(jnp.bfloat16)


def per_device(
    short_inputs,
    long_inputs,
    short_keys,
    short_values,
    long_keys,
    long_values,
    short_lengths,
    long_lengths,
    attn_gain,
    mlp_gain,
    query_scale,
    q_weight,
    k_weight,
    v_weight,
    o_weight,
    up_weight,
    down_weight,
):
    step_count, short_count, model_width = short_inputs.shape
    heads_local, head_dim = query_scale.shape
    share_width = model_width // lax.axis_size("tp")
    all_rows = jnp.concatenate([short_inputs, long_inputs], axis=1)
    flat_rows = all_rows.reshape(-1, model_width)
    normed = rms_scale(flat_rows.astype(jnp.float32), attn_gain).astype(jnp.bfloat16)
    queries = (
        project_heads(normed, q_weight, step_count, heads_local) * query_scale * head_dim ** (-0.5)
    ).astype(jnp.bfloat16)
    new_keys = project_heads(normed, k_weight, step_count, heads_local).astype(jnp.bfloat16)
    new_values = project_heads(normed, v_weight, step_count, heads_local).astype(jnp.bfloat16)
    short_max, short_sum, short_weighted = cache_partial(
        queries[:, :short_count], short_keys, short_values, short_lengths, 0
    )
    short_out = add_fresh(
        queries[:, :short_count],
        short_max,
        short_sum,
        short_weighted,
        new_keys[:, :short_count],
        new_values[:, :short_count],
    )
    long_offset = lax.axis_index("seq") * long_keys.shape[1]
    long_max, long_sum, long_weighted = cache_partial(
        queries[:, short_count:], long_keys, long_values, long_lengths, long_offset
    )
    global_max = lax.pmax(long_max, "seq")
    factor = jnp.exp(long_max - global_max)
    long_sum, long_weighted = lax.psum(
        (long_sum * factor, long_weighted * factor[..., None]), "seq"
    )
    long_max = global_max
    long_out = add_fresh(
        queries[:, short_count:],
        long_max,
        long_sum,
        long_weighted,
        new_keys[:, short_count:],
        new_values[:, short_count:],
    )
    attended = jnp.concatenate([short_out, long_out], axis=1).reshape(flat_rows.shape[0], -1)
    head_terms = jnp.dot(attended, o_weight, preferred_element_type=jnp.float32)
    col_start = lax.axis_index("tp") * share_width
    residual_mid = flat_rows.astype(jnp.float32) + lax.psum(head_terms, "tp")
    mid_share = lax.dynamic_slice_in_dim(residual_mid, col_start, share_width, 1)
    normed_mid = rms_scale(residual_mid, mlp_gain).astype(jnp.bfloat16)
    hidden_pre = jnp.dot(normed_mid, up_weight, preferred_element_type=jnp.float32)
    hidden = jax.nn.silu(hidden_pre).astype(jnp.bfloat16)
    down_terms = jnp.dot(hidden, down_weight, preferred_element_type=jnp.float32)
    output = mid_share + lax.psum_scatter(down_terms, "tp", scatter_dimension=1, tiled=True)
    output = output.astype(jnp.bfloat16).reshape(step_count, -1, share_width)
    return (output[:, :short_count], output[:, short_count:])


def solution(mesh):
    return jax.shard_map(
        per_device,
        mesh=mesh,
        in_specs=(
            P(None, "seq", None),
            P(),
            P("seq", None, "tp"),
            P("seq", None, "tp"),
            P(None, "seq", "tp"),
            P(None, "seq", "tp"),
            P("seq"),
            P(),
            P(),
            P(),
            P("tp", None),
            P(None, "tp"),
            P(None, "tp"),
            P(None, "tp"),
            P("tp", None),
            P(None, "tp"),
            P("tp", None),
        ),
        out_specs=(P(None, "seq", "tp"), P(None, None, "tp")),
        check_vma=False,
    )
```

profile of v0, /device:TPU:8, one launch (start us, length us, event | category | flops | bytes accessed | tf_op | source)
XLA Modules:
  0.0 556.9 jit_solution(6196157313265670975)
XLA Ops:
  7.3 0.9 iota_compare_fusion
  8.2 0.9 copy.137
  9.1 2.8 multiply_reduce_fusion
  12.1 0.8 reshape.201
  12.9 3.7 convolution_convert_fusion.1
  17.0 3.7 convolution_convert_fusion
  20.7 1.0 copy-done.5
  21.9 0.8 copy.160
  22.7 3.7 multiply_convert_fusion.3
  27.8 24.1 %pmax.7 = f32[4,12,4]{0,2,1:T(4,128)S(1)} all-reduce(f32[4,12,4]{0,2,1:T(4,128)S(1)} %get-tuple-element.28), channel_id=1, replica_groups=mesh['seq'=8,'tp'=4] {'seq'}, use_global_device_ids=true, to_apply=%region_6.7 | all-reduce | flops 192 | bytes 1536 | tf_op jit(solution)/shard_map/pmax | solution.py:106
  53.1 0.7 copy.162
  53.8 0.8 copy.161
  54.6 3.1 copy.139
  57.7 2.4 copy.148
  60.2 3.1 copy.143
  63.3 3.0 fusion.47
  66.3 2.3 copy.145
  68.6 0.8 fusion.25
  69.6 6.4 %copy.138 = bf16[320,16,320]{0,2,1:T(8,128)(2,1)} copy(bf16[320,16,320]{2,1,0:T(8,128)(2,1)} %param.19) | data formatting | bytes 6553600 | tf_op args[2]
  76.1 8.0 %copy.140 = bf16[320,16,4,80]{3,1,2,0:T(8,128)(2,1)} copy(bf16[320,16,4,80]{0,3,2,1:T(8,128)(2,1)} %bitcast.128) | data formatting | bytes 6553600 | tf_op jit(solution)/shard_map/reshape | solution.py:23
  84.1 5.6 %bitcast_reduce_fusion = (f32[4,320,4]{0,2,1:T(4,128)S(1)}, f32[320,4,4,16]{3,2,1,0:T(4,128)S(1)}) fusion(pred[320,16]{1,0:T(8,128)(4,1)S(1)} %iota_compare_fusion, bf16[4,320,4,80]{3,0,2,1:T(4,128)(2,1)S(1)} %copy.139, bf16[320,16,4,80]{3,1,2,0:T(8,128)(2,1)} %copy.140), kind=kOutput, calls=%fused_computation.14 | convolution fusion | flops 13265920 | bytes 4449280 | tf_op jit(solution)/shard_map/sbhd,bchd->sbhc/dot_general | solution.py:25
  89.7 3.5 fusion.8
  93.2 1.0 fusion.44
  95.0 1.1 copy.151
  96.2 1.7 copy.149
  97.9 6.4 %copy.141 = bf16[320,16,320]{0,2,1:T(8,128)(2,1)} copy(bf16[320,16,320]{2,1,0:T(8,128)(2,1)} %param.20) | data formatting | bytes 6553600 | tf_op args[3]
  104.3 8.1 %copy.142 = bf16[320,16,4,80]{3,1,2,0:T(8,128)(2,1)} copy(bf16[320,16,4,80]{0,3,2,1:T(8,128)(2,1)} %bitcast.129) | data formatting | bytes 6553600 | tf_op jit(solution)/shard_map/reshape | solution.py:24
  112.5 5.1 fusion.10
  117.6 0.9 fusion.19
  118.5 24.7 %all-reduce = (f32[4,12,4,80]{3,0,2,1:T(4,128)}, f32[4,12,4]{0,2,1:T(4,128)}) all-reduce(f32[4,12,4,80]{3,0,2,1:T(4,128)} %fusion.19, f32[4,12,4]{0,2,1:T(4,128)} %bitcast.147), channel_id=1, replica_groups=mesh['seq'=8,'tp'=4] {'seq'}, use_global_device_ids=true, to_apply=%region_7.8 | all-reduce | flops 15552 | bytes 124416 | tf_op jit(solution)/shard_map/psum | solution.py:108
  143.2 0.8 multiply_add_fusion
  143.9 1.1 fusion.21
  145.1 6.5 %fusion.7 = bf16[4,320,4,80]{3,0,2,1:T(4,128)(2,1)S(1)} fusion(f32[320,4,4,80]{3,2,1,0:T(4,128)} %fusion.10, bf16[4,320,4,80]{3,0,2,1:T(4,128)(2,1)S(1)} %copy-done.10, bf16[4,320,4,4]{3,0,2,1:T(4,128)(2,1)S(1)} %copy-done.11, f32[4,320,4]{0,2,1:T(4,128)} %copy.151, f32[4,320,4]{0,2,1:T(4,128)} %bitcast.139), kind=kOutput, calls=%fused_computation.17 | convolution fusion | flops 4915200 | bytes 3358720 | tf_op jit(solution)/shard_map/sbht,tbhd->sbhd/dot_general | solution.py:52
  151.7 1.1 pad_maximum_fusion
  152.7 1.6 copy.163
  154.3 0.7 reshape.202
  155.0 4.7 fusion.49
  159.8 0.8 copy-done.9
  160.6 6.0 %maximum_convert_fusion = f32[4,332,1280]{2,1,0:T(8,128)} fusion(bf16[4,12,1280]{2,1,0:T(8,128)(2,1)S(1)} %copy-done.9, bf16[4,320,1280]{2,1,0:T(8,128)(2,1)} %param.17), kind=kLoop, calls=%fused_computation.6 | loop fusion | flops 6799360 | bytes 10199040 | tf_op jit(solution)/shard_map/convert_element_type | solution.py:123
  166.7 5.1 reshape.204
  171.8 224.5 %all-reduce.3.cloned.1.call-done = f32[1328,1280]{1,0:T(8,128)} async-done(((f32[1328,1280]{1,0:T(8,128)}), f32[1328,1280]{1,0:T(8,128)}) %all-reduce.3.cloned.1.call-update) | async-done | bytes 6799376 | tf_op jit(solution)/shard_map/psum | solution.py:123
  396.3 8.4 %multiply_reduce_fusion.1 = (f32[1328]{0:T(1024)S(1)}, f32[1328,1280]{1,0:T(8,128)}) fusion(f32[1328,1280]{1,0:T(8,128)} %reshape.204, f32[1328,1280]{1,0:T(8,128)} %all-reduce.3.cloned.1.call-done), kind=kLoop, calls=%fused_computation.4 | loop fusion | flops 5098192 | bytes 20403392 | tf_op jit(solution)/shard_map/reduce_sum | solution.py:11
  404.7 9.7 %convolution_bitcast_fusion = f32[1280,1328]{1,0:T(8,128)} fusion(bf16[320,1280]{1,0:T(8,128)(2,1)S(1)} %copy-done.23, bf16[1280,320]{0,1:T(8,128)(2,1)S(1)} %copy-done.24, f32[1328,1280]{1,0:T(8,128)} %get-tuple-element.15, f32[1280]{0:T(1024)S(1)} %copy-done.26, f32[1328]{0:T(1024)S(1)} %add_rsqrt_fusion), kind=kOutput, calls=%fused_computation | convolution fusion | flops 2183019520 | bytes 15247552
  414.4 127.0 %reduce-scatter.4.cloned.1.call-done = f32[320,1328]{1,0:T(8,128)} async-done(((f32[1280,1328]{1,0:T(8,128)}), f32[320,1328]{1,0:T(8,128)}) %reduce-scatter.4.cloned.1.call-update) | async-done | bytes 1699856
  541.4 2.2 copy.172
  543.6 3.4 add_convert_fusion
  546.9 1.5 reshape.209
  548.4 1.0 slice.40
  (85 shorter events, 5.1 us)
Async XLA Ops:
  7.2 147.8 %copy-start = (bf16[320,1280]{1,0:T(8,128)(2,1)S(1)}, bf16[320,1280]{1,0:T(8,128)(2,1)}, u32[]{:S(2)}) copy-start(bf16[320,1280]{1,0:T(8,128)(2,1)} %param.31) | copy-start | bytes 2457604
  7.2 4.7 copy-start.13
  7.2 4.9 copy-start.14
  7.2 5.7 %copy-start.25 = (f32[1280]{0:T(1024)S(1)}, f32[1280]{0:T(1024)}, u32[]{:S(2)}) copy-start(f32[1280]{0:T(1024)} %param.25) | copy-start | bytes 15364
  7.2 389.1 %all-reduce.3.cloned.1.call-start = ((), (), s32[]{:S(2)}) async-start(), calls=%async_computation.1 | async-start | bytes 13598720 | tf_op jit(solution)/shard_map/psum | solution.py:123
  7.3 45.7 %copy-start.18 = (pred[4,4]{1,0:T(4,128)(4,1)}, pred[4,4]{1,0:T(4,128)(4,1)S(1)}, u32[]{:S(2)}) copy-start(pred[4,4]{1,0:T(4,128)(4,1)S(1)} %iota_compare_fusion.1) | copy-start | bytes 52
  9.1 13.5 %copy-start.8 = (bf16[4,12,1280]{2,1,0:T(8,128)(2,1)}, bf16[4,12,1280]{2,1,0:T(8,128)(2,1)S(1)}, u32[]{:S(2)}) copy-start(bf16[4,12,1280]{2,1,0:T(8,128)(2,1)S(1)} %copy.137) | copy-start | bytes 368644
  16.6 4.1 copy-start.4
  17.0 5.7 %copy-start.27 = (f32[4,80]{1,0:T(4,128)S(1)}, f32[4,80]{1,0:T(4,128)}, u32[]{:S(2)}) copy-start(f32[4,80]{1,0:T(4,128)} %param.27) | copy-start | bytes 3844
  20.7 1.0 copy-start.5
  22.7 4.8 copy-start.22
  26.4 28.2 %copy-start.7 = (bf16[4,332,4,80]{1,3,2,0:T(8,128)(2,1)}, bf16[4,332,4,80]{1,3,2,0:T(8,128)(2,1)S(1)}, u32[]{:S(2)}) copy-start(bf16[4,332,4,80]{1,3,2,0:T(8,128)(2,1)S(1)} %multiply_convert_fusion.3) | copy-start | bytes 2549764
  26.4 31.3 %copy-start.6 = (bf16[4,332,4,80]{1,3,2,0:T(8,128)(2,1)S(1)}, bf16[4,332,4,80]{1,3,2,0:T(8,128)(2,1)}, u32[]{:S(2)}) copy-start(bf16[4,332,4,80]{1,3,2,0:T(8,128)(2,1)} %copy-done.5) | copy-start | bytes 2549764
  27.5 32.7 %copy-start.20 = (pred[12,16]{1,0:T(8,128)(4,1)}, pred[12,16]{1,0:T(8,128)(4,1)S(1)}, u32[]{:S(2)}) copy-start(pred[12,16]{1,0:T(8,128)(4,1)S(1)} %broadcast_compare_fusion) | copy-start | bytes 580
  27.8 26.8 %copy-start.15 = (f32[4,12,4,16]{3,0,2,1:T(4,128)}, f32[4,12,4,16]{3,0,2,1:T(4,128)S(1)}, u32[]{:S(2)}) copy-start(f32[4,12,4,16]{3,0,2,1:T(4,128)S(1)} %get-tuple-element.29) | copy-start | bytes 36868
  89.7 4.6 copy-start.1
  89.7 4.6 copy-start.3
  93.2 1.3 copy-start.19
  104.3 8.1 %copy-start.2 = (f32[320,4,4,16]{3,2,1,0:T(4,128)S(1)}, f32[320,4,4,16]{3,2,1,0:T(4,128)}, u32[]{:S(2)}) copy-start(f32[320,4,4,16]{3,2,1,0:T(4,128)} %copy-done.1) | copy-start | bytes 983044
  112.5 5.1 copy-start.12
  112.5 5.1 copy-start.16
  112.5 5.1 copy-start.17
  112.5 5.1 copy-start.21
  117.6 27.5 %copy-start.10 = (bf16[4,320,4,80]{3,0,2,1:T(4,128)(2,1)S(1)}, bf16[4,320,4,80]{3,0,2,1:T(4,128)(2,1)}, u32[]{:S(2)}) copy-start(bf16[4,320,4,80]{3,0,2,1:T(4,128)(2,1)} %copy.148) | copy-start | bytes 2457604
  117.6 27.5 %copy-start.11 = (bf16[4,320,4,4]{3,0,2,1:T(4,128)(2,1)S(1)}, bf16[4,320,4,4]{3,0,2,1:T(4,128)(2,1)}, u32[]{:S(2)}) copy-start(bf16[4,320,4,4]{3,0,2,1:T(4,128)(2,1)} %copy.149) | copy-start | bytes 122884
  159.7 0.9 copy-start.9
  159.7 381.7 %reduce-scatter.4.cloned.1.call-start = ((), (), s32[]{:S(2)}) async-start(), calls=%async_computation.2 | async-start | bytes 9011200
  171.8 232.9 %copy-start.23 = (bf16[320,1280]{1,0:T(8,128)(2,1)S(1)}, bf16[320,1280]{1,0:T(8,128)(2,1)}, u32[]{:S(2)}) copy-start(bf16[320,1280]{1,0:T(8,128)(2,1)} %param.33) | copy-start | bytes 2457604
  171.8 232.9 %copy-start.24 = (bf16[1280,320]{0,1:T(8,128)(2,1)S(1)}, bf16[1280,320]{0,1:T(8,128)(2,1)}, u32[]{:S(2)}) copy-start(bf16[1280,320]{0,1:T(8,128)(2,1)} %param.32) | copy-start | bytes 2457604
  171.8 232.9 %copy-start.26 = (f32[1280]{0:T(1024)S(1)}, f32[1280]{0:T(1024)}, u32[]{:S(2)}) copy-start(f32[1280]{0:T(1024)} %param.26) | copy-start | bytes 15364
Sparse Core Ops, SparseCore 0:
  159.8 236.4 all-reduce.2
  414.6 126.8 reduce-scatter.3
where the time goes:
time: 560 us; the launch traced here: 557 us
  waiting for transfers between devices  352 us (63%)
  local copies, waits for them, and re-layouts  63.9 us (11%)
  blocking collectives  48.8 us (9%)
  matrix products  48.2 us (9%)
  other arithmetic  30 us (5%)
  between operations  14.5 us (3%)
    psum x1, waiting for transfers between devices, per_device(): residual_mid = flat_rows.astype(jnp.float32) + lax.psum(head_terms, 'tp')  225 us
    unnamed x3, waiting for transfers between devices  127 us
    psum x1, blocking collectives, per_device(): lax.psum((long_sum * factor, long_weighted * factor[..., None]), 'seq')  24.7 us
    pmax x1, blocking collectives, per_device(): global_max = lax.pmax(long_max, 'seq')  24.1 us
    unnamed x61, local copies, waits for them, and re-layouts  18.6 us
  transfers between devices with their start and end apart: 2, of which 2 were waited for; matrix products, arithmetic and copies ran while one was open for 2% of the time, Pallas kernels for 0%

commit v1 on v0

v1 whole, which is shorter than its diff:
```python
import functools

import jax
import jax.numpy as jnp
from jax import lax
from jax.experimental import pallas as pl
from jax.experimental.pallas import tpu as pltpu
from jax.sharding import PartitionSpec as P

norm_eps = 1e-06
masked_fill = -1e30
GROUP = 16
F32 = jnp.float32
BF16 = jnp.bfloat16
MIB = 1024 * 1024


def rms_scale(rows, gain_row):
    mean_square = jnp.sum(rows * rows, axis=-1, keepdims=True) / rows.shape[-1]
    return (rows * lax.rsqrt(mean_square + norm_eps) * gain_row).astype(BF16)


def dot(a, b):
    return jnp.dot(a, b, preferred_element_type=F32)


def dot_t(a, b):
    return lax.dot_general(a, b, (((1,), (1,)), ((), ())), preferred_element_type=F32)


def lane_heads(rows, width, heads):
    return lax.broadcasted_iota(jnp.int32, (rows, width), 1) // (width // heads)


def stack_heads(queries, heads):
    head_of = lane_heads(*queries.shape, heads)
    return jnp.concatenate([jnp.where(head_of == h, queries, jnp.zeros_like(queries)) for h in range(heads)], axis=0)


def pick_heads(stacked, heads, width):
    n = stacked.shape[0] // heads
    head_of = lane_heads(n, width, heads)
    picked = jnp.broadcast_to(stacked[:n], (n, width))
    for h in range(1, heads):
        picked = jnp.where(head_of == h, stacked[h * n : (h + 1) * n], picked)
    return picked


def slot_bias(lens, slots, columns):
    at = lax.broadcasted_iota(jnp.int32, (GROUP, columns), 1) - slots * lax.broadcasted_iota(jnp.int32, (GROUP, columns), 0)
    return jnp.where((at >= 0) & (at < lens), 0.0, masked_fill)


def fresh_bias(steps):
    n = steps * GROUP
    row = lax.broadcasted_iota(jnp.int32, (n, n), 0)
    col = lax.broadcasted_iota(jnp.int32, (n, n), 1)
    seen = (row % GROUP == col % GROUP) & (col // GROUP <= row // GROUP)
    return jnp.where(seen, 0.0, masked_fill)


def add_rows(scores, bias):
    reps = scores.shape[0] // bias.shape[0]
    return (scores.reshape(reps, *bias.shape) + bias[None]).reshape(scores.shape)


def pick_lens(len_row, base):
    lane = lax.broadcasted_iota(jnp.int32, (GROUP, len_row.shape[1]), 1)
    row = lax.broadcasted_iota(jnp.int32, (GROUP, len_row.shape[1]), 0)
    return jnp.sum(jnp.where(lane == base + row, len_row, 0), axis=1, keepdims=True)


def qkv_rows(normed, qw_ref, kw_ref, vw_ref, scale_row, inv):
    queries = (dot(normed, qw_ref[...]) * scale_row * inv).astype(BF16)
    return queries, dot(normed, kw_ref[...]).astype(BF16), dot(normed, vw_ref[...]).astype(BF16)


def scale_lanes(scale_ref):
    return jnp.concatenate([scale_ref[h : h + 1, :] for h in range(scale_ref.shape[0])], axis=1)


def long_kernel(at_ref, x_ref, k_ref, v_ref, len_ref, gain_ref, scale_ref, qw_ref, kw_ref, vw_ref, part_ref, q_ref, kn_ref, vn_ref, rows_ref):
    steps, count, model = x_ref.shape
    heads, head_dim = scale_ref.shape
    width = heads * head_dim
    slots = k_ref.shape[1]
    rows_ref[...] = jnp.zeros_like(rows_ref)
    for s in range(steps):
        rows_ref[s * GROUP : s * GROUP + count, :] = x_ref[s].astype(F32)
    normed = rms_scale(rows_ref[...], gain_ref[...])
    q, kn, vn = qkv_rows(normed, qw_ref, kw_ref, vw_ref, scale_lanes(scale_ref), head_dim**-0.5)
    q_ref[...] = q
    kn_ref[...] = kn
    vn_ref[...] = vn
    lens = jnp.minimum(pick_lens(len_ref[...], 0) - at_ref[0] * slots, slots)
    keys = k_ref[...].reshape(count * slots, width)
    values = v_ref[...].reshape(count * slots, width)
    bias = slot_bias(lens, slots, count * slots)
    scores = add_rows(dot_t(stack_heads(q, heads), keys), bias)
    row_max = jnp.max(scores, axis=1, keepdims=True)
    probs = jnp.where(scores > 0.5 * masked_fill, jnp.exp(scores - row_max), 0.0)
    weight_sum = jnp.sum(probs, axis=1, keepdims=True)
    acc = pick_heads(dot(probs.astype(BF16), values), heads, width)
    n = steps * GROUP
    part_ref[:, :width] = acc
    lane = lax.broadcasted_iota(jnp.int32, (n, part_ref.shape[1] - width), 1)
    tail = jnp.zeros(lane.shape, F32)
    for h in range(heads):
        tail = jnp.where(lane == h, row_max[h * n : (h + 1) * n], tail)
        tail = jnp.where(lane == heads + h, weight_sum[h * n : (h + 1) * n], tail)
    part_ref[:, width:] = tail


def merge_long(my_seq, parts, held_ref, q, kn, vn, heads):
    n, width = q.shape
    for i, part in enumerate(parts):
        held_ref[my_seq ^ i] = part[...]
    scores = add_rows(dot_t(stack_heads(q, heads), kn), fresh_bias(n // GROUP))
    total_max = jnp.max(scores, axis=1, keepdims=True)

    def column(i, first):
        return jnp.concatenate([held_ref[i, :, first + h : first + h + 1] for h in range(heads)], axis=0)

    for i in range(len(parts)):
        total_max = jnp.maximum(total_max, column(i, width))
    probs = jnp.exp(scores - total_max)
    denom = jnp.sum(probs, axis=1, keepdims=True)
    acc = pick_heads(dot(probs.astype(BF16), vn), heads, width)
    for i in range(len(parts)):
        factor = jnp.exp(column(i, width) - total_max)
        denom = denom + factor * column(i, width + heads)
        acc = acc + held_ref[i, :, :width] * pick_heads(factor, heads, width)
    return (acc / pick_heads(denom, heads, width)).astype(BF16)


def short_kernel(n_parts, first, at_ref, x_ref, k_ref, v_ref, len_ref, gain_ref, scale_ref, qw_ref, kw_ref, vw_ref, *refs):
    parts, refs = refs[:n_parts], refs[n_parts:]
    if n_parts:
        longs, refs = refs[:3], refs[3:]
    steps, block, model = x_ref.shape
    heads, head_dim = scale_ref.shape
    width = heads * head_dim
    slots = k_ref.shape[1]
    outs, att_ref = refs[:steps], refs[steps]
    n = steps * GROUP
    i = pl.program_id(0)
    normed = rms_scale(x_ref[...].reshape(steps * block, model).astype(F32), gain_ref[...])
    q, kn, vn = qkv_rows(normed, qw_ref, kw_ref, vw_ref, scale_lanes(scale_ref), head_dim**-0.5)
    late = fresh_bias(steps)
    for sub in range(block // GROUP):
        lo, hi = sub * GROUP, (sub + 1) * GROUP

        def take(rows):
            return jnp.concatenate([rows[s * block + lo : s * block + hi] for s in range(steps)], axis=0)

        keys = k_ref[lo:hi].reshape(GROUP * slots, width)
        values = v_ref[lo:hi].reshape(GROUP * slots, width)
        lens = pick_lens(len_ref[...], first + i * block + lo)
        stacked = stack_heads(take(q), heads)
        scores = add_rows(dot_t(stacked, keys), slot_bias(lens, slots, GROUP * slots))
        fresh = add_rows(dot_t(stacked, take(kn)), late)
        row_max = jnp.maximum(jnp.max(scores, axis=1, keepdims=True), jnp.max(fresh, axis=1, keepdims=True))
        probs = jnp.exp(scores - row_max)
        fresh_probs = jnp.exp(fresh - row_max)
        denom = jnp.sum(probs, axis=1, keepdims=True) + jnp.sum(fresh_probs, axis=1, keepdims=True)
        weighted = dot(probs.astype(BF16), values) + dot(fresh_probs.astype(BF16), take(vn))
        out = (pick_heads(weighted, heads, width) / pick_heads(denom, heads, width)).astype(BF16)
        start = pl.multiple_of(i * block + lo, GROUP)
        for s in range(steps):
            att_ref[s, pl.ds(start, GROUP), :] = out[s * GROUP : (s + 1) * GROUP]

    @pl.when(i == pl.num_programs(0) - 1)
    def _():
        half = att_ref.shape[1] // 2
        if n_parts:
            long_ref, held_ref = refs[steps + 1], refs[steps + 2]
            merged = merge_long(at_ref[0], parts, held_ref, longs[0][...], longs[1][...], longs[2][...], heads)
            for s in range(steps):
                long_ref[s] = merged[s * GROUP : (s + 1) * GROUP]
        for k in range(steps):
            rows = att_ref[at_ref[1] ^ k]
            outs[k][:half, :] = jnp.concatenate([rows[:half], rows[half:]], axis=1)
            if n_parts:
                mine = long_ref[at_ref[1] ^ k]
                outs[k][half:, :] = jnp.concatenate([mine, jnp.zeros_like(mine)], axis=1)


def pack_kernel(at_ref, o_ref, up_ref, down_ref, out_ref):
    rows = o_ref.shape[0]
    out_ref[:rows, :] = o_ref[...]
    out_ref[rows : 2 * rows, :] = jnp.concatenate([up_ref[:rows, :], up_ref[rows:, :]], axis=1)
    out_ref[2 * rows :, :] = down_ref[...]


def unpack_kernel(tp, at_ref, own_o, own_up, own_down, *refs):
    o_ref, up_ref, down_ref = refs[-3:]
    width = own_o.shape[0]
    rows, lanes = refs[0].shape[0] // 3, refs[0].shape[1]
    mine = at_ref[0] % 8
    o_ref[:width, :] = own_o[...]
    up_ref[:, :width] = own_up[...]
    down_ref[:width, :] = own_down[...]
    for k in range(1, tp):
        for m in range(8):
            piece_ref = refs[(k - 1) * 8 + m]
            piece = mine ^ m
            row = pl.multiple_of(k * width + (piece // 2) * rows, 16)
            lane = pl.multiple_of((piece % 2) * lanes, 128)
            o_ref[pl.ds(row, rows), pl.ds(lane, lanes)] = piece_ref[:rows, :]
            down_ref[pl.ds(row, rows), pl.ds(lane, lanes)] = piece_ref[2 * rows :, :]
            both = piece_ref[rows : 2 * rows, :]
            top = pl.multiple_of(piece * 2 * rows, 16)
            up_ref[pl.ds(top, rows), k * width : (k + 1) * width] = both[:, : lanes // 2]
            up_ref[pl.ds(top + rows, rows), k * width : (k + 1) * width] = both[:, lanes // 2 :]


def mlp_kernel(with_long, tp, at_ref, x_ref, *refs):
    if with_long:
        xl_ref, refs = refs[0], refs[1:]
    gain_ref, atts, (o_ref, up_ref, down_ref) = refs[0], refs[1 : 1 + tp], refs[1 + tp : 4 + tp]
    outs, refs = refs[4 + tp : 4 + 2 * tp], refs[4 + 2 * tp :]
    half = x_ref.shape[1] // 2
    width = o_ref.shape[0] // tp
    x = x_ref[0].astype(F32)
    if with_long:
        xs_ref = refs[1]
        count = xl_ref.shape[1]
        xs_ref[...] = jnp.zeros_like(xs_ref)
        xs_ref[:count, :] = xl_ref[0].astype(F32)
        x = jnp.concatenate([x, xs_ref[...]], axis=0)

    def rows_of(piece):
        blocks = [piece[:half, :width], piece[:half, width:]]
        if with_long:
            blocks.append(piece[half:, :width])
        return jnp.concatenate(blocks, axis=0)

    attended = jnp.concatenate([rows_of(piece[...]) for piece in atts], axis=1)
    mid = x + dot(attended, o_ref[...])
    normed = rms_scale(mid, gain_ref[...])
    pre = dot(normed, up_ref[...])
    hidden = (pre * (0.5 + 0.5 * jnp.tanh(0.5 * pre))).astype(BF16)
    out = mid + dot(hidden, down_ref[...])
    out = out.astype(BF16)
    cols_ref = refs[0]
    for b in range(tp):
        cols = out[:, b * width : (b + 1) * width]
        cols_ref[b, :half, :] = jnp.concatenate([cols[:half], cols[half : 2 * half]], axis=1)
        if with_long:
            tail = cols[2 * half :]
            cols_ref[b, half:, :] = jnp.concatenate([tail, jnp.zeros_like(tail)], axis=1)
    for k in range(tp):
        outs[k][...] = cols_ref[at_ref[1] ^ k]


def place_kernel(tp, at_ref, *refs):
    early, late, (short_ref, long_ref) = refs[:tp], refs[tp : 2 * tp], refs[2 * tp :]
    half = early[0].shape[0]
    width = short_ref.shape[2]
    count = long_ref.shape[1]
    for k in range(tp):
        step = at_ref[1] ^ k
        for c, piece in enumerate((early[k], late[k])):
            short_ref[step, 2 * c * half : (2 * c + 1) * half, :] = piece[:half, :width]
            short_ref[step, (2 * c + 1) * half : (2 * c + 2) * half, :] = piece[:half, width:]
        long_ref[step] = late[k][half:, :width][:count]


def swap(value, axis, k):
    size = lax.axis_size(axis)
    return lax.ppermute(value, axis, [(i, i ^ k) for i in range(size)])


def whole(array):
    return pl.BlockSpec(array.shape, lambda *_: (0,) * array.ndim)


def call(kernel, at, operands, outs, specs=None, grid=(1,), scratch=(), limit=48, flops=0, name=None):
    specs = specs or {}
    return pl.pallas_call(
        kernel,
        grid_spec=pltpu.PrefetchScalarGridSpec(
            num_scalar_prefetch=1,
            grid=grid,
            in_specs=[specs.get(i, whole(a)) for i, a in enumerate(operands)],
            out_specs=[whole(o) for o in outs],
            scratch_shapes=list(scratch),
        ),
        out_shape=list(outs),
        compiler_params=pltpu.CompilerParams(vmem_limit_bytes=limit * MIB),
        cost_estimate=pl.CostEstimate(flops=flops, bytes_accessed=sum(a.size * a.dtype.itemsize for a in (*operands, *outs)), transcendentals=0),
        name=name,
    )(at, *operands)


def per_device(
    short_inputs,
    long_inputs,
    short_keys,
    short_values,
    long_keys,
    long_values,
    short_lengths,
    long_lengths,
    attn_gain,
    mlp_gain,
    query_scale,
    q_weight,
    k_weight,
    v_weight,
    o_weight,
    up_weight,
    down_weight,
):
    steps, count, model = short_inputs.shape
    long_count = long_inputs.shape[1]
    heads, head_dim = query_scale.shape
    width = heads * head_dim
    tp, seq = lax.axis_size("tp"), lax.axis_size("seq")
    slots = short_keys.shape[1]
    at = jnp.stack([lax.axis_index("seq"), lax.axis_index("tp")]).astype(jnp.int32)
    shape = jax.ShapeDtypeStruct
    attn_gain, mlp_gain = attn_gain[None], mlp_gain[None]
    short_len, long_len = short_lengths[None], long_lengths[None]

    rows, lanes = width // 4, model // 2
    (own,) = call(
        pack_kernel,
        at,
        (o_weight, up_weight, down_weight),
        (shape((3 * rows, lanes), BF16),),
        specs={
            0: pl.BlockSpec((rows, lanes), lambda _, at: ((at[0] % 8) // 2, at[0] % 2)),
            1: pl.BlockSpec((2 * rows, width), lambda _, at: (at[0] % 8, 0)),
            2: pl.BlockSpec((rows, lanes), lambda _, at: ((at[0] % 8) // 2, at[0] % 2)),
        },
        name="pack_weights",
    )
    pieces = []
    for k in range(1, tp):
        mine = swap(own, "tp", k)
        same_core = [mine] + [swap(mine, "seq", j) for j in (2, 4, 6)]
        other_core = [swap(piece, "seq", 1) for piece in same_core]
        pieces += [piece for pair in zip(same_core, other_core) for piece in pair]
    weights = call(
        functools.partial(unpack_kernel, tp),
        at,
        (o_weight, up_weight, down_weight, *pieces),
        (shape((tp * width, model), BF16), shape((model, tp * width), BF16), shape((tp * width, model), BF16)),
        name="unpack_weights",
    )

    n = steps * GROUP
    part, long_q, long_kn, long_vn = call(
        long_kernel,
        at,
        (long_inputs, long_keys, long_values, long_len, attn_gain, query_scale, q_weight, k_weight, v_weight),
        (shape((n, width + 64), F32),) + (shape((n, width), BF16),) * 3,
        scratch=(pltpu.VMEM((n, model), F32),),
        flops=2 * n * model * width * 3,
        name="long_partial",
    )
    parts = [part] + [swap(part, "seq", i) for i in range(1, seq)]

    half = count // 2
    block = 32
    tall = half // 2

    def attend(chunk, extra, extra_rows, scratch):
        first = chunk * (half // block)
        return call(
            functools.partial(short_kernel, max(0, len(extra) - 3), chunk * half),
            at,
            (short_inputs, short_keys, short_values, short_len, attn_gain, query_scale, q_weight, k_weight, v_weight, *extra),
            (shape((tall + extra_rows, 2 * width), BF16),) * steps,
            specs={
                0: pl.BlockSpec((steps, block, model), lambda i, at: (0, first + i, 0)),
                1: pl.BlockSpec((block, slots, width), lambda i, at: (first + i, 0, 0)),
                2: pl.BlockSpec((block, slots, width), lambda i, at: (first + i, 0, 0)),
            },
            grid=(half // block,),
            scratch=(pltpu.VMEM((steps, half, width), BF16), *scratch),
            flops=2 * steps * half * model * width * 3,
            name="short_attention",
        )

    early = attend(0, (), 0, ())
    early = [early[0]] + [swap(early[k], "tp", k) for k in range(1, tp)]
    late = attend(
        1,
        (*parts, long_q, long_kn, long_vn),
        GROUP,
        (pltpu.VMEM((steps, GROUP, width), BF16), pltpu.VMEM((seq, n, width + 64), F32)),
    )
    late = [late[0]] + [swap(late[k], "tp", k) for k in range(1, tp)]

    def feed_forward(chunk, pieces):
        with_long = chunk == 1
        extra = (long_inputs,) if with_long else ()
        total = half + GROUP * with_long
        specs = {0: pl.BlockSpec((1, half, model), lambda _, at: (at[1], chunk, 0))}
        if with_long:
            specs[1] = pl.BlockSpec((1, long_count, model), lambda _, at: (at[1], 0, 0))
        outs = call(
            functools.partial(mlp_kernel, with_long, tp),
            at,
            (short_inputs, *extra, mlp_gain, *pieces, *weights),
            (shape(pieces[0].shape, BF16),) * tp,
            specs=specs,
            scratch=(pltpu.VMEM((tp, *pieces[0].shape), BF16),) + ((pltpu.VMEM((GROUP, model), F32),) if with_long else ()),
            flops=2 * total * model * model * 3,
            name="feed_forward",
        )
        return [outs[0]] + [swap(outs[k], "tp", k) for k in range(1, tp)]

    early = feed_forward(0, early)
    late = feed_forward(1, late)
    return tuple(
        call(
            functools.partial(place_kernel, tp),
            at,
            (*early, *late),
            (shape((steps, count, width), BF16), shape((steps, long_count, width), BF16)),
            name="place_outputs",
        )
    )


def solution(mesh):
    return jax.shard_map(
        per_device,
        mesh=mesh,
        in_specs=(
            P(None, "seq", None),
            P(),
            P("seq", None, "tp"),
            P("seq", None, "tp"),
            P(None, "seq", "tp"),
            P(None, "seq", "tp"),
            P("seq"),
            P(),
            P(),
            P(),
            P("tp", None),
            P(None, "tp"),
            P(None, "tp"),
            P(None, "tp"),
            P("tp", None),
            P(None, "tp"),
            P("tp", None),
        ),
        out_specs=(P(None, "seq", "tp"), P(None, None, "tp")),
        check_vma=False,
    )
```

time: 560 us -> 157 us (0.28)
  waiting for transfers between devices: 352 us -> 49.4 us
  local copies, waits for them, and re-layouts: 63.9 us -> 9.61 us
  Pallas kernels: 0 us -> 49.1 us
  blocking collectives: 48.8 us -> 0 us
  matrix products: 48.2 us -> 0 us
  starting transfers between devices: 0.08 us -> 45.9 us
  other arithmetic: 30 us -> 0.08 us
  between operations: 14.5 us -> 0.95 us
    psum x1 -> x0, waiting for transfers between devices: 225 us -> none  [per_device(): residual_mid = flat_rows.astype(jnp.float32) + lax.psum(head_terms, 'tp')]
    unnamed x3 -> x0, waiting for transfers between devices: 127 us -> none
    ppermute x0 -> x43, waiting for transfers between devices: none -> 49.4 us  [swap(): return lax.ppermute(value, axis, [(i, i ^ k) for i in range(size)])]
    pallas_call x0 -> x8, Pallas kernels: none -> 49.1 us  [call(): pl.pallas_call(kernel, grid_spec=pltpu.PrefetchScalarGridSpec(num_scalar_...]
    ppermute x0 -> x43, starting transfers between devices: none -> 45.9 us  [swap(): return lax.ppermute(value, axis, [(i, i ^ k) for i in range(size)])]
    dot_general x12 -> x0, matrix products: 38.5 us -> none  [the longest x3 11.1 us: project_heads(): product = jnp.dot(flat_rows, weight, preferred_element_type=jnp.float32)]
    psum x1 -> x0, blocking collectives: 24.7 us -> none  [per_device(): lax.psum((long_sum * factor, long_weighted * factor[..., None]), 'seq')]
    pmax x1 -> x0, blocking collectives: 24.1 us -> none  [per_device(): global_max = lax.pmax(long_max, 'seq')]
  transfers between devices with their start and end apart: 2 -> 43, of which waited for: 2 -> 14; matrix products, arithmetic and copies ran while one was open for 2% -> 2% of each run, Pallas kernels for 0% -> 30%
where the time goes in v1:
time: 157 us; the launch traced here: 155 us
  waiting for transfers between devices  49.4 us (31%)
  Pallas kernels  49.1 us (31%)
  starting transfers between devices  45.9 us (29%)
  local copies, waits for them, and re-layouts  9.61 us (6%)
    ppermute x43, waiting for transfers between devices, swap(): return lax.ppermute(value, axis, [(i, i ^ k) for i in range(size)])  49.4 us
    pallas_call x8, Pallas kernels, call(): pl.pallas_call(kernel, grid_spec=pltpu.PrefetchScalarGridSpec(num_scalar_...  49.1 us
    ppermute x43, starting transfers between devices, swap(): return lax.ppermute(value, axis, [(i, i ^ k) for i in range(size)])  45.9 us
    unnamed x41, local copies, waits for them, and re-layouts  8.97 us
  transfers between devices with their start and end apart: 43, of which 14 were waited for; matrix products, arithmetic and copies ran while one was open for 2% of the time, Pallas kernels for 30%

profile of v1, /device:TPU:8, one launch (start us, length us, event | category | flops | bytes accessed | tf_op | source)
XLA Modules:
  0.0 155.1 jit_solution(1472272168363192580)
XLA Ops:
  0.7 1.7 %copy.23.up_ref.own_up = bf16[1280,320]{1,0:T(8,128)(2,1)S(1)} copy(bf16[1280,320]{0,1:T(8,128)(2,1)} %param.32) | data formatting | bytes 1638400 | tf_op args[15]
  2.5 1.4 copy-done.2
  3.9 1.1 copy-done.3
  5.0 1.4 pack_weights.1
  6.4 1.6 %collective-permute-start.19 = (bf16[240,640]{1,0:T(8,128)(2,1)}, bf16[240,640]{1,0:T(8,128)(2,1)S(1)}, u32[]{:S(2)}, u32[]{:S(2)}) collective-permute-start(bf16[240,640]{1,0:T(8,128)(2,1)} %pack_weights.1), channel_id=1, source_target_pairs={{0,3},{1,2},{2,1},{3,0},{4,7},{5,6},{6,5},{7,4},{8,11},{9,10},{10,... | collective-permute-start | bytes 921608 | tf_op jit(solution)/shard_map/ppermute | solution.py:271
  8.0 1.0 collective-permute-start.11
  10.4 1.6 %copy.21.vw_ref = bf16[1280,320]{1,0:T(8,128)(2,1)S(1)} copy(bf16[1280,320]{0,1:T(8,128)(2,1)} %param.30) | data formatting | bytes 1638400 | tf_op args[13]
  12.0 0.9 copy-done.4
  12.9 0.9 copy-done.5
  13.8 1.6 %long_partial.1 = (f32[64,384]{1,0:T(8,128)S(1)}, bf16[64,320]{1,0:T(8,128)(2,1)S(1)}, bf16[64,320]{1,0:T(8,128)(2,1)S(1)}, bf16[64,320]{1,0:T(8,128)(2,1)S(1)}) custom-call(s32[2]{0:T(128)S(1)} %pad_add_fusion.at_ref, bf16[4,12,1280]{2,1,0:T(8,128)(2,1)S(1)} %copy.31.x_ref.refs_0_, bf16[12,16,320]{2,1,0:T(8,128)(2,1)S(1)} %copy-done.4, ...), custom_call_target="tpu_custom_call" | custom-call | flops 157286400 | bytes 3053872 | tf_op jit(solution)/shard_map/long_partial/pallas_call | solution.py:280
  15.4 1.7 %collective-permute-start.36 = (f32[64,384]{1,0:T(8,128)S(1)}, f32[64,384]{1,0:T(8,128)S(1)}, u32[]{:S(2)}, u32[]{:S(2)}) collective-permute-start(f32[64,384]{1,0:T(8,128)S(1)} %get-tuple-element.36.refs_0_), channel_id=1, source_target_pairs={{0,28},{4,24},{8,20},{12,16},{16,12},{20,8},{24,4},{28,0},{1,29},{... | collective-permute-start | bytes 294920 | tf_op jit(solution)/shard_map/ppermute | solution.py:271
  17.1 1.1 collective-permute-start.35
  18.2 1.4 collective-permute-start.34
  19.6 1.6 %collective-permute-done.36.refs_7_ = f32[64,384]{1,0:T(8,128)S(1)} collective-permute-done((f32[64,384]{1,0:T(8,128)S(1)}, f32[64,384]{1,0:T(8,128)S(1)}, u32[]{:S(2)}, u32[]{:S(2)}) %collective-permute-start.36) | collective-permute-done | bytes 98336 | tf_op jit(solution)/shard_map/ppermute | solution.py:271
  21.1 2.1 %collective-permute-start.33 = (f32[64,384]{1,0:T(8,128)S(1)}, f32[64,384]{1,0:T(8,128)S(1)}, u32[]{:S(2)}, u32[]{:S(2)}) collective-permute-start(f32[64,384]{1,0:T(8,128)S(1)} %get-tuple-element.36.refs_0_), channel_id=1, source_target_pairs={{0,16},{4,20},{8,24},{12,28},{16,0},{20,4},{24,8},{28,12},{1,17},{... | collective-permute-start | bytes 294920 | tf_op jit(solution)/shard_map/ppermute | solution.py:271
  23.5 0.9 collective-permute-start.32
  24.4 1.3 collective-permute-done.34.refs_5_
  25.7 1.4 collective-permute-start.3
  27.1 2.6 %collective-permute-done.19.refs_16_ = bf16[240,640]{1,0:T(8,128)(2,1)S(1)} collective-permute-done((bf16[240,640]{1,0:T(8,128)(2,1)}, bf16[240,640]{1,0:T(8,128)(2,1)S(1)}, u32[]{:S(2)}, u32[]{:S(2)}) %collective-permute-start.19) | collective-permute-done | bytes 307232 | tf_op jit(solution)/shard_map/ppermute | solution.py:271
  29.7 2.4 %collective-permute-start.25 = (bf16[240,640]{1,0:T(8,128)(2,1)S(1)}, bf16[240,640]{1,0:T(8,128)(2,1)S(1)}, u32[]{:S(2)}, u32[]{:S(2)}) collective-permute-start(bf16[240,640]{1,0:T(8,128)(2,1)S(1)} %collective-permute-done.19.refs_16_), channel_id=1, source_target_pairs={{0,24},{4,28},{8,16},{12,20},{16,8},{20,12},{24,0},{28,4},{1,25},{... | collective-permute-start | bytes 921608 | tf_op jit(solution)/shard_map/ppermute | solution.py:271
  32.7 7.4 %collective-permute-done.31.refs_2_ = f32[64,384]{1,0:T(8,128)S(1)} collective-permute-done((f32[64,384]{1,0:T(8,128)S(1)}, f32[64,384]{1,0:T(8,128)S(1)}, u32[]{:S(2)}, u32[]{:S(2)}) %collective-permute-start.31) | collective-permute-done | bytes 98336 | tf_op jit(solution)/shard_map/ppermute | solution.py:271
  40.7 1.5 collective-permute-start.21
  42.2 1.6 %collective-permute-start.17 = (bf16[240,640]{1,0:T(8,128)(2,1)}, bf16[240,640]{1,0:T(8,128)(2,1)S(1)}, u32[]{:S(2)}, u32[]{:S(2)}) collective-permute-start(bf16[240,640]{1,0:T(8,128)(2,1)} %collective-permute-done.11.refs_8_), channel_id=1, source_target_pairs={{0,24},{4,28},{8,16},{12,20},{16,8},{20,12},{24,0},{28,4},{1,25},{... | collective-permute-start | bytes 921608 | tf_op jit(solution)/shard_map/ppermute | solution.py:271
  44.2 4.1 %collective-permute-done.23.refs_20_ = bf16[240,640]{1,0:T(8,128)(2,1)S(1)} collective-permute-done((bf16[240,640]{1,0:T(8,128)(2,1)S(1)}, bf16[240,640]{1,0:T(8,128)(2,1)S(1)}, u32[]{:S(2)}, u32[]{:S(2)}) %collective-permute-start.23) | collective-permute-done | bytes 307232 | tf_op jit(solution)/shard_map/ppermute | solution.py:271
  48.4 3.5 %collective-permute-start.13 = (bf16[240,640]{1,0:T(8,128)(2,1)}, bf16[240,640]{1,0:T(8,128)(2,1)S(1)}, u32[]{:S(2)}, u32[]{:S(2)}) collective-permute-start(bf16[240,640]{1,0:T(8,128)(2,1)} %collective-permute-done.11.refs_8_), channel_id=1, source_target_pairs={{0,8},{4,12},{8,0},{12,4},{16,24},{20,28},{24,16},{28,20},{1,9},{5... | collective-permute-start | bytes 921608 | tf_op jit(solution)/shard_map/ppermute | solution.py:271
  51.9 1.2 collective-permute-start.9
  53.0 4.1 %collective-permute-done.17.refs_14_ = bf16[240,640]{1,0:T(8,128)(2,1)S(1)} collective-permute-done((bf16[240,640]{1,0:T(8,128)(2,1)}, bf16[240,640]{1,0:T(8,128)(2,1)S(1)}, u32[]{:S(2)}, u32[]{:S(2)}) %collective-permute-start.17) | collective-permute-done | bytes 307232 | tf_op jit(solution)/shard_map/ppermute | solution.py:271
  57.8 3.7 %collective-permute-done.15.refs_12_ = bf16[240,640]{1,0:T(8,128)(2,1)S(1)} collective-permute-done((bf16[240,640]{1,0:T(8,128)(2,1)}, bf16[240,640]{1,0:T(8,128)(2,1)S(1)}, u32[]{:S(2)}, u32[]{:S(2)}) %collective-permute-start.15) | collective-permute-done | bytes 307232 | tf_op jit(solution)/shard_map/ppermute | solution.py:271
  61.5 3.5 %collective-permute-start.5 = (bf16[240,640]{1,0:T(8,128)(2,1)S(1)}, bf16[240,640]{1,0:T(8,128)(2,1)S(1)}, u32[]{:S(2)}, u32[]{:S(2)}) collective-permute-start(bf16[240,640]{1,0:T(8,128)(2,1)S(1)} %collective-permute-done.3.refs_0_), channel_id=1, source_target_pairs={{0,8},{4,12},{8,0},{12,4},{16,24},{20,28},{24,16},{28,20},{1,9},{5... | collective-permute-start | bytes 921608 | tf_op jit(solution)/shard_map/ppermute | solution.py:271
  65.5 4.9 %collective-permute-done.9.refs_6_ = bf16[240,640]{1,0:T(8,128)(2,1)S(1)} collective-permute-done((bf16[240,640]{1,0:T(8,128)(2,1)S(1)}, bf16[240,640]{1,0:T(8,128)(2,1)S(1)}, u32[]{:S(2)}, u32[]{:S(2)}) %collective-permute-start.9) | collective-permute-done | bytes 307232 | tf_op jit(solution)/shard_map/ppermute | solution.py:271
  70.4 3.0 %collective-permute-done.7.refs_4_ = bf16[240,640]{1,0:T(8,128)(2,1)S(1)} collective-permute-done((bf16[240,640]{1,0:T(8,128)(2,1)S(1)}, bf16[240,640]{1,0:T(8,128)(2,1)S(1)}, u32[]{:S(2)}, u32[]{:S(2)}) %collective-permute-start.7) | collective-permute-done | bytes 307232 | tf_op jit(solution)/shard_map/ppermute | solution.py:271
  75.7 10.8 %short_attention.2 = (bf16[80,640]{1,0:T(8,128)(2,1)S(1)}, bf16[80,640]{1,0:T(8,128)(2,1)S(1)}, bf16[80,640]{1,0:T(8,128)(2,1)S(1)}, bf16[80,640]{1,0:T(8,128)(2,1)S(1)}) custom-call(s32[2]{0:T(128)S(1)} %pad_add_fusion.at_ref, bf16[4,320,1280]{2,1,0:T(8,128)(2,1)} %x_ref.8, bf16[320,16,320]{2,1,0:T(8,128)(2,1)} %k_ref.5, bf16[320,16,320]{2,1,0:T(8,128)(2,1)} %v_ref.5, ...), custom_call_target="tpu_custom_call" | custom-call | flops 1572864000 | bytes 12705280 | tf_op jit(solution)/shard_map/short_attention/pallas_call | solution.py:280
  86.6 0.9 collective-permute-start
  87.5 2.4 %collective-permute-start.1 = (bf16[80,640]{1,0:T(8,128)(2,1)S(1)}, bf16[80,640]{1,0:T(8,128)(2,1)S(1)}, u32[]{:S(2)}, u32[]{:S(2)}) collective-permute-start(bf16[80,640]{1,0:T(8,128)(2,1)S(1)} %get-tuple-element.27), channel_id=1, source_target_pairs={{0,2},{1,3},{2,0},{3,1},{4,6},{5,7},{6,4},{7,5},{8,10},{9,11},{10,... | collective-permute-start | bytes 307208 | tf_op jit(solution)/shard_map/ppermute | solution.py:271
  90.4 12.7 %short_attention.3 = (bf16[96,640]{1,0:T(8,128)(2,1)S(1)}, bf16[96,640]{1,0:T(8,128)(2,1)S(1)}, bf16[96,640]{1,0:T(8,128)(2,1)S(1)}, bf16[96,640]{1,0:T(8,128)(2,1)S(1)}) custom-call(s32[2]{0:T(128)S(1)} %pad_add_fusion.at_ref, bf16[4,320,1280]{2,1,0:T(8,128)(2,1)} %x_ref.8, bf16[320,16,320]{2,1,0:T(8,128)(2,1)} %k_ref.5, bf16[320,16,320]{2,1,0:T(8,128)(2,1)} %v_ref.5, ...), custom_call_target="tpu_custom_call" | custom-call | flops 1572864000 | bytes 13696512 | tf_op jit(solution)/shard_map/short_attention/pallas_call | solution.py:280
  103.1 1.5 collective-permute-start.37
  104.7 2.4 %collective-permute-start.38 = (bf16[96,640]{1,0:T(8,128)(2,1)S(1)}, bf16[96,640]{1,0:T(8,128)(2,1)S(1)}, u32[]{:S(2)}, u32[]{:S(2)}) collective-permute-start(bf16[96,640]{1,0:T(8,128)(2,1)S(1)} %get-tuple-element.42), channel_id=1, source_target_pairs={{0,2},{1,3},{2,0},{3,1},{4,6},{5,7},{6,4},{7,5},{8,10},{9,11},{10,... | collective-permute-start | bytes 368648 | tf_op jit(solution)/shard_map/ppermute | solution.py:271
  107.1 7.2 %unpack_weights.1 = (bf16[1280,1280]{1,0:T(8,128)(2,1)}, bf16[1280,1280]{1,0:T(8,128)(2,1)}, bf16[1280,1280]{1,0:T(8,128)(2,1)}) custom-call(s32[2]{0:T(128)S(1)} %pad_add_fusion.at_ref, bf16[320,1280]{1,0:T(8,128)(2,1)} %own_o.1, bf16[1280,320]{1,0:T(8,128)(2,1)} %copy-done.1, bf16[320,1280]{1,0:T(8,128)(2,1)} %own_down.1, ...), custom_call_target="tpu_custom_call" | custom-call | bytes 19660800 | tf_op jit(solution)/shard_map/unpack_weights/pallas_call | solution.py:280
  114.3 0.8 collective-permute-start.39
  115.1 6.8 %feed_forward.2 = (bf16[80,640]{1,0:T(8,128)(2,1)S(1)}, bf16[80,640]{1,0:T(8,128)(2,1)S(1)}, bf16[80,640]{1,0:T(8,128)(2,1)S(1)}, bf16[80,640]{1,0:T(8,128)(2,1)S(1)}) custom-call(s32[2]{0:T(128)S(1)} %pad_add_fusion.at_ref, bf16[4,320,1280]{2,1,0:T(8,128)(2,1)S(1)} %copy-done, f32[1,1280]{1,0:T(1,128)S(1)} %broadcast_in_dim.12.refs_0_.refs_1_, ...), custom_call_target="tpu_custom_call" | custom-call | flops 1572864000 | bytes 13931520 | tf_op jit(solution)/shard_map/feed_forward/pallas_call | solution.py:280
  121.9 1.2 collective-permute-start.27
  123.1 6.9 %feed_forward.3 = (bf16[96,640]{1,0:T(8,128)(2,1)S(1)}, bf16[96,640]{1,0:T(8,128)(2,1)S(1)}, bf16[96,640]{1,0:T(8,128)(2,1)S(1)}, bf16[96,640]{1,0:T(8,128)(2,1)S(1)}) custom-call(s32[2]{0:T(128)S(1)} %pad_add_fusion.at_ref, bf16[4,320,1280]{2,1,0:T(8,128)(2,1)S(1)} %copy-done, bf16[4,12,1280]{2,1,0:T(8,128)(2,1)S(1)} %copy.31.x_ref.refs_0_, ...), custom_call_target="tpu_custom_call" | custom-call | flops 1730150400 | bytes 14218240 | tf_op jit(solution)/shard_map/feed_forward/pallas_call | solution.py:280
  130.0 0.9 collective-permute-start.40
  131.0 3.5 %collective-permute-start.41 = (bf16[96,640]{1,0:T(8,128)(2,1)S(1)}, bf16[96,640]{1,0:T(8,128)(2,1)S(1)}, u32[]{:S(2)}, u32[]{:S(2)}) collective-permute-start(bf16[96,640]{1,0:T(8,128)(2,1)S(1)} %get-tuple-element.46), channel_id=1, source_target_pairs={{0,2},{1,3},{2,0},{3,1},{4,6},{5,7},{6,4},{7,5},{8,10},{9,11},{10,... | collective-permute-start | bytes 368648 | tf_op jit(solution)/shard_map/ppermute | solution.py:271
  134.4 2.4 %collective-permute-start.28 = (bf16[80,640]{1,0:T(8,128)(2,1)S(1)}, bf16[80,640]{1,0:T(8,128)(2,1)S(1)}, u32[]{:S(2)}, u32[]{:S(2)}) collective-permute-start(bf16[80,640]{1,0:T(8,128)(2,1)S(1)} %get-tuple-element.34), channel_id=1, source_target_pairs={{0,2},{1,3},{2,0},{3,1},{4,6},{5,7},{6,4},{7,5},{8,10},{9,11},{10,... | collective-permute-start | bytes 307208 | tf_op jit(solution)/shard_map/ppermute | solution.py:271
  137.4 13.3 %collective-permute-done.28.refs_2_ = bf16[80,640]{1,0:T(8,128)(2,1)S(1)} collective-permute-done((bf16[80,640]{1,0:T(8,128)(2,1)S(1)}, bf16[80,640]{1,0:T(8,128)(2,1)S(1)}, u32[]{:S(2)}, u32[]{:S(2)}) %collective-permute-start.28) | collective-permute-done | bytes 102432 | tf_op jit(solution)/shard_map/ppermute | solution.py:271
  150.7 2.0 %collective-permute-done.29.refs_3_ = bf16[80,640]{1,0:T(8,128)(2,1)S(1)} collective-permute-done((bf16[80,640]{1,0:T(8,128)(2,1)S(1)}, bf16[80,640]{1,0:T(8,128)(2,1)S(1)}, u32[]{:S(2)}, u32[]{:S(2)}) %collective-permute-start.29) | collective-permute-done | bytes 102432 | tf_op jit(solution)/shard_map/ppermute | solution.py:271
  152.7 1.7 %place_outputs.1 = (bf16[4,320,320]{2,1,0:T(8,128)(2,1)}, bf16[4,12,320]{2,1,0:T(8,128)(2,1)S(1)}) custom-call(s32[2]{0:T(128)S(1)} %pad_add_fusion.at_ref, bf16[80,640]{1,0:T(8,128)(2,1)S(1)} %get-tuple-element.32.refs_0_, bf16[80,640]{1,0:T(8,128)(2,1)S(1)} %collective-permute-done.27.refs_1_, bf16[80,640]{1,0:T(8,128)(2,1)S(1)} %collective-permute-done.28.refs_2_, ...), custom_call_target="tpu_custom_call" | custom-call | bytes 1751040 | tf_op jit(solution)/shard_map/place_outputs/pallas_call | solution.py:280
  (92 shorter events, 8.4 us)
Async XLA Ops:
  6.4 23.3 %collective-permute-start.19 = (bf16[240,640]{1,0:T(8,128)(2,1)}, bf16[240,640]{1,0:T(8,128)(2,1)S(1)}, u32[]{:S(2)}, u32[]{:S(2)}) collective-permute-start(bf16[240,640]{1,0:T(8,128)(2,1)} %pack_weights.1), channel_id=1, source_target_pairs={{0,3},{1,2},{2,1},{3,0},{4,7},{5,6},{6,5},{7,4},{8,11},{9,10},{10,... | collective-permute-start | bytes 921608 | tf_op jit(solution)/shard_map/ppermute | solution.py:271
  8.0 34.2 %collective-permute-start.11 = (bf16[240,640]{1,0:T(8,128)(2,1)}, bf16[240,640]{1,0:T(8,128)(2,1)}, u32[]{:S(2)}, u32[]{:S(2)}) collective-permute-start(bf16[240,640]{1,0:T(8,128)(2,1)} %pack_weights.1), channel_id=1, source_target_pairs={{0,2},{1,3},{2,0},{3,1},{4,6},{5,7},{6,4},{7,5},{8,10},{9,11},{10,... | collective-permute-start | bytes 921608 | tf_op jit(solution)/shard_map/ppermute | solution.py:271
  9.7 66.0 %copy-start.17 = (s32[320]{0:T(512)S(1)}, s32[320]{0:T(512)}, u32[]{:S(2)}) copy-start(s32[320]{0:T(512)} %param.23) | copy-start | bytes 3844
  9.7 66.0 %copy-start.16 = (f32[1280]{0:T(1024)S(1)}, f32[1280]{0:T(1024)}, u32[]{:S(2)}) copy-start(f32[1280]{0:T(1024)} %param.26) | copy-start | bytes 15364
  15.4 5.7 %collective-permute-start.36 = (f32[64,384]{1,0:T(8,128)S(1)}, f32[64,384]{1,0:T(8,128)S(1)}, u32[]{:S(2)}, u32[]{:S(2)}) collective-permute-start(f32[64,384]{1,0:T(8,128)S(1)} %get-tuple-element.36.refs_0_), channel_id=1, source_target_pairs={{0,28},{4,24},{8,20},{12,16},{16,12},{20,8},{24,4},{28,0},{1,29},{... | collective-permute-start | bytes 294920 | tf_op jit(solution)/shard_map/ppermute | solution.py:271
  17.1 6.4 %collective-permute-start.35 = (f32[64,384]{1,0:T(8,128)S(1)}, f32[64,384]{1,0:T(8,128)S(1)}, u32[]{:S(2)}, u32[]{:S(2)}) collective-permute-start(f32[64,384]{1,0:T(8,128)S(1)} %get-tuple-element.36.refs_0_), channel_id=1, source_target_pairs={{0,24},{4,28},{8,16},{12,20},{16,8},{20,12},{24,0},{28,4},{1,25},{... | collective-permute-start | bytes 294920 | tf_op jit(solution)/shard_map/ppermute | solution.py:271
  18.2 7.4 %collective-permute-start.34 = (f32[64,384]{1,0:T(8,128)S(1)}, f32[64,384]{1,0:T(8,128)S(1)}, u32[]{:S(2)}, u32[]{:S(2)}) collective-permute-start(f32[64,384]{1,0:T(8,128)S(1)} %get-tuple-element.36.refs_0_), channel_id=1, source_target_pairs={{0,20},{4,16},{8,28},{12,24},{16,4},{20,0},{24,12},{28,8},{1,21},{... | collective-permute-start | bytes 294920 | tf_op jit(solution)/shard_map/ppermute | solution.py:271
  21.1 11.0 %collective-permute-start.33 = (f32[64,384]{1,0:T(8,128)S(1)}, f32[64,384]{1,0:T(8,128)S(1)}, u32[]{:S(2)}, u32[]{:S(2)}) collective-permute-start(f32[64,384]{1,0:T(8,128)S(1)} %get-tuple-element.36.refs_0_), channel_id=1, source_target_pairs={{0,16},{4,20},{8,24},{12,28},{16,0},{20,4},{24,8},{28,12},{1,17},{... | collective-permute-start | bytes 294920 | tf_op jit(solution)/shard_map/ppermute | solution.py:271
  23.5 9.2 %collective-permute-start.32 = (f32[64,384]{1,0:T(8,128)S(1)}, f32[64,384]{1,0:T(8,128)S(1)}, u32[]{:S(2)}, u32[]{:S(2)}) collective-permute-start(f32[64,384]{1,0:T(8,128)S(1)} %get-tuple-element.36.refs_0_), channel_id=1, source_target_pairs={{0,12},{4,8},{8,4},{12,0},{16,28},{20,24},{24,20},{28,16},{1,13},{... | collective-permute-start | bytes 294920 | tf_op jit(solution)/shard_map/ppermute | solution.py:271
  25.7 16.5 %collective-permute-start.3 = (bf16[240,640]{1,0:T(8,128)(2,1)}, bf16[240,640]{1,0:T(8,128)(2,1)S(1)}, u32[]{:S(2)}, u32[]{:S(2)}) collective-permute-start(bf16[240,640]{1,0:T(8,128)(2,1)} %pack_weights.1), channel_id=1, source_target_pairs={{0,1},{1,0},{2,3},{3,2},{4,5},{5,4},{6,7},{7,6},{8,9},{9,8},{10,11... | collective-permute-start | bytes 921608 | tf_op jit(solution)/shard_map/ppermute | solution.py:271
  29.7 14.0 %collective-permute-start.25 = (bf16[240,640]{1,0:T(8,128)(2,1)S(1)}, bf16[240,640]{1,0:T(8,128)(2,1)S(1)}, u32[]{:S(2)}, u32[]{:S(2)}) collective-permute-start(bf16[240,640]{1,0:T(8,128)(2,1)S(1)} %collective-permute-done.19.refs_16_), channel_id=1, source_target_pairs={{0,24},{4,28},{8,16},{12,20},{16,8},{20,12},{24,0},{28,4},{1,25},{... | collective-permute-start | bytes 921608 | tf_op jit(solution)/shard_map/ppermute | solution.py:271
  32.2 8.0 %collective-permute-start.31 = (f32[64,384]{1,0:T(8,128)S(1)}, f32[64,384]{1,0:T(8,128)S(1)}, u32[]{:S(2)}, u32[]{:S(2)}) collective-permute-start(f32[64,384]{1,0:T(8,128)S(1)} %get-tuple-element.36.refs_0_), channel_id=1, source_target_pairs={{0,8},{4,12},{8,0},{12,4},{16,24},{20,28},{24,16},{28,20},{1,9},{5... | collective-permute-start | bytes 294920 | tf_op jit(solution)/shard_map/ppermute | solution.py:271
  32.7 7.9 %collective-permute-start.30 = (f32[64,384]{1,0:T(8,128)S(1)}, f32[64,384]{1,0:T(8,128)S(1)}, u32[]{:S(2)}, u32[]{:S(2)}) collective-permute-start(f32[64,384]{1,0:T(8,128)S(1)} %get-tuple-element.36.refs_0_), channel_id=1, source_target_pairs={{0,4},{4,0},{8,12},{12,8},{16,20},{20,16},{24,28},{28,24},{1,5},{5... | collective-permute-start | bytes 294920 | tf_op jit(solution)/shard_map/ppermute | solution.py:271
  40.2 8.2 %collective-permute-start.23 = (bf16[240,640]{1,0:T(8,128)(2,1)S(1)}, bf16[240,640]{1,0:T(8,128)(2,1)S(1)}, u32[]{:S(2)}, u32[]{:S(2)}) collective-permute-start(bf16[240,640]{1,0:T(8,128)(2,1)S(1)} %collective-permute-done.19.refs_16_), channel_id=1, source_target_pairs={{0,16},{4,20},{8,24},{12,28},{16,0},{20,4},{24,8},{28,12},{1,17},{... | collective-permute-start | bytes 921608 | tf_op jit(solution)/shard_map/ppermute | solution.py:271
  40.7 11.2 %collective-permute-start.21 = (bf16[240,640]{1,0:T(8,128)(2,1)S(1)}, bf16[240,640]{1,0:T(8,128)(2,1)S(1)}, u32[]{:S(2)}, u32[]{:S(2)}) collective-permute-start(bf16[240,640]{1,0:T(8,128)(2,1)S(1)} %collective-permute-done.19.refs_16_), channel_id=1, source_target_pairs={{0,8},{4,12},{8,0},{12,4},{16,24},{20,28},{24,16},{28,20},{1,9},{5... | collective-permute-start | bytes 921608 | tf_op jit(solution)/shard_map/ppermute | solution.py:271
  42.2 9.7 %collective-permute-start.20 = (bf16[240,640]{1,0:T(8,128)(2,1)S(1)}, bf16[240,640]{1,0:T(8,128)(2,1)S(1)}, u32[]{:S(2)}, u32[]{:S(2)}) collective-permute-start(bf16[240,640]{1,0:T(8,128)(2,1)S(1)} %collective-permute-done.19.refs_16_), channel_id=1, source_target_pairs={{0,4},{4,0},{8,12},{12,8},{16,20},{20,16},{24,28},{28,24},{1,5},{5... | collective-permute-start | bytes 921608 | tf_op jit(solution)/shard_map/ppermute | solution.py:271
  42.2 15.0 %collective-permute-start.17 = (bf16[240,640]{1,0:T(8,128)(2,1)}, bf16[240,640]{1,0:T(8,128)(2,1)S(1)}, u32[]{:S(2)}, u32[]{:S(2)}) collective-permute-start(bf16[240,640]{1,0:T(8,128)(2,1)} %collective-permute-done.11.refs_8_), channel_id=1, source_target_pairs={{0,24},{4,28},{8,16},{12,20},{16,8},{20,12},{24,0},{28,4},{1,25},{... | collective-permute-start | bytes 921608 | tf_op jit(solution)/shard_map/ppermute | solution.py:271
  43.7 42.8 %copy-start.10 = (bf16[240,640]{1,0:T(8,128)(2,1)}, bf16[240,640]{1,0:T(8,128)(2,1)S(1)}, u32[]{:S(2)}) copy-start(bf16[240,640]{1,0:T(8,128)(2,1)S(1)} %collective-permute-done.25.refs_22_) | copy-start | bytes 921604
  43.7 17.8 %collective-permute-start.15 = (bf16[240,640]{1,0:T(8,128)(2,1)}, bf16[240,640]{1,0:T(8,128)(2,1)S(1)}, u32[]{:S(2)}, u32[]{:S(2)}) collective-permute-start(bf16[240,640]{1,0:T(8,128)(2,1)} %collective-permute-done.11.refs_8_), channel_id=1, source_target_pairs={{0,16},{4,20},{8,24},{12,28},{16,0},{20,4},{24,8},{28,12},{1,17},{... | collective-permute-start | bytes 921608 | tf_op jit(solution)/shard_map/ppermute | solution.py:271
  48.4 38.1 %copy-start.11 = (bf16[240,640]{1,0:T(8,128)(2,1)}, bf16[240,640]{1,0:T(8,128)(2,1)S(1)}, u32[]{:S(2)}) copy-start(bf16[240,640]{1,0:T(8,128)(2,1)S(1)} %collective-permute-done.23.refs_20_) | copy-start | bytes 921604
  48.4 16.6 %collective-permute-start.13 = (bf16[240,640]{1,0:T(8,128)(2,1)}, bf16[240,640]{1,0:T(8,128)(2,1)S(1)}, u32[]{:S(2)}, u32[]{:S(2)}) collective-permute-start(bf16[240,640]{1,0:T(8,128)(2,1)} %collective-permute-done.11.refs_8_), channel_id=1, source_target_pairs={{0,8},{4,12},{8,0},{12,4},{16,24},{20,28},{24,16},{28,20},{1,9},{5... | collective-permute-start | bytes 921608 | tf_op jit(solution)/shard_map/ppermute | solution.py:271
  51.9 13.2 %collective-permute-start.12 = (bf16[240,640]{1,0:T(8,128)(2,1)}, bf16[240,640]{1,0:T(8,128)(2,1)S(1)}, u32[]{:S(2)}, u32[]{:S(2)}) collective-permute-start(bf16[240,640]{1,0:T(8,128)(2,1)} %collective-permute-done.11.refs_8_), channel_id=1, source_target_pairs={{0,4},{4,0},{8,12},{12,8},{16,20},{20,16},{24,28},{28,24},{1,5},{5... | collective-permute-start | bytes 921608 | tf_op jit(solution)/shard_map/ppermute | solution.py:271
  51.9 18.5 %collective-permute-start.9 = (bf16[240,640]{1,0:T(8,128)(2,1)S(1)}, bf16[240,640]{1,0:T(8,128)(2,1)S(1)}, u32[]{:S(2)}, u32[]{:S(2)}) collective-permute-start(bf16[240,640]{1,0:T(8,128)(2,1)S(1)} %collective-permute-done.3.refs_0_), channel_id=1, source_target_pairs={{0,24},{4,28},{8,16},{12,20},{16,8},{20,12},{24,0},{28,4},{1,25},{... | collective-permute-start | bytes 921608 | tf_op jit(solution)/shard_map/ppermute | solution.py:271
  57.2 16.2 %collective-permute-start.7 = (bf16[240,640]{1,0:T(8,128)(2,1)S(1)}, bf16[240,640]{1,0:T(8,128)(2,1)S(1)}, u32[]{:S(2)}, u32[]{:S(2)}) collective-permute-start(bf16[240,640]{1,0:T(8,128)(2,1)S(1)} %collective-permute-done.3.refs_0_), channel_id=1, source_target_pairs={{0,16},{4,20},{8,24},{12,28},{16,0},{20,4},{24,8},{28,12},{1,17},{... | collective-permute-start | bytes 921608 | tf_op jit(solution)/shard_map/ppermute | solution.py:271
  61.5 12.4 %collective-permute-start.5 = (bf16[240,640]{1,0:T(8,128)(2,1)S(1)}, bf16[240,640]{1,0:T(8,128)(2,1)S(1)}, u32[]{:S(2)}, u32[]{:S(2)}) collective-permute-start(bf16[240,640]{1,0:T(8,128)(2,1)S(1)} %collective-permute-done.3.refs_0_), channel_id=1, source_target_pairs={{0,8},{4,12},{8,0},{12,4},{16,24},{20,28},{24,16},{28,20},{1,9},{5... | collective-permute-start | bytes 921608 | tf_op jit(solution)/shard_map/ppermute | solution.py:271
  65.0 8.9 %collective-permute-start.4 = (bf16[240,640]{1,0:T(8,128)(2,1)S(1)}, bf16[240,640]{1,0:T(8,128)(2,1)S(1)}, u32[]{:S(2)}, u32[]{:S(2)}) collective-permute-start(bf16[240,640]{1,0:T(8,128)(2,1)S(1)} %collective-permute-done.3.refs_0_), channel_id=1, source_target_pairs={{0,4},{4,0},{8,12},{12,8},{16,20},{20,16},{24,28},{28,24},{1,5},{5... | collective-permute-start | bytes 921608 | tf_op jit(solution)/shard_map/ppermute | solution.py:271
  65.0 9.4 %collective-permute-start.26 = (bf16[240,640]{1,0:T(8,128)(2,1)S(1)}, bf16[240,640]{1,0:T(8,128)(2,1)S(1)}, u32[]{:S(2)}, u32[]{:S(2)}) collective-permute-start(bf16[240,640]{1,0:T(8,128)(2,1)S(1)} %collective-permute-done.25.refs_22_), channel_id=1, source_target_pairs={{0,4},{4,0},{8,12},{12,8},{16,20},{20,16},{24,28},{28,24},{1,5},{5... | collective-permute-start | bytes 921608 | tf_op jit(solution)/shard_map/ppermute | solution.py:271
  70.4 4.2 %collective-permute-start.24 = (bf16[240,640]{1,0:T(8,128)(2,1)S(1)}, bf16[240,640]{1,0:T(8,128)(2,1)S(1)}, u32[]{:S(2)}, u32[]{:S(2)}) collective-permute-start(bf16[240,640]{1,0:T(8,128)(2,1)S(1)} %collective-permute-done.23.refs_20_), channel_id=1, source_target_pairs={{0,4},{4,0},{8,12},{12,8},{16,20},{20,16},{24,28},{28,24},{1,5},{5... | collective-permute-start | bytes 921608 | tf_op jit(solution)/shard_map/ppermute | solution.py:271
  73.4 1.6 %collective-permute-start.22 = (bf16[240,640]{1,0:T(8,128)(2,1)S(1)}, bf16[240,640]{1,0:T(8,128)(2,1)S(1)}, u32[]{:S(2)}, u32[]{:S(2)}) collective-permute-start(bf16[240,640]{1,0:T(8,128)(2,1)S(1)} %collective-permute-done.21.refs_18_), channel_id=1, source_target_pairs={{0,4},{4,0},{8,12},{12,8},{16,20},{20,16},{24,28},{28,24},{1,5},{5... | collective-permute-start | bytes 921608 | tf_op jit(solution)/shard_map/ppermute | solution.py:271
  74.0 1.6 %collective-permute-start.18 = (bf16[240,640]{1,0:T(8,128)(2,1)S(1)}, bf16[240,640]{1,0:T(8,128)(2,1)S(1)}, u32[]{:S(2)}, u32[]{:S(2)}) collective-permute-start(bf16[240,640]{1,0:T(8,128)(2,1)S(1)} %collective-permute-done.17.refs_14_), channel_id=1, source_target_pairs={{0,4},{4,0},{8,12},{12,8},{16,20},{20,16},{24,28},{28,24},{1,5},{5... | collective-permute-start | bytes 921608 | tf_op jit(solution)/shard_map/ppermute | solution.py:271
  74.0 12.6 %collective-permute-start.16 = (bf16[240,640]{1,0:T(8,128)(2,1)S(1)}, bf16[240,640]{1,0:T(8,128)(2,1)S(1)}, u32[]{:S(2)}, u32[]{:S(2)}) collective-permute-start(bf16[240,640]{1,0:T(8,128)(2,1)S(1)} %collective-permute-done.15.refs_12_), channel_id=1, source_target_pairs={{0,4},{4,0},{8,12},{12,8},{16,20},{20,16},{24,28},{28,24},{1,5},{5... | collective-permute-start | bytes 921608 | tf_op jit(solution)/shard_map/ppermute | solution.py:271
  74.5 12.1 %copy-start.12 = (bf16[240,640]{1,0:T(8,128)(2,1)}, bf16[240,640]{1,0:T(8,128)(2,1)S(1)}, u32[]{:S(2)}) copy-start(bf16[240,640]{1,0:T(8,128)(2,1)S(1)} %collective-permute-done.26.refs_23_) | copy-start | bytes 921604
  74.5 13.0 %collective-permute-start.14 = (bf16[240,640]{1,0:T(8,128)(2,1)S(1)}, bf16[240,640]{1,0:T(8,128)(2,1)S(1)}, u32[]{:S(2)}, u32[]{:S(2)}) collective-permute-start(bf16[240,640]{1,0:T(8,128)(2,1)S(1)} %collective-permute-done.13.refs_10_), channel_id=1, source_target_pairs={{0,4},{4,0},{8,12},{12,8},{16,20},{20,16},{24,28},{28,24},{1,5},{5... | collective-permute-start | bytes 921608 | tf_op jit(solution)/shard_map/ppermute | solution.py:271
  74.6 15.3 %collective-permute-start.10 = (bf16[240,640]{1,0:T(8,128)(2,1)S(1)}, bf16[240,640]{1,0:T(8,128)(2,1)S(1)}, u32[]{:S(2)}, u32[]{:S(2)}) collective-permute-start(bf16[240,640]{1,0:T(8,128)(2,1)S(1)} %collective-permute-done.9.refs_6_), channel_id=1, source_target_pairs={{0,4},{4,0},{8,12},{12,8},{16,20},{20,16},{24,28},{28,24},{1,5},{5... | collective-permute-start | bytes 921608 | tf_op jit(solution)/shard_map/ppermute | solution.py:271
  75.0 28.1 %collective-permute-start.8 = (bf16[240,640]{1,0:T(8,128)(2,1)S(1)}, bf16[240,640]{1,0:T(8,128)(2,1)S(1)}, u32[]{:S(2)}, u32[]{:S(2)}) collective-permute-start(bf16[240,640]{1,0:T(8,128)(2,1)S(1)} %collective-permute-done.7.refs_4_), channel_id=1, source_target_pairs={{0,4},{4,0},{8,12},{12,8},{16,20},{20,16},{24,28},{28,24},{1,5},{5... | collective-permute-start | bytes 921608 | tf_op jit(solution)/shard_map/ppermute | solution.py:271
  75.6 29.1 %collective-permute-start.6 = (bf16[240,640]{1,0:T(8,128)(2,1)S(1)}, bf16[240,640]{1,0:T(8,128)(2,1)S(1)}, u32[]{:S(2)}, u32[]{:S(2)}) collective-permute-start(bf16[240,640]{1,0:T(8,128)(2,1)S(1)} %collective-permute-done.5.refs_2_), channel_id=1, source_target_pairs={{0,4},{4,0},{8,12},{12,8},{16,20},{20,16},{24,28},{28,24},{1,5},{5... | collective-permute-start | bytes 921608 | tf_op jit(solution)/shard_map/ppermute | solution.py:271
  86.6 27.7 %collective-permute-start = (bf16[80,640]{1,0:T(8,128)(2,1)S(1)}, bf16[80,640]{1,0:T(8,128)(2,1)S(1)}, u32[]{:S(2)}, u32[]{:S(2)}) collective-permute-start(bf16[80,640]{1,0:T(8,128)(2,1)S(1)} %get-tuple-element.26), channel_id=1, source_target_pairs={{0,1},{1,0},{2,3},{3,2},{4,5},{5,4},{6,7},{7,6},{8,9},{9,8},{10,11... | collective-permute-start | bytes 307208 | tf_op jit(solution)/shard_map/ppermute | solution.py:271
  87.5 27.6 %collective-permute-start.1 = (bf16[80,640]{1,0:T(8,128)(2,1)S(1)}, bf16[80,640]{1,0:T(8,128)(2,1)S(1)}, u32[]{:S(2)}, u32[]{:S(2)}) collective-permute-start(bf16[80,640]{1,0:T(8,128)(2,1)S(1)} %get-tuple-element.27), channel_id=1, source_target_pairs={{0,2},{1,3},{2,0},{3,1},{4,6},{5,7},{6,4},{7,5},{8,10},{9,11},{10,... | collective-permute-start | bytes 307208 | tf_op jit(solution)/shard_map/ppermute | solution.py:271
  89.9 25.2 %collective-permute-start.2 = (bf16[80,640]{1,0:T(8,128)(2,1)S(1)}, bf16[80,640]{1,0:T(8,128)(2,1)S(1)}, u32[]{:S(2)}, u32[]{:S(2)}) collective-permute-start(bf16[80,640]{1,0:T(8,128)(2,1)S(1)} %get-tuple-element.28), channel_id=1, source_target_pairs={{0,3},{1,2},{2,1},{3,0},{4,7},{5,6},{6,5},{7,4},{8,11},{9,10},{10,... | collective-permute-start | bytes 307208 | tf_op jit(solution)/shard_map/ppermute | solution.py:271
  103.1 19.9 %collective-permute-start.37 = (bf16[96,640]{1,0:T(8,128)(2,1)S(1)}, bf16[96,640]{1,0:T(8,128)(2,1)S(1)}, u32[]{:S(2)}, u32[]{:S(2)}) collective-permute-start(bf16[96,640]{1,0:T(8,128)(2,1)S(1)} %get-tuple-element.41), channel_id=1, source_target_pairs={{0,1},{1,0},{2,3},{3,2},{4,5},{5,4},{6,7},{7,6},{8,9},{9,8},{10,11... | collective-permute-start | bytes 368648 | tf_op jit(solution)/shard_map/ppermute | solution.py:271
  104.7 18.4 %collective-permute-start.38 = (bf16[96,640]{1,0:T(8,128)(2,1)S(1)}, bf16[96,640]{1,0:T(8,128)(2,1)S(1)}, u32[]{:S(2)}, u32[]{:S(2)}) collective-permute-start(bf16[96,640]{1,0:T(8,128)(2,1)S(1)} %get-tuple-element.42), channel_id=1, source_target_pairs={{0,2},{1,3},{2,0},{3,1},{4,6},{5,7},{6,4},{7,5},{8,10},{9,11},{10,... | collective-permute-start | bytes 368648 | tf_op jit(solution)/shard_map/ppermute | solution.py:271
  114.3 8.8 %collective-permute-start.39 = (bf16[96,640]{1,0:T(8,128)(2,1)S(1)}, bf16[96,640]{1,0:T(8,128)(2,1)S(1)}, u32[]{:S(2)}, u32[]{:S(2)}) collective-permute-start(bf16[96,640]{1,0:T(8,128)(2,1)S(1)} %get-tuple-element.43), channel_id=1, source_target_pairs={{0,3},{1,2},{2,1},{3,0},{4,7},{5,6},{6,5},{7,4},{8,11},{9,10},{10,... | collective-permute-start | bytes 368648 | tf_op jit(solution)/shard_map/ppermute | solution.py:271
  121.9 15.0 %collective-permute-start.27 = (bf16[80,640]{1,0:T(8,128)(2,1)S(1)}, bf16[80,640]{1,0:T(8,128)(2,1)S(1)}, u32[]{:S(2)}, u32[]{:S(2)}) collective-permute-start(bf16[80,640]{1,0:T(8,128)(2,1)S(1)} %get-tuple-element.33), channel_id=1, source_target_pairs={{0,1},{1,0},{2,3},{3,2},{4,5},{5,4},{6,7},{7,6},{8,9},{9,8},{10,11... | collective-permute-start | bytes 307208 | tf_op jit(solution)/shard_map/ppermute | solution.py:271
  130.0 22.7 %collective-permute-start.40 = (bf16[96,640]{1,0:T(8,128)(2,1)S(1)}, bf16[96,640]{1,0:T(8,128)(2,1)S(1)}, u32[]{:S(2)}, u32[]{:S(2)}) collective-permute-start(bf16[96,640]{1,0:T(8,128)(2,1)S(1)} %get-tuple-element.45), channel_id=1, source_target_pairs={{0,1},{1,0},{2,3},{3,2},{4,5},{5,4},{6,7},{7,6},{8,9},{9,8},{10,11... | collective-permute-start | bytes 368648 | tf_op jit(solution)/shard_map/ppermute | solution.py:271
  131.0 21.7 %collective-permute-start.41 = (bf16[96,640]{1,0:T(8,128)(2,1)S(1)}, bf16[96,640]{1,0:T(8,128)(2,1)S(1)}, u32[]{:S(2)}, u32[]{:S(2)}) collective-permute-start(bf16[96,640]{1,0:T(8,128)(2,1)S(1)} %get-tuple-element.46), channel_id=1, source_target_pairs={{0,2},{1,3},{2,0},{3,1},{4,6},{5,7},{6,4},{7,5},{8,10},{9,11},{10,... | collective-permute-start | bytes 368648 | tf_op jit(solution)/shard_map/ppermute | solution.py:271
  134.4 18.3 %collective-permute-start.42 = (bf16[96,640]{1,0:T(8,128)(2,1)S(1)}, bf16[96,640]{1,0:T(8,128)(2,1)S(1)}, u32[]{:S(2)}, u32[]{:S(2)}) collective-permute-start(bf16[96,640]{1,0:T(8,128)(2,1)S(1)} %get-tuple-element.47), channel_id=1, source_target_pairs={{0,3},{1,2},{2,1},{3,0},{4,7},{5,6},{6,5},{7,4},{8,11},{9,10},{10,... | collective-permute-start | bytes 368648 | tf_op jit(solution)/shard_map/ppermute | solution.py:271
  134.4 16.2 %collective-permute-start.28 = (bf16[80,640]{1,0:T(8,128)(2,1)S(1)}, bf16[80,640]{1,0:T(8,128)(2,1)S(1)}, u32[]{:S(2)}, u32[]{:S(2)}) collective-permute-start(bf16[80,640]{1,0:T(8,128)(2,1)S(1)} %get-tuple-element.34), channel_id=1, source_target_pairs={{0,2},{1,3},{2,0},{3,1},{4,6},{5,7},{6,4},{7,5},{8,10},{9,11},{10,... | collective-permute-start | bytes 307208 | tf_op jit(solution)/shard_map/ppermute | solution.py:271
  136.9 15.8 %collective-permute-start.29 = (bf16[80,640]{1,0:T(8,128)(2,1)S(1)}, bf16[80,640]{1,0:T(8,128)(2,1)S(1)}, u32[]{:S(2)}, u32[]{:S(2)}) collective-permute-start(bf16[80,640]{1,0:T(8,128)(2,1)S(1)} %get-tuple-element.35), channel_id=1, source_target_pairs={{0,3},{1,2},{2,1},{3,0},{4,7},{5,6},{6,5},{7,4},{8,11},{9,10},{10,... | collective-permute-start | bytes 307208 | tf_op jit(solution)/shard_map/ppermute | solution.py:271
  (13 other events, 78.7 us)

commit v2 on v0

v2 whole, which is shorter than its diff:
```python
import functools

import jax
import jax.numpy as jnp
from jax import lax
from jax.experimental import pallas as pl
from jax.experimental.pallas import tpu as pltpu
from jax.sharding import PartitionSpec as P

norm_eps = 1e-06
masked_fill = -1e30
GROUP = 16
F32 = jnp.float32
BF16 = jnp.bfloat16
MIB = 1024 * 1024


def rms_scale(rows, gain_row):
    mean_square = jnp.sum(rows * rows, axis=-1, keepdims=True) / rows.shape[-1]
    return (rows * lax.rsqrt(mean_square + norm_eps) * gain_row).astype(BF16)


def dot(a, b):
    return jnp.dot(a, b, preferred_element_type=F32)


def dot_t(a, b):
    return lax.dot_general(a, b, (((1,), (1,)), ((), ())), preferred_element_type=F32)


def lane_heads(rows, width, heads):
    return lax.broadcasted_iota(jnp.int32, (rows, width), 1) // (width // heads)


def stack_heads(queries, heads):
    head_of = lane_heads(*queries.shape, heads)
    return jnp.concatenate([jnp.where(head_of == h, queries, jnp.zeros_like(queries)) for h in range(heads)], axis=0)


def pick_heads(stacked, heads, width, head_dim=None):
    n = stacked.shape[0] // heads
    head_of = lax.broadcasted_iota(jnp.int32, (n, width), 1) // (head_dim or width // heads)
    picked = jnp.broadcast_to(stacked[:n], (n, width))
    for h in range(1, heads):
        picked = jnp.where(head_of == h, stacked[h * n : (h + 1) * n], picked)
    return picked


def slot_bias(lens, slots, columns):
    at = lax.broadcasted_iota(jnp.int32, (GROUP, columns), 1) - slots * lax.broadcasted_iota(jnp.int32, (GROUP, columns), 0)
    return jnp.where((at >= 0) & (at < lens), 0.0, masked_fill)


def fresh_bias(steps):
    n = steps * GROUP
    row = lax.broadcasted_iota(jnp.int32, (n, n), 0)
    col = lax.broadcasted_iota(jnp.int32, (n, n), 1)
    seen = (row % GROUP == col % GROUP) & (col // GROUP <= row // GROUP)
    return jnp.where(seen, 0.0, masked_fill)


def add_rows(scores, bias):
    reps = scores.shape[0] // bias.shape[0]
    return (scores.reshape(reps, *bias.shape) + bias[None]).reshape(scores.shape)


def pick_lens(len_row, base):
    lane = lax.broadcasted_iota(jnp.int32, (GROUP, len_row.shape[1]), 1)
    row = lax.broadcasted_iota(jnp.int32, (GROUP, len_row.shape[1]), 0)
    return jnp.sum(jnp.where(lane == base + row, len_row, 0), axis=1, keepdims=True)


def scale_lanes(scale_ref):
    return jnp.concatenate([scale_ref[h : h + 1, :] for h in range(scale_ref.shape[0])], axis=1)


def qkv_kernel(at_ref, x_ref, xl_ref, gain_ref, scale_ref, qw_ref, kw_ref, vw_ref, q_ref, kn_ref, vn_ref, ql_ref, knl_ref, vnl_ref, w_ref, rows_ref, sem):
    heads, head_dim = scale_ref.shape
    width = heads * head_dim
    short, count = x_ref.shape[1], xl_ref.shape[1]

    @pl.when(pl.program_id(0) == 0)
    def _():
        copies = [pltpu.make_async_copy(ref, w_ref.at[pl.ds(i * width, width), :], sem.at[i]) for i, ref in enumerate((qw_ref, kw_ref, vw_ref))]
        for copy in copies:
            copy.start()
        rows_ref[short:, :] = jnp.zeros((GROUP, rows_ref.shape[1]), F32)
        for copy in copies:
            copy.wait()

    rows_ref[:short, :] = x_ref[0].astype(F32)
    rows_ref[short : short + count, :] = xl_ref[0].astype(F32)
    normed = rms_scale(rows_ref[...], gain_ref[...][None])
    product = dot_t(normed, w_ref[...])
    queries = (product[:, :width] * scale_lanes(scale_ref) * head_dim**-0.5).astype(BF16)
    keys = product[:, width : 2 * width].astype(BF16)
    values = product[:, 2 * width :].astype(BF16)
    for rows, short_ref, long_ref in ((queries, q_ref, ql_ref), (keys, kn_ref, knl_ref), (values, vn_ref, vnl_ref)):
        short_ref[0] = rows[:short]
        long_ref[0] = rows[short:]


def put_sums(part_ref, row_max, weight_sum, width, heads):
    n = part_ref.shape[0]
    lane = lax.broadcasted_iota(jnp.int32, (n, part_ref.shape[1] - width), 1)
    tail = jnp.zeros(lane.shape, F32)
    for h in range(heads):
        tail = jnp.where(lane == h, row_max[h * n : (h + 1) * n], tail)
        tail = jnp.where(lane == heads + h, weight_sum[h * n : (h + 1) * n], tail)
    part_ref[:, width:] = tail


def get_column(part, first, heads):
    return jnp.concatenate([part[:, first + h : first + h + 1] for h in range(heads)], axis=0)


def long_kernel(heads, at_ref, q_ref, k_ref, v_ref, len_ref, part_ref):
    steps, _, width = q_ref.shape
    count, slots, _ = k_ref.shape
    n = steps * GROUP
    lens = jnp.minimum(pick_lens(len_ref[...][None], 0) - at_ref[0] * slots, slots)
    keys = k_ref[...].reshape(count * slots, width)
    values = v_ref[...].reshape(count * slots, width)
    bias = slot_bias(lens, slots, count * slots)
    scores = add_rows(dot_t(stack_heads(q_ref[...].reshape(n, width), heads), keys), bias)
    row_max = jnp.max(scores, axis=1, keepdims=True)
    probs = jnp.where(scores > 0.5 * masked_fill, jnp.exp(scores - row_max), 0.0)
    weight_sum = jnp.sum(probs, axis=1, keepdims=True)
    part_ref[:, :width] = pick_heads(dot(probs.astype(BF16), values), heads, width)
    put_sums(part_ref, row_max, weight_sum, width, heads)


def pair_kernel(heads, width, at_ref, mine_ref, other_ref, out_ref):
    even = at_ref[0] % 2 == 0
    mine, other = mine_ref[...], other_ref[...]
    parts = (jnp.where(even, mine, other), jnp.where(even, other, mine))
    maxes = [get_column(part, width, heads) for part in parts]
    row_max = jnp.maximum(*maxes)
    weight_sum = jnp.zeros_like(row_max)
    acc = jnp.zeros((mine.shape[0], width), F32)
    for part, part_max in zip(parts, maxes):
        factor = jnp.exp(part_max - row_max)
        weight_sum = weight_sum + factor * get_column(part, width + heads, heads)
        acc = acc + part[:, :width] * pick_heads(factor, heads, width)
    out_ref[:, :width] = acc
    put_sums(out_ref, row_max, weight_sum, width, heads)


def merge_long(my_chip, parts, held_ref, q, kn, vn, heads):
    n, width = q.shape
    for i, part in enumerate(parts):
        held_ref[my_chip ^ i] = part[...]
    scores = add_rows(dot_t(stack_heads(q, heads), kn), fresh_bias(n // GROUP))
    total_max = jnp.max(scores, axis=1, keepdims=True)
    held = [held_ref[i] for i in range(len(parts))]
    maxes = [get_column(part, width, heads) for part in held]
    for part_max in maxes:
        total_max = jnp.maximum(total_max, part_max)
    probs = jnp.exp(scores - total_max)
    denom = jnp.sum(probs, axis=1, keepdims=True)
    acc = pick_heads(dot(probs.astype(BF16), vn), heads, width)
    for part, part_max in zip(held, maxes):
        factor = jnp.exp(part_max - total_max)
        denom = denom + factor * get_column(part, width + heads, heads)
        acc = acc + part[:, :width] * pick_heads(factor, heads, width)
    return acc / pick_heads(denom, heads, width)


def short_kernel(heads, at_ref, q_ref, kn_ref, vn_ref, k_ref, v_ref, len_ref, *refs):
    att_ref = refs[-1]
    steps, block, width = q_ref.shape
    slots = k_ref.shape[1]
    few = GROUP // 2
    n = steps * few
    cached = few * slots
    i = pl.program_id(0)
    row = lax.broadcasted_iota(jnp.int32, (n, n), 0)
    col = lax.broadcasted_iota(jnp.int32, (n, n), 1)
    seen = (row % few == col % few) & (col // few <= row // few)
    late = jnp.where(seen, 0.0, masked_fill)
    slot = lax.broadcasted_iota(jnp.int32, (few, cached), 1) - slots * lax.broadcasted_iota(jnp.int32, (few, cached), 0)
    lane = lax.broadcasted_iota(jnp.int32, (few, len_ref.shape[0]), 1)
    request = lax.broadcasted_iota(jnp.int32, (few, len_ref.shape[0]), 0)
    groups = range(block // few)
    queries, keys, values, biases = [], [], [], []
    for g in groups:
        at, lo = slice(g * few, (g + 1) * few), g // 2 * GROUP
        half = g % 2 * few
        new = [ref[:, lo : lo + GROUP, :].astype(F32)[:, half : half + few, :].reshape(n, width).astype(BF16) for ref in (q_ref, kn_ref, vn_ref)]
        queries.append(stack_heads(new[0], heads))
        keys.append(jnp.concatenate([k_ref[at].reshape(cached, width), new[1]], axis=0))
        values.append(jnp.concatenate([v_ref[at].reshape(cached, width), new[2]], axis=0))
        lens = jnp.sum(jnp.where(lane == i * block + g * few + request, len_ref[...][None], 0), axis=1, keepdims=True)
        bias = jnp.where((slot >= 0) & (slot < lens), 0.0, masked_fill)
        biases.append(jnp.concatenate([jnp.concatenate([bias] * steps, axis=0), late], axis=1))
    scores = [add_rows(dot_t(queries[g], keys[g]), biases[g]) for g in groups]
    row_max = [jnp.max(scores[g], axis=1, keepdims=True) for g in groups]
    probs = [jnp.exp(scores[g] - row_max[g]) for g in groups]
    inverse = [1.0 / jnp.sum(probs[g], axis=1, keepdims=True) for g in groups]
    probs = [probs[g].astype(BF16) for g in groups]
    weighted = [dot(probs[g], values[g]) for g in groups]
    outs = [pick_heads(weighted[g] * inverse[g], heads, width) for g in groups]
    for g in groups[::2]:
        for s in range(steps):
            both = jnp.concatenate([outs[g][s * few : (s + 1) * few], outs[g + 1][s * few : (s + 1) * few]], axis=0)
            att_ref[s, g * few : (g + 2) * few, :] = both.astype(BF16)


def send_kernel(heads, at_ref, att_ref, ql_ref, knl_ref, vnl_ref, *refs):
    steps, count, width = att_ref.shape
    parts, outs, (long_ref, held_ref) = refs[: -2 - steps], refs[-2 - steps : -2], refs[-2:]
    half, n = count // 2, steps * GROUP
    longs = [ref[...].reshape(n, width) for ref in (ql_ref, knl_ref, vnl_ref)]
    merged = merge_long(at_ref[0] // 2, parts, held_ref, *longs, heads)
    for s in range(steps):
        long_ref[s] = merged[s * GROUP : (s + 1) * GROUP]
    for k in range(steps):
        rows = att_ref[at_ref[1] ^ k]
        mine = long_ref[at_ref[1] ^ k]
        outs[k][:half, :] = jnp.concatenate([rows[:half], rows[half:]], axis=1)
        outs[k][half:, :] = jnp.concatenate([mine[: GROUP // 2], mine[GROUP // 2 :]], axis=1).astype(BF16)


def pack_kernel(at_ref, o_ref, up_ref, down_ref, out_ref):
    for i, ref in enumerate((o_ref, up_ref, down_ref)):
        out_ref[i] = ref[...]


def stack_kernel(count, at_ref, *refs):
    for i in range(count):
        refs[-1][3 * i : 3 * i + 3] = refs[i][...]


def cut_kernel(cut, at_ref, x_ref, y_ref, *refs):
    refs[-2][...] = y_ref[:cut]
    refs[-1][...] = x_ref[cut:]


def mlp_kernel(tp, at_ref, x_ref, xl_ref, gain_ref, *refs):
    atts, owns, refs = refs[:tp], refs[tp : tp + 3], refs[tp + 3 :]
    pieces, outs, (cols_ref, xs_ref, w_ref, sem) = refs[: -tp - 4], refs[-tp - 4 : -4], refs[-4:]
    width, model = owns[0].shape
    rows, lanes = pieces[0].shape[1:]
    mine = at_ref[0] % 8
    copies = [pltpu.make_async_copy(ref, w_ref.at[i, pl.ds(0, width), :], sem.at[i]) for i, ref in enumerate(owns)]
    first = pieces[6].shape[0]
    for i, piece in enumerate(pieces):
        chip, start = (min(i // 2, 3), first if i // 2 == 4 else 0)
        place = mine ^ (2 * chip + i % 2)
        at = start
        while at < start + piece.shape[0]:
            unit, share = at // 3, at % 3
            size = min(3 - share, start + piece.shape[0] - at)
            row = pl.multiple_of((unit + 1) * width + (place // 2) * rows, 16)
            lane = pl.multiple_of((place % 2) * lanes, 128)
            target = w_ref.at[pl.ds(share, size), pl.ds(row, rows), pl.ds(lane, lanes)]
            copies.append(pltpu.make_async_copy(piece.at[pl.ds(at - start, size)], target, sem.at[len(copies)]))
            at += size
    for copy in copies:
        copy.start()
    half = x_ref.shape[1] // 2
    count = xl_ref.shape[1]
    xs_ref[...] = jnp.zeros_like(xs_ref)
    xs_ref[:count, :] = xl_ref[0].astype(F32)
    x = jnp.concatenate([x_ref[0].astype(F32), xs_ref[...]], axis=0)

    def rows_of(piece):
        tail = piece[half:].astype(F32)
        tail = jnp.concatenate([tail[:, :width], tail[:, width:]], axis=0).astype(BF16)
        return jnp.concatenate([piece[:half, :width], piece[:half, width:], tail], axis=0)

    attended = jnp.concatenate([rows_of(piece[...]) for piece in atts], axis=1)
    for copy in copies:
        copy.wait()
    mid = x + dot(attended, w_ref[0])
    normed = rms_scale(mid, gain_ref[...][None])
    pre = dot_t(normed, w_ref[1])
    hidden = (pre * (0.5 + 0.5 * jnp.tanh(0.5 * pre))).astype(BF16)
    out = mid + dot(hidden, w_ref[2])
    for b in range(tp):
        cols = out[:, b * width : (b + 1) * width]
        cols_ref[b, :half, :] = jnp.concatenate([cols[:half], cols[half : 2 * half]], axis=1).astype(BF16)
        tail = cols[2 * half :]
        cols_ref[b, half:, :] = jnp.concatenate([tail[: GROUP // 2], tail[GROUP // 2 :]], axis=1).astype(BF16)
    for k in range(tp):
        outs[k][...] = cols_ref[at_ref[1] ^ k]


def place_kernel(tp, at_ref, *refs):
    pieces, (short_ref, long_ref) = refs[:tp], refs[tp:]
    half, width = short_ref.shape[1] // 2, short_ref.shape[2]
    count = long_ref.shape[1]
    for k in range(tp):
        step = at_ref[1] ^ k
        short_ref[step, :half, :] = pieces[k][:half, :width]
        short_ref[step, half:, :] = pieces[k][:half, width:]
        tail = pieces[k][half:, :].astype(F32)
        long_ref[step] = jnp.concatenate([tail[:, :width], tail[:, width:]], axis=0)[:count].astype(BF16)


def swap(value, axis, k):
    size = lax.axis_size(axis)
    return lax.ppermute(value, axis, [(i, i ^ k) for i in range(size)])


def whole(array):
    return pl.BlockSpec(array.shape, lambda *_: (0,) * array.ndim)


def call(kernel, at, operands, outs, specs=None, out_specs=None, grid=(1,), scratch=(), limit=16, flops=0, moved=1024, name=None):
    specs, out_specs = specs or {}, out_specs or {}
    return pl.pallas_call(
        kernel,
        grid_spec=pltpu.PrefetchScalarGridSpec(
            num_scalar_prefetch=1,
            grid=grid,
            in_specs=[specs.get(i, whole(a)) for i, a in enumerate(operands)],
            out_specs=[out_specs.get(i, whole(o)) for i, o in enumerate(outs)],
            scratch_shapes=list(scratch),
        ),
        out_shape=list(outs),
        compiler_params=pltpu.CompilerParams(vmem_limit_bytes=limit * MIB),
        cost_estimate=pl.CostEstimate(flops=flops, bytes_accessed=moved, transcendentals=0),
        name=name,
    )(at, *operands)


def per_device(
    short_inputs,
    long_inputs,
    short_keys,
    short_values,
    long_keys,
    long_values,
    short_lengths,
    long_lengths,
    attn_gain,
    mlp_gain,
    query_scale,
    q_weight,
    k_weight,
    v_weight,
    o_weight,
    up_weight,
    down_weight,
):
    steps, count, model = short_inputs.shape
    long_count = long_inputs.shape[1]
    heads, head_dim = query_scale.shape
    width = heads * head_dim
    tp, seq = lax.axis_size("tp"), lax.axis_size("seq")
    slots = short_keys.shape[1]
    at = jnp.stack([lax.axis_index("seq"), lax.axis_index("tp")]).astype(jnp.int32)
    shape = jax.ShapeDtypeStruct
    in_hbm = pl.BlockSpec(memory_space=pltpu.HBM)
    short_len, long_len = short_lengths, long_lengths

    rows, lanes = width // 4, model // 2
    shares = (o_weight, up_weight.T, down_weight)
    eighth = pl.BlockSpec((rows, lanes), lambda _, at: ((at[0] % 8) // 2, at[0] % 2))
    (own,) = call(
        pack_kernel,
        at,
        shares,
        (shape((3, rows, lanes), BF16),),
        specs={0: eighth, 1: eighth, 2: eighth},
        limit=60,
        name="pack_weights",
    )
    units = [swap(own, "tp", k) for k in range(1, tp)]

    n = steps * GROUP
    step_rows = pl.BlockSpec((1, count, width), lambda i, at: (i, 0, 0))
    long_rows = pl.BlockSpec((1, GROUP, width), lambda i, at: (i, 0, 0))
    q, kn, vn, q_long, kn_long, vn_long = call(
        qkv_kernel,
        at,
        (short_inputs, long_inputs, attn_gain, query_scale, q_weight.T, k_weight.T, v_weight.T),
        (shape((steps, count, width), BF16),) * 3 + (shape((steps, GROUP, width), BF16),) * 3,
        specs={
            0: pl.BlockSpec((1, count, model), lambda i, at: (i, 0, 0)),
            1: pl.BlockSpec((1, long_count, model), lambda i, at: (i, 0, 0)),
            4: in_hbm,
            5: in_hbm,
            6: in_hbm,
        },
        out_specs={0: step_rows, 1: step_rows, 2: step_rows, 3: long_rows, 4: long_rows, 5: long_rows},
        grid=(steps,),
        scratch=(pltpu.VMEM((3 * width, model), BF16), pltpu.VMEM((count + GROUP, model), F32), pltpu.SemaphoreType.DMA((3,))),
        limit=60,
        name="qkv",
    )

    part_shape = shape((n, width + 64), F32)
    (part,) = call(functools.partial(long_kernel, heads), at, (q_long, long_keys, long_values, long_len), (part_shape,), name="long_partial")
    (part,) = call(functools.partial(pair_kernel, heads, width), at, (part, swap(part, "seq", 1)), (part_shape,), name="long_pair")
    parts = [part] + [swap(part, "seq", 2 * i) for i in range(1, seq // 2)]

    block = count // 2
    packed = shape((count // 2 + GROUP // 2, 2 * width), BF16)
    fresh_rows = pl.BlockSpec((steps, block, width), lambda i, at: (0, i, 0))
    cache_rows = pl.BlockSpec((block, slots, width), lambda i, at: (i, 0, 0))
    (att,) = call(
        functools.partial(short_kernel, heads),
        at,
        (q, kn, vn, short_keys, short_values, short_len, part),
        (shape((steps, count, width), BF16),),
        specs={0: fresh_rows, 1: fresh_rows, 2: fresh_rows, 3: cache_rows, 4: cache_rows, 6: in_hbm},
        out_specs={0: fresh_rows},
        grid=(count // block,),
        limit=60,
        name="short_attention",
    )
    att_sent = call(
        functools.partial(send_kernel, heads),
        at,
        (att, q_long, kn_long, vn_long, *parts),
        (packed,) * steps,
        scratch=(pltpu.VMEM((steps, GROUP, width), F32), pltpu.VMEM((seq // 2, n, width + 64), F32)),
        name="send_attended",
    )
    received = [att_sent[0]] + [swap(att_sent[k], "tp", k) for k in range(1, tp)]

    blocks = 3 * (tp - 1)
    cut = blocks // 2 + 1
    (mine,) = call(
        functools.partial(stack_kernel, tp - 1),
        at,
        (*units, att, *parts[1:]),
        (shape((blocks, rows, lanes), BF16),),
        specs={tp - 1 + i: in_hbm for i in range(len(parts))},
        name="stack_weights",
    )
    along_x, along_y = swap(mine, "seq", 2), swap(mine, "seq", 4)
    first, second = call(
        functools.partial(cut_kernel, cut),
        at,
        (along_x, along_y, *received[1:]),
        (shape((cut, rows, lanes), BF16), shape((blocks - cut, rows, lanes), BF16)),
        specs={2 + i: in_hbm for i in range(tp - 1)},
        name="cut_weights",
    )
    spread = [mine, along_x, along_y, swap(first, "seq", 2), swap(second, "seq", 4)]
    pieces = [piece for held in spread for piece in (held, swap(held, "seq", 1))]

    outs = call(
        functools.partial(mlp_kernel, tp),
        at,
        (short_inputs, long_inputs, mlp_gain, *received, *shares, *pieces),
        (packed,) * tp,
        specs={
            0: pl.BlockSpec((1, count, model), lambda _, at: (at[1], 0, 0)),
            1: pl.BlockSpec((1, long_count, model), lambda _, at: (at[1], 0, 0)),
            **{3 + tp + i: in_hbm for i in range(3 + len(pieces))},
        },
        scratch=(
            pltpu.VMEM((tp, *packed.shape), BF16),
            pltpu.VMEM((GROUP, model), F32),
            pltpu.VMEM((3, tp * width, model), BF16),
            pltpu.SemaphoreType.DMA((3 + 9 * (tp - 1),)),
        ),
        flops=2 * (count + GROUP) * model * model * 3,
        limit=36,
        name="feed_forward",
    )
    outs = [outs[0]] + [swap(outs[k], "tp", k) for k in range(1, tp)]
    return tuple(
        call(
            functools.partial(place_kernel, tp),
            at,
            outs,
            (shape((steps, count, width), BF16), shape((steps, long_count, width), BF16)),
            name="place_outputs",
        )
    )


def solution(mesh):
    return jax.shard_map(
        per_device,
        mesh=mesh,
        in_specs=(
            P(None, "seq", None),
            P(),
            P("seq", None, "tp"),
            P("seq", None, "tp"),
            P(None, "seq", "tp"),
            P(None, "seq", "tp"),
            P("seq"),
            P(),
            P(),
            P(),
            P("tp", None),
            P(None, "tp"),
            P(None, "tp"),
            P(None, "tp"),
            P("tp", None),
            P(None, "tp"),
            P("tp", None),
        ),
        out_specs=(P(None, "seq", "tp"), P(None, None, "tp")),
        check_vma=False,
    )
```

time: 560 us -> 117 us (0.21)
  waiting for transfers between devices: 352 us -> 53.7 us
  local copies, waits for them, and re-layouts: 63.9 us -> 6.53 us
  blocking collectives: 48.8 us -> 0 us
  matrix products: 48.2 us -> 0 us
  Pallas kernels: 0 us -> 34 us
  other arithmetic: 30 us -> 0.65 us
  starting transfers between devices: 0.08 us -> 20.4 us
  between operations: 14.5 us -> 0.92 us
    psum x1 -> x0, waiting for transfers between devices: 225 us -> none  [per_device(): residual_mid = flat_rows.astype(jnp.float32) + lax.psum(head_terms, 'tp')]
    unnamed x3 -> x0, waiting for transfers between devices: 127 us -> none
    ppermute x0 -> x22, waiting for transfers between devices: none -> 53.7 us  [swap(): return lax.ppermute(value, axis, [(i, i ^ k) for i in range(size)])]
    dot_general x12 -> x0, matrix products: 38.5 us -> none  [the longest x3 11.1 us: project_heads(): product = jnp.dot(flat_rows, weight, preferred_element_type=jnp.float32)]
    pallas_call x0 -> x10, Pallas kernels: none -> 34 us  [call(): pl.pallas_call(kernel, grid_spec=pltpu.PrefetchScalarGridSpec(num_scalar_...]
    psum x1 -> x0, blocking collectives: 24.7 us -> none  [per_device(): lax.psum((long_sum * factor, long_weighted * factor[..., None]), 'seq')]
    pmax x1 -> x0, blocking collectives: 24.1 us -> none  [per_device(): global_max = lax.pmax(long_max, 'seq')]
    ppermute x0 -> x22, starting transfers between devices: none -> 20.4 us  [swap(): return lax.ppermute(value, axis, [(i, i ^ k) for i in range(size)])]
  transfers between devices with their start and end apart: 2 -> 22, of which waited for: 2 -> 11; matrix products, arithmetic and copies ran while one was open for 2% -> 1% of each run, Pallas kernels for 0% -> 19%
where the time goes in v2:
time: 117 us; the launch traced here: 116 us
  waiting for transfers between devices  53.7 us (46%)
  Pallas kernels  34 us (29%)
  starting transfers between devices  20.4 us (17%)
  local copies, waits for them, and re-layouts  6.53 us (6%)
    ppermute x22, waiting for transfers between devices, swap(): return lax.ppermute(value, axis, [(i, i ^ k) for i in range(size)])  53.7 us
    pallas_call x10, Pallas kernels, call(): pl.pallas_call(kernel, grid_spec=pltpu.PrefetchScalarGridSpec(num_scalar_...  34 us
    ppermute x22, starting transfers between devices, swap(): return lax.ppermute(value, axis, [(i, i ^ k) for i in range(size)])  20.4 us
    unnamed x39, local copies, waits for them, and re-layouts  5.9 us
  transfers between devices with their start and end apart: 22, of which 11 were waited for; matrix products, arithmetic and copies ran while one was open for 1% of the time, Pallas kernels for 19%

profile of v2, /device:TPU:8, one launch (start us, length us, event | category | flops | bytes accessed | tf_op | source)
XLA Modules:
  0.0 116.2 jit_solution(4040063420827541607)
XLA Ops:
  0.6 0.7 pad_add_fusion.at_ref
  1.3 2.5 %pack_weights.1 = bf16[3,80,640]{2,1,0:T(8,128)(2,1)} custom-call(s32[2]{0:T(128)} %pad_add_fusion.at_ref, bf16[320,1280]{1,0:T(8,128)(2,1)} %refs_4_.1, bf16[320,1280]{1,0:T(8,128)(2,1)} %bitcast.6, bf16[320,1280]{1,0:T(8,128)(2,1)} %refs_6_.1), custom_call_target="tpu_custom_call" | custom-call | bytes 1024 | tf_op jit(solution)/shard_map/pack_weights/pallas_call | solution.py:312
  3.8 1.6 %collective-permute-start.9 = (bf16[3,80,640]{2,1,0:T(8,128)(2,1)}, bf16[3,80,640]{2,1,0:T(8,128)(2,1)S(1)}, u32[]{:S(2)}, u32[]{:S(2)}) collective-permute-start(bf16[3,80,640]{2,1,0:T(8,128)(2,1)} %pack_weights.1), channel_id=1, source_target_pairs={{0,3},{1,2},{2,1},{3,0},{4,7},{5,6},{6,5},{7,4},{8,11},{9,10},{10,... | collective-permute-start | bytes 921608 | tf_op jit(solution)/shard_map/ppermute | solution.py:303
  5.4 1.0 collective-permute-start.8
  6.4 1.5 %collective-permute-start.7 = (bf16[3,80,640]{2,1,0:T(8,128)(2,1)}, bf16[3,80,640]{2,1,0:T(8,128)(2,1)S(1)}, u32[]{:S(2)}, u32[]{:S(2)}) collective-permute-start(bf16[3,80,640]{2,1,0:T(8,128)(2,1)} %pack_weights.1), channel_id=1, source_target_pairs={{0,1},{1,0},{2,3},{3,2},{4,5},{5,4},{6,7},{7,6},{8,9},{9,8},{10,11... | collective-permute-start | bytes 921608 | tf_op jit(solution)/shard_map/ppermute | solution.py:303
  7.9 1.6 %copy.20.xl_ref = bf16[4,12,1280]{2,1,0:T(8,128)(2,1)} copy(bf16[4,12,1280]{2,0,1:T(4,128)(2,1)} %param.18) | data formatting | bytes 245760 | tf_op args[1]
  9.5 9.7 %qkv.1 = (bf16[4,320,320]{2,1,0:T(8,128)(2,1)}, bf16[4,320,320]{2,1,0:T(8,128)(2,1)}, bf16[4,320,320]{2,1,0:T(8,128)(2,1)}, bf16[4,16,320]{2,1,0:T(8,128)(2,1)},...) custom-call(s32[2]{0:T(128)} %pad_add_fusion.at_ref, bf16[4,320,1280]{2,1,0:T(8,128)(2,1)} %x_ref.3, ...), custom_call_target="tpu_custom_call" | custom-call | bytes 1024 | tf_op jit(solution)/shard_map/qkv/pallas_call | solution.py:312
  19.2 0.8 copy-done.9
  20.0 1.1 long_partial.1.mine_ref
  21.1 0.1 collective-permute-start
  21.2 1.3 %collective-permute-done.other_ref = f32[64,384]{1,0:T(8,128)S(1)} collective-permute-done((f32[64,384]{1,0:T(8,128)S(1)}, f32[64,384]{1,0:T(8,128)S(1)}, u32[]{:S(2)}, u32[]{:S(2)}) %collective-permute-start) | collective-permute-done | bytes 98336 | tf_op jit(solution)/shard_map/ppermute | solution.py:303
  22.5 0.9 long_pair.1.refs_0_
  23.4 2.5 %collective-permute-start.3 = (f32[64,384]{1,0:T(8,128)S(1)}, f32[64,384]{1,0:T(8,128)S(1)}, u32[]{:S(2)}, u32[]{:S(2)}) collective-permute-start(f32[64,384]{1,0:T(8,128)S(1)} %long_pair.1.refs_0_), channel_id=1, source_target_pairs={{0,24},{4,28},{8,16},{12,20},{16,8},{20,12},{24,0},{28,4},{1,25},{... | collective-permute-start | bytes 294920 | tf_op jit(solution)/shard_map/ppermute | solution.py:303
  26.0 0.5 collective-permute-start.2
  26.5 2.9 %collective-permute-done.3.refs_3_.refs_6_ = f32[64,384]{1,0:T(8,128)S(1)} collective-permute-done((f32[64,384]{1,0:T(8,128)S(1)}, f32[64,384]{1,0:T(8,128)S(1)}, u32[]{:S(2)}, u32[]{:S(2)}) %collective-permute-start.3) | collective-permute-done | bytes 98336 | tf_op jit(solution)/shard_map/ppermute | solution.py:303
  29.3 1.5 %collective-permute-start.1 = (f32[64,384]{1,0:T(8,128)S(1)}, f32[64,384]{1,0:T(8,128)S(1)}, u32[]{:S(2)}, u32[]{:S(2)}) collective-permute-start(f32[64,384]{1,0:T(8,128)S(1)} %long_pair.1.refs_0_), channel_id=1, source_target_pairs={{0,8},{4,12},{8,0},{12,4},{16,24},{20,28},{24,16},{28,20},{1,9},{5... | collective-permute-start | bytes 294920 | tf_op jit(solution)/shard_map/ppermute | solution.py:303
  30.9 0.0 copy-start.5
  30.9 0.0 copy-start.17
  30.9 8.3 %short_attention.1.att_ref.refs_3_ = bf16[4,320,320]{2,1,0:T(8,128)(2,1)} custom-call(s32[2]{0:T(128)} %pad_add_fusion.at_ref, bf16[4,320,320]{2,1,0:T(8,128)(2,1)} %get-tuple-element.18.q_ref, bf16[4,320,320]{2,1,0:T(8,128)(2,1)} %get-tuple-element.19.kn_ref, bf16[4,320,320]{2,1,0:T(8,128)(2,1)} %get-tuple-element.20.vn_ref, bf16[320,16,320]{2,1,0:T(8,128)(2,1)} %k_ref.3, ...), custom_call_target="tpu_custom_call" | custom-call | bytes 1024 | tf_op jit(solution)/shard_map/short_attention/pallas_call | solution.py:312
  39.3 1.3 %copy-done.1 = bf16[4,320,320]{2,1,0:T(8,128)(2,1)S(1)} copy-done((bf16[4,320,320]{2,1,0:T(8,128)(2,1)S(1)}, bf16[4,320,320]{2,1,0:T(8,128)(2,1)}, u32[]{:S(2)}) %copy-start.1) | copy-done | bytes 819224
  40.6 0.6 stack_weights.1.refs_7_
  41.3 1.6 %collective-permute-start.13 = (bf16[9,80,640]{2,1,0:T(8,128)(2,1)S(1)}, bf16[9,80,640]{2,1,0:T(8,128)(2,1)S(1)}, u32[]{:S(2)}, u32[]{:S(2)}) collective-permute-start(bf16[9,80,640]{2,1,0:T(8,128)(2,1)S(1)} %stack_weights.1.refs_7_), channel_id=1, source_target_pairs={{0,16},{4,20},{8,24},{12,28},{16,0},{20,4},{24,8},{28,12},{1,17},{... | collective-permute-start | bytes 2764808 | tf_op jit(solution)/shard_map/ppermute | solution.py:303
  42.8 0.5 collective-permute-start.11
  43.4 1.2 %copy-done.2 = bf16[4,320,320]{2,1,0:T(8,128)(2,1)S(1)} copy-done((bf16[4,320,320]{2,1,0:T(8,128)(2,1)S(1)}, bf16[4,320,320]{2,1,0:T(8,128)(2,1)}, u32[]{:S(2)}) %copy-start.2) | copy-done | bytes 819224
  44.6 0.9 copy-done.8
  45.5 2.1 %send_attended.1 = (bf16[168,640]{1,0:T(8,128)(2,1)S(1)}, bf16[168,640]{1,0:T(8,128)(2,1)S(1)}, bf16[168,640]{1,0:T(8,128)(2,1)S(1)}, bf16[168,640]{1,0:T(8,128)(2,1)S(1)}) custom-call(s32[2]{0:T(128)S(1)} %copy-done.14, bf16[4,320,320]{2,1,0:T(8,128)(2,1)S(1)} %copy-done.2, bf16[4,16,320]{2,1,0:T(8,128)(2,1)S(1)} %copy-done.10, ...), custom_call_target="tpu_custom_call" | custom-call | bytes 1024 | tf_op jit(solution)/shard_map/send_attended/pallas_call | solution.py:312
  47.6 0.9 collective-permute-start.4
  48.5 2.2 %collective-permute-start.5 = (bf16[168,640]{1,0:T(8,128)(2,1)S(1)}, bf16[168,640]{1,0:T(8,128)(2,1)S(1)}, u32[]{:S(2)}, u32[]{:S(2)}) collective-permute-start(bf16[168,640]{1,0:T(8,128)(2,1)S(1)} %get-tuple-element.26), channel_id=1, source_target_pairs={{0,2},{1,3},{2,0},{3,1},{4,6},{5,7},{6,4},{7,5},{8,10},{9,11},{10,... | collective-permute-start | bytes 645128 | tf_op jit(solution)/shard_map/ppermute | solution.py:303
  50.7 0.5 collective-permute-start.6
  51.2 4.6 %collective-permute-done.4.refs_0_.refs_1_ = bf16[168,640]{1,0:T(8,128)(2,1)S(1)} collective-permute-done((bf16[168,640]{1,0:T(8,128)(2,1)S(1)}, bf16[168,640]{1,0:T(8,128)(2,1)S(1)}, u32[]{:S(2)}, u32[]{:S(2)}) %collective-permute-start.4) | collective-permute-done | bytes 215072 | tf_op jit(solution)/shard_map/ppermute | solution.py:303
  55.8 9.1 %collective-permute-done.5.refs_1_.refs_2_ = bf16[168,640]{1,0:T(8,128)(2,1)S(1)} collective-permute-done((bf16[168,640]{1,0:T(8,128)(2,1)S(1)}, bf16[168,640]{1,0:T(8,128)(2,1)S(1)}, u32[]{:S(2)}, u32[]{:S(2)}) %collective-permute-start.5) | collective-permute-done | bytes 215072 | tf_op jit(solution)/shard_map/ppermute | solution.py:303
  64.9 3.7 %collective-permute-done.6.refs_2_.refs_3_ = bf16[168,640]{1,0:T(8,128)(2,1)S(1)} collective-permute-done((bf16[168,640]{1,0:T(8,128)(2,1)S(1)}, bf16[168,640]{1,0:T(8,128)(2,1)S(1)}, u32[]{:S(2)}, u32[]{:S(2)}) %collective-permute-start.6) | collective-permute-done | bytes 215072 | tf_op jit(solution)/shard_map/ppermute | solution.py:303
  68.6 0.6 cut_weights.1
  69.2 1.6 %collective-permute-start.15 = (bf16[5,80,640]{2,1,0:T(8,128)(2,1)S(1)}, bf16[5,80,640]{2,1,0:T(8,128)(2,1)S(1)}, u32[]{:S(2)}, u32[]{:S(2)}) collective-permute-start(bf16[5,80,640]{2,1,0:T(8,128)(2,1)S(1)} %get-tuple-element.28), channel_id=1, source_target_pairs={{0,8},{4,12},{8,0},{12,4},{16,24},{20,28},{24,16},{28,20},{1,9},{5... | collective-permute-start | bytes 1536008 | tf_op jit(solution)/shard_map/ppermute | solution.py:303
  70.8 0.5 collective-permute-start.14
  71.3 0.5 collective-permute-start.17
  71.8 8.9 %collective-permute-done.15.refs_13_ = bf16[5,80,640]{2,1,0:T(8,128)(2,1)S(1)} collective-permute-done((bf16[5,80,640]{2,1,0:T(8,128)(2,1)S(1)}, bf16[5,80,640]{2,1,0:T(8,128)(2,1)S(1)}, u32[]{:S(2)}, u32[]{:S(2)}) %collective-permute-start.15) | collective-permute-done | bytes 512032 | tf_op jit(solution)/shard_map/ppermute | solution.py:303
  80.7 2.5 %collective-permute-done.17.refs_15_ = bf16[4,80,640]{2,1,0:T(8,128)(2,1)S(1)} collective-permute-done((bf16[4,80,640]{2,1,0:T(8,128)(2,1)S(1)}, bf16[4,80,640]{2,1,0:T(8,128)(2,1)S(1)}, u32[]{:S(2)}, u32[]{:S(2)}) %collective-permute-start.17) | collective-permute-done | bytes 409632 | tf_op jit(solution)/shard_map/ppermute | solution.py:303
  83.2 1.7 %collective-permute-done.18.refs_16_ = bf16[4,80,640]{2,1,0:T(8,128)(2,1)S(1)} collective-permute-done((bf16[4,80,640]{2,1,0:T(8,128)(2,1)S(1)}, bf16[4,80,640]{2,1,0:T(8,128)(2,1)S(1)}, u32[]{:S(2)}, u32[]{:S(2)}) %collective-permute-start.18) | collective-permute-done | bytes 409632 | tf_op jit(solution)/shard_map/ppermute | solution.py:303
  85.0 6.4 %feed_forward.1 = (bf16[168,640]{1,0:T(8,128)(2,1)S(1)}, bf16[168,640]{1,0:T(8,128)(2,1)S(1)}, bf16[168,640]{1,0:T(8,128)(2,1)S(1)}, bf16[168,640]{1,0:T(8,128)(2,1)S(1)}) custom-call(s32[2]{0:T(128)S(1)} %copy-done.14, bf16[4,320,1280]{2,1,0:T(8,128)(2,1)S(1)} %copy-done, bf16[4,12,1280]{2,1,0:T(8,128)(2,1)S(1)} %copy-done.6, f32[1280]{0:T(1024)S(1)} %copy-done.17, ...), custom_call_target="tpu_custom_call" | custom-call | flops 3303014400 | bytes 1024 | tf_op jit(solution)/shard_map/feed_forward/pallas_call | solution.py:312
  91.4 0.1 collective-permute-start.19
  91.5 3.0 %collective-permute-start.20 = (bf16[168,640]{1,0:T(8,128)(2,1)S(1)}, bf16[168,640]{1,0:T(8,128)(2,1)S(1)}, u32[]{:S(2)}, u32[]{:S(2)}) collective-permute-start(bf16[168,640]{1,0:T(8,128)(2,1)S(1)} %get-tuple-element.32), channel_id=1, source_target_pairs={{0,2},{1,3},{2,0},{3,1},{4,6},{5,7},{6,4},{7,5},{8,10},{9,11},{10,... | collective-permute-start | bytes 645128 | tf_op jit(solution)/shard_map/ppermute | solution.py:303
  94.5 0.5 collective-permute-start.21
  95.0 5.7 %collective-permute-done.19.refs_1_ = bf16[168,640]{1,0:T(8,128)(2,1)S(1)} collective-permute-done((bf16[168,640]{1,0:T(8,128)(2,1)S(1)}, bf16[168,640]{1,0:T(8,128)(2,1)S(1)}, u32[]{:S(2)}, u32[]{:S(2)}) %collective-permute-start.19) | collective-permute-done | bytes 215072 | tf_op jit(solution)/shard_map/ppermute | solution.py:303
  100.6 8.8 %collective-permute-done.20.refs_2_ = bf16[168,640]{1,0:T(8,128)(2,1)S(1)} collective-permute-done((bf16[168,640]{1,0:T(8,128)(2,1)S(1)}, bf16[168,640]{1,0:T(8,128)(2,1)S(1)}, u32[]{:S(2)}, u32[]{:S(2)}) %collective-permute-start.20) | collective-permute-done | bytes 215072 | tf_op jit(solution)/shard_map/ppermute | solution.py:303
  109.4 4.5 %collective-permute-done.21.refs_3_ = bf16[168,640]{1,0:T(8,128)(2,1)S(1)} collective-permute-done((bf16[168,640]{1,0:T(8,128)(2,1)S(1)}, bf16[168,640]{1,0:T(8,128)(2,1)S(1)}, u32[]{:S(2)}, u32[]{:S(2)}) %collective-permute-start.21) | collective-permute-done | bytes 215072 | tf_op jit(solution)/shard_map/ppermute | solution.py:303
  113.9 1.7 %place_outputs.1 = (bf16[4,320,320]{2,1,0:T(8,128)(2,1)}, bf16[4,12,320]{2,1,0:T(8,128)(2,1)S(1)}) custom-call(s32[2]{0:T(128)S(1)} %copy-done.14, bf16[168,640]{1,0:T(8,128)(2,1)S(1)} %get-tuple-element.30.refs_0_, bf16[168,640]{1,0:T(8,128)(2,1)S(1)} %collective-permute-done.19.refs_1_, bf16[168,640]{1,0:T(8,128)(2,1)S(1)} %collective-permute-done.20.refs_2_, ...), custom_call_target="tpu_custom_call" | custom-call | bytes 1024 | tf_op jit(solution)/shard_map/place_outputs/pallas_call | solution.py:312
  115.6 0.6 copy.21
  (47 shorter events, 0.1 us)
Async XLA Ops:
  1.3 17.9 %copy-start.11 = (bf16[12,16,320]{2,1,0:T(8,128)(2,1)S(1)}, bf16[12,16,320]{2,1,0:T(8,128)(2,1)}, u32[]{:S(2)}) copy-start(bf16[12,16,320]{2,1,0:T(8,128)(2,1)} %k_ref.2) | copy-start | bytes 368644
  1.3 17.9 %copy-start.12 = (bf16[12,16,320]{2,1,0:T(8,128)(2,1)S(1)}, bf16[12,16,320]{2,1,0:T(8,128)(2,1)}, u32[]{:S(2)}) copy-start(bf16[12,16,320]{2,1,0:T(8,128)(2,1)} %v_ref.2) | copy-start | bytes 368644
  1.3 17.9 %copy-start.13 = (s32[2]{0:T(128)S(1)}, s32[2]{0:T(128)}, u32[]{:S(2)}) copy-start(s32[2]{0:T(128)} %pad_add_fusion.at_ref) | copy-start | bytes 28
  1.3 17.9 %copy-start.18 = (s32[12]{0:T(128)S(1)}, s32[12]{0:T(128)}, u32[]{:S(2)}) copy-start(s32[12]{0:T(128)} %len_ref.2) | copy-start | bytes 148
  3.8 35.4 %collective-permute-start.9 = (bf16[3,80,640]{2,1,0:T(8,128)(2,1)}, bf16[3,80,640]{2,1,0:T(8,128)(2,1)S(1)}, u32[]{:S(2)}, u32[]{:S(2)}) collective-permute-start(bf16[3,80,640]{2,1,0:T(8,128)(2,1)} %pack_weights.1), channel_id=1, source_target_pairs={{0,3},{1,2},{2,1},{3,0},{4,7},{5,6},{6,5},{7,4},{8,11},{9,10},{10,... | collective-permute-start | bytes 921608 | tf_op jit(solution)/shard_map/ppermute | solution.py:303
  5.4 33.8 %collective-permute-start.8 = (bf16[3,80,640]{2,1,0:T(8,128)(2,1)}, bf16[3,80,640]{2,1,0:T(8,128)(2,1)S(1)}, u32[]{:S(2)}, u32[]{:S(2)}) collective-permute-start(bf16[3,80,640]{2,1,0:T(8,128)(2,1)} %pack_weights.1), channel_id=1, source_target_pairs={{0,2},{1,3},{2,0},{3,1},{4,6},{5,7},{6,4},{7,5},{8,10},{9,11},{10,... | collective-permute-start | bytes 921608 | tf_op jit(solution)/shard_map/ppermute | solution.py:303
  6.4 32.8 %collective-permute-start.7 = (bf16[3,80,640]{2,1,0:T(8,128)(2,1)}, bf16[3,80,640]{2,1,0:T(8,128)(2,1)S(1)}, u32[]{:S(2)}, u32[]{:S(2)}) collective-permute-start(bf16[3,80,640]{2,1,0:T(8,128)(2,1)} %pack_weights.1), channel_id=1, source_target_pairs={{0,1},{1,0},{2,3},{3,2},{4,5},{5,4},{6,7},{7,6},{8,9},{9,8},{10,11... | collective-permute-start | bytes 921608 | tf_op jit(solution)/shard_map/ppermute | solution.py:303
  19.2 0.8 copy-start.9
  21.1 1.4 %collective-permute-start = (f32[64,384]{1,0:T(8,128)S(1)}, f32[64,384]{1,0:T(8,128)S(1)}, u32[]{:S(2)}, u32[]{:S(2)}) collective-permute-start(f32[64,384]{1,0:T(8,128)S(1)} %long_partial.1.mine_ref), channel_id=1, source_target_pairs={{0,4},{4,0},{8,12},{12,8},{16,20},{20,16},{24,28},{28,24},{1,5},{5... | collective-permute-start | bytes 294920 | tf_op jit(solution)/shard_map/ppermute | solution.py:303
  23.4 7.4 %copy-start.7 = (f32[64,384]{1,0:T(8,128)}, f32[64,384]{1,0:T(8,128)S(1)}, u32[]{:S(2)}) copy-start(f32[64,384]{1,0:T(8,128)S(1)} %long_pair.1.refs_0_) | copy-start | bytes 294916
  23.4 5.9 %collective-permute-start.3 = (f32[64,384]{1,0:T(8,128)S(1)}, f32[64,384]{1,0:T(8,128)S(1)}, u32[]{:S(2)}, u32[]{:S(2)}) collective-permute-start(f32[64,384]{1,0:T(8,128)S(1)} %long_pair.1.refs_0_), channel_id=1, source_target_pairs={{0,24},{4,28},{8,16},{12,20},{16,8},{20,12},{24,0},{28,4},{1,25},{... | collective-permute-start | bytes 294920 | tf_op jit(solution)/shard_map/ppermute | solution.py:303
  26.0 13.3 %collective-permute-start.2 = (f32[64,384]{1,0:T(8,128)S(1)}, f32[64,384]{1,0:T(8,128)S(1)}, u32[]{:S(2)}, u32[]{:S(2)}) collective-permute-start(f32[64,384]{1,0:T(8,128)S(1)} %long_pair.1.refs_0_), channel_id=1, source_target_pairs={{0,16},{4,20},{8,24},{12,28},{16,0},{20,4},{24,8},{28,12},{1,17},{... | collective-permute-start | bytes 294920 | tf_op jit(solution)/shard_map/ppermute | solution.py:303
  29.3 9.9 %collective-permute-start.1 = (f32[64,384]{1,0:T(8,128)S(1)}, f32[64,384]{1,0:T(8,128)S(1)}, u32[]{:S(2)}, u32[]{:S(2)}) collective-permute-start(f32[64,384]{1,0:T(8,128)S(1)} %long_pair.1.refs_0_), channel_id=1, source_target_pairs={{0,8},{4,12},{8,0},{12,4},{16,24},{20,28},{24,16},{28,20},{1,9},{5... | collective-permute-start | bytes 294920 | tf_op jit(solution)/shard_map/ppermute | solution.py:303
  30.8 8.4 %copy-start.14 = (s32[2]{0:T(128)S(1)}, s32[2]{0:T(128)}, u32[]{:S(2)}) copy-start(s32[2]{0:T(128)} %pad_add_fusion.at_ref) | copy-start | bytes 28
  30.8 12.5 %copy-start.10 = (bf16[4,16,320]{2,1,0:T(8,128)(2,1)S(1)}, bf16[4,16,320]{2,1,0:T(8,128)(2,1)}, u32[]{:S(2)}) copy-start(bf16[4,16,320]{2,1,0:T(8,128)(2,1)} %get-tuple-element.21.q_ref.ql_ref) | copy-start | bytes 122884
  30.9 12.5 %copy-start.15 = (bf16[4,16,320]{2,1,0:T(8,128)(2,1)S(1)}, bf16[4,16,320]{2,1,0:T(8,128)(2,1)}, u32[]{:S(2)}) copy-start(bf16[4,16,320]{2,1,0:T(8,128)(2,1)} %get-tuple-element.22.knl_ref) | copy-start | bytes 122884
  30.9 12.5 %copy-start.16 = (bf16[4,16,320]{2,1,0:T(8,128)(2,1)S(1)}, bf16[4,16,320]{2,1,0:T(8,128)(2,1)}, u32[]{:S(2)}) copy-start(bf16[4,16,320]{2,1,0:T(8,128)(2,1)} %get-tuple-element.23.vnl_ref) | copy-start | bytes 122884
  30.9 54.1 %copy-start.3 = (bf16[320,1280]{1,0:T(8,128)(2,1)S(1)}, bf16[320,1280]{1,0:T(8,128)(2,1)}, u32[]{:S(2)}) copy-start(bf16[320,1280]{1,0:T(8,128)(2,1)} %refs_4_.1) | copy-start | bytes 2457604
  30.9 54.1 %copy-start.4 = (bf16[1280,320]{0,1:T(8,128)(2,1)S(1)}, bf16[1280,320]{0,1:T(8,128)(2,1)}, u32[]{:S(2)}) copy-start(bf16[1280,320]{0,1:T(8,128)(2,1)} %param.32) | copy-start | bytes 2457604
  30.9 54.1 %copy-start.5 = (bf16[320,1280]{1,0:T(8,128)(2,1)S(1)}, bf16[320,1280]{1,0:T(8,128)(2,1)}, u32[]{:S(2)}) copy-start(bf16[320,1280]{1,0:T(8,128)(2,1)} %refs_6_.1) | copy-start | bytes 2457604
  30.9 54.1 %copy-start.6 = (bf16[4,12,1280]{2,1,0:T(8,128)(2,1)S(1)}, bf16[4,12,1280]{2,1,0:T(8,128)(2,1)}, u32[]{:S(2)}) copy-start(bf16[4,12,1280]{2,1,0:T(8,128)(2,1)} %copy.20.xl_ref) | copy-start | bytes 368644
  30.9 54.1 %copy-start.17 = (f32[1280]{0:T(1024)S(1)}, f32[1280]{0:T(1024)}, u32[]{:S(2)}) copy-start(f32[1280]{0:T(1024)} %gain_ref.3) | copy-start | bytes 15364
  39.2 45.8 %copy-start = (bf16[4,320,1280]{2,1,0:T(8,128)(2,1)S(1)}, bf16[4,320,1280]{2,1,0:T(8,128)(2,1)}, u32[]{:S(2)}) copy-start(bf16[4,320,1280]{2,1,0:T(8,128)(2,1)} %x_ref.3) | copy-start | bytes 9830404
  39.3 1.4 %copy-start.1 = (bf16[4,320,320]{2,1,0:T(8,128)(2,1)S(1)}, bf16[4,320,320]{2,1,0:T(8,128)(2,1)}, u32[]{:S(2)}) copy-start(bf16[4,320,320]{2,1,0:T(8,128)(2,1)} %short_attention.1.att_ref.refs_3_) | copy-start | bytes 2457604
  41.3 27.4 %collective-permute-start.13 = (bf16[9,80,640]{2,1,0:T(8,128)(2,1)S(1)}, bf16[9,80,640]{2,1,0:T(8,128)(2,1)S(1)}, u32[]{:S(2)}, u32[]{:S(2)}) collective-permute-start(bf16[9,80,640]{2,1,0:T(8,128)(2,1)S(1)} %stack_weights.1.refs_7_), channel_id=1, source_target_pairs={{0,16},{4,20},{8,24},{12,28},{16,0},{20,4},{24,8},{28,12},{1,17},{... | collective-permute-start | bytes 2764808 | tf_op jit(solution)/shard_map/ppermute | solution.py:303
  42.8 25.8 %collective-permute-start.11 = (bf16[9,80,640]{2,1,0:T(8,128)(2,1)S(1)}, bf16[9,80,640]{2,1,0:T(8,128)(2,1)S(1)}, u32[]{:S(2)}, u32[]{:S(2)}) collective-permute-start(bf16[9,80,640]{2,1,0:T(8,128)(2,1)S(1)} %stack_weights.1.refs_7_), channel_id=1, source_target_pairs={{0,8},{4,12},{8,0},{12,4},{16,24},{20,28},{24,16},{28,20},{1,9},{5... | collective-permute-start | bytes 2764808 | tf_op jit(solution)/shard_map/ppermute | solution.py:303
  43.4 1.2 %copy-start.2 = (bf16[4,320,320]{2,1,0:T(8,128)(2,1)S(1)}, bf16[4,320,320]{2,1,0:T(8,128)(2,1)}, u32[]{:S(2)}) copy-start(bf16[4,320,320]{2,1,0:T(8,128)(2,1)} %short_attention.1.att_ref.refs_3_) | copy-start | bytes 2457604
  44.6 0.9 copy-start.8
  47.6 8.2 %collective-permute-start.4 = (bf16[168,640]{1,0:T(8,128)(2,1)S(1)}, bf16[168,640]{1,0:T(8,128)(2,1)S(1)}, u32[]{:S(2)}, u32[]{:S(2)}) collective-permute-start(bf16[168,640]{1,0:T(8,128)(2,1)S(1)} %get-tuple-element.25), channel_id=1, source_target_pairs={{0,1},{1,0},{2,3},{3,2},{4,5},{5,4},{6,7},{7,6},{8,9},{9,8},{10,11... | collective-permute-start | bytes 645128 | tf_op jit(solution)/shard_map/ppermute | solution.py:303
  48.5 16.5 %collective-permute-start.5 = (bf16[168,640]{1,0:T(8,128)(2,1)S(1)}, bf16[168,640]{1,0:T(8,128)(2,1)S(1)}, u32[]{:S(2)}, u32[]{:S(2)}) collective-permute-start(bf16[168,640]{1,0:T(8,128)(2,1)S(1)} %get-tuple-element.26), channel_id=1, source_target_pairs={{0,2},{1,3},{2,0},{3,1},{4,6},{5,7},{6,4},{7,5},{8,10},{9,11},{10,... | collective-permute-start | bytes 645128 | tf_op jit(solution)/shard_map/ppermute | solution.py:303
  50.7 17.9 %collective-permute-start.6 = (bf16[168,640]{1,0:T(8,128)(2,1)S(1)}, bf16[168,640]{1,0:T(8,128)(2,1)S(1)}, u32[]{:S(2)}, u32[]{:S(2)}) collective-permute-start(bf16[168,640]{1,0:T(8,128)(2,1)S(1)} %get-tuple-element.27), channel_id=1, source_target_pairs={{0,3},{1,2},{2,1},{3,0},{4,7},{5,6},{6,5},{7,4},{8,11},{9,10},{10,... | collective-permute-start | bytes 645128 | tf_op jit(solution)/shard_map/ppermute | solution.py:303
  69.2 11.5 %collective-permute-start.15 = (bf16[5,80,640]{2,1,0:T(8,128)(2,1)S(1)}, bf16[5,80,640]{2,1,0:T(8,128)(2,1)S(1)}, u32[]{:S(2)}, u32[]{:S(2)}) collective-permute-start(bf16[5,80,640]{2,1,0:T(8,128)(2,1)S(1)} %get-tuple-element.28), channel_id=1, source_target_pairs={{0,8},{4,12},{8,0},{12,4},{16,24},{20,28},{24,16},{28,20},{1,9},{5... | collective-permute-start | bytes 1536008 | tf_op jit(solution)/shard_map/ppermute | solution.py:303
  70.8 12.4 %collective-permute-start.10 = (bf16[9,80,640]{2,1,0:T(8,128)(2,1)S(1)}, bf16[9,80,640]{2,1,0:T(8,128)(2,1)S(1)}, u32[]{:S(2)}, u32[]{:S(2)}) collective-permute-start(bf16[9,80,640]{2,1,0:T(8,128)(2,1)S(1)} %stack_weights.1.refs_7_), channel_id=1, source_target_pairs={{0,4},{4,0},{8,12},{12,8},{16,20},{20,16},{24,28},{28,24},{1,5},{5... | collective-permute-start | bytes 2764808 | tf_op jit(solution)/shard_map/ppermute | solution.py:303
  70.8 14.1 %collective-permute-start.14 = (bf16[9,80,640]{2,1,0:T(8,128)(2,1)S(1)}, bf16[9,80,640]{2,1,0:T(8,128)(2,1)S(1)}, u32[]{:S(2)}, u32[]{:S(2)}) collective-permute-start(bf16[9,80,640]{2,1,0:T(8,128)(2,1)S(1)} %collective-permute-done.13.y_ref.refs_11_), channel_id=1, source_target_pairs={{0,4},{4,0},{8,12},{12,8},{16,20},{20,16},{24,28},{28,24},{1,5},{5... | collective-permute-start | bytes 2764808 | tf_op jit(solution)/shard_map/ppermute | solution.py:303
  71.3 13.6 %collective-permute-start.12 = (bf16[9,80,640]{2,1,0:T(8,128)(2,1)S(1)}, bf16[9,80,640]{2,1,0:T(8,128)(2,1)S(1)}, u32[]{:S(2)}, u32[]{:S(2)}) collective-permute-start(bf16[9,80,640]{2,1,0:T(8,128)(2,1)S(1)} %collective-permute-done.11.x_ref.refs_9_), channel_id=1, source_target_pairs={{0,4},{4,0},{8,12},{12,8},{16,20},{20,16},{24,28},{28,24},{1,5},{5... | collective-permute-start | bytes 2764808 | tf_op jit(solution)/shard_map/ppermute | solution.py:303
  71.3 11.9 %collective-permute-start.17 = (bf16[4,80,640]{2,1,0:T(8,128)(2,1)S(1)}, bf16[4,80,640]{2,1,0:T(8,128)(2,1)S(1)}, u32[]{:S(2)}, u32[]{:S(2)}) collective-permute-start(bf16[4,80,640]{2,1,0:T(8,128)(2,1)S(1)} %get-tuple-element.29), channel_id=1, source_target_pairs={{0,16},{4,20},{8,24},{12,28},{16,0},{20,4},{24,8},{28,12},{1,17},{... | collective-permute-start | bytes 1228808 | tf_op jit(solution)/shard_map/ppermute | solution.py:303
  80.7 4.3 %collective-permute-start.16 = (bf16[5,80,640]{2,1,0:T(8,128)(2,1)S(1)}, bf16[5,80,640]{2,1,0:T(8,128)(2,1)S(1)}, u32[]{:S(2)}, u32[]{:S(2)}) collective-permute-start(bf16[5,80,640]{2,1,0:T(8,128)(2,1)S(1)} %collective-permute-done.15.refs_13_), channel_id=1, source_target_pairs={{0,4},{4,0},{8,12},{12,8},{16,20},{20,16},{24,28},{28,24},{1,5},{5... | collective-permute-start | bytes 1536008 | tf_op jit(solution)/shard_map/ppermute | solution.py:303
  83.2 1.7 %collective-permute-start.18 = (bf16[4,80,640]{2,1,0:T(8,128)(2,1)S(1)}, bf16[4,80,640]{2,1,0:T(8,128)(2,1)S(1)}, u32[]{:S(2)}, u32[]{:S(2)}) collective-permute-start(bf16[4,80,640]{2,1,0:T(8,128)(2,1)S(1)} %collective-permute-done.17.refs_15_), channel_id=1, source_target_pairs={{0,4},{4,0},{8,12},{12,8},{16,20},{20,16},{24,28},{28,24},{1,5},{5... | collective-permute-start | bytes 1228808 | tf_op jit(solution)/shard_map/ppermute | solution.py:303
  91.4 9.2 %collective-permute-start.19 = (bf16[168,640]{1,0:T(8,128)(2,1)S(1)}, bf16[168,640]{1,0:T(8,128)(2,1)S(1)}, u32[]{:S(2)}, u32[]{:S(2)}) collective-permute-start(bf16[168,640]{1,0:T(8,128)(2,1)S(1)} %get-tuple-element.31), channel_id=1, source_target_pairs={{0,1},{1,0},{2,3},{3,2},{4,5},{5,4},{6,7},{7,6},{8,9},{9,8},{10,11... | collective-permute-start | bytes 645128 | tf_op jit(solution)/shard_map/ppermute | solution.py:303
  91.5 17.9 %collective-permute-start.20 = (bf16[168,640]{1,0:T(8,128)(2,1)S(1)}, bf16[168,640]{1,0:T(8,128)(2,1)S(1)}, u32[]{:S(2)}, u32[]{:S(2)}) collective-permute-start(bf16[168,640]{1,0:T(8,128)(2,1)S(1)} %get-tuple-element.32), channel_id=1, source_target_pairs={{0,2},{1,3},{2,0},{3,1},{4,6},{5,7},{6,4},{7,5},{8,10},{9,11},{10,... | collective-permute-start | bytes 645128 | tf_op jit(solution)/shard_map/ppermute | solution.py:303
  94.5 19.4 %collective-permute-start.21 = (bf16[168,640]{1,0:T(8,128)(2,1)S(1)}, bf16[168,640]{1,0:T(8,128)(2,1)S(1)}, u32[]{:S(2)}, u32[]{:S(2)}) collective-permute-start(bf16[168,640]{1,0:T(8,128)(2,1)S(1)} %get-tuple-element.33), channel_id=1, source_target_pairs={{0,3},{1,2},{2,1},{3,0},{4,7},{5,6},{6,5},{7,4},{8,11},{9,10},{10,... | collective-permute-start | bytes 645128 | tf_op jit(solution)/shard_map/ppermute | solution.py:303

commit v3 on v2

--- a/solution.py
+++ b/solution.py
@@ -70,6 +70,11 @@
     return jnp.sum(jnp.where(lane == base + row, len_row, 0), axis=1, keepdims=True)
 
 
+def step_rows_of(rows, step):
+    at = lax.broadcasted_iota(jnp.int32, rows.shape, 1)
+    return jnp.sum(jnp.where(at == step, rows.astype(F32), 0.0), axis=1)
+
+
 def scale_lanes(scale_ref):
     return jnp.concatenate([scale_ref[h : h + 1, :] for h in range(scale_ref.shape[0])], axis=1)
 
@@ -77,7 +82,7 @@
 def qkv_kernel(at_ref, x_ref, xl_ref, gain_ref, scale_ref, qw_ref, kw_ref, vw_ref, q_ref, kn_ref, vn_ref, ql_ref, knl_ref, vnl_ref, w_ref, rows_ref, sem):
     heads, head_dim = scale_ref.shape
     width = heads * head_dim
-    short, count = x_ref.shape[1], xl_ref.shape[1]
+    short, count = x_ref.shape[1], xl_ref.shape[0]
 
     @pl.when(pl.program_id(0) == 0)
     def _():
@@ -89,7 +94,7 @@
             copy.wait()
 
     rows_ref[:short, :] = x_ref[0].astype(F32)
-    rows_ref[short : short + count, :] = xl_ref[0].astype(F32)
+    rows_ref[short : short + count, :] = step_rows_of(xl_ref[...], pl.program_id(0))
     normed = rms_scale(rows_ref[...], gain_ref[...][None])
     product = dot_t(normed, w_ref[...])
     queries = (product[:, :width] * scale_lanes(scale_ref) * head_dim**-0.5).astype(BF16)
@@ -130,7 +135,7 @@
     put_sums(part_ref, row_max, weight_sum, width, heads)
 
 
-def pair_kernel(heads, width, at_ref, mine_ref, other_ref, out_ref):
+def pair_kernel(heads, width, at_ref, mine_ref, other_ref, after_ref, out_ref):
     even = at_ref[0] % 2 == 0
     mine, other = mine_ref[...], other_ref[...]
     parts = (jnp.where(even, mine, other), jnp.where(even, other, mine))
@@ -259,9 +264,9 @@
     for copy in copies:
         copy.start()
     half = x_ref.shape[1] // 2
-    count = xl_ref.shape[1]
+    count = xl_ref.shape[0]
     xs_ref[...] = jnp.zeros_like(xs_ref)
-    xs_ref[:count, :] = xl_ref[0].astype(F32)
+    xs_ref[:count, :] = step_rows_of(xl_ref[...], at_ref[1])
     x = jnp.concatenate([x_ref[0].astype(F32), xs_ref[...]], axis=0)
 
     def rows_of(piece):
@@ -289,13 +294,17 @@
 def place_kernel(tp, at_ref, *refs):
     pieces, (short_ref, long_ref) = refs[:tp], refs[tp:]
     half, width = short_ref.shape[1] // 2, short_ref.shape[2]
-    count = long_ref.shape[1]
+    count = long_ref.shape[0]
+    longs = jnp.zeros(long_ref.shape, F32)
+    at = lax.broadcasted_iota(jnp.int32, longs.shape, 1)
     for k in range(tp):
         step = at_ref[1] ^ k
         short_ref[step, :half, :] = pieces[k][:half, :width]
         short_ref[step, half:, :] = pieces[k][:half, width:]
         tail = pieces[k][half:, :].astype(F32)
-        long_ref[step] = jnp.concatenate([tail[:, :width], tail[:, width:]], axis=0)[:count].astype(BF16)
+        tail = jnp.concatenate([tail[:, :width], tail[:, width:]], axis=0)[:count]
+        longs = jnp.where(at == step, tail[:, None, :], longs)
+    long_ref[...] = longs.astype(BF16)
 
 
 def swap(value, axis, k):
@@ -354,6 +363,7 @@
     shape = jax.ShapeDtypeStruct
     in_hbm = pl.BlockSpec(memory_space=pltpu.HBM)
     short_len, long_len = short_lengths, long_lengths
+    long_rows_in = jnp.swapaxes(long_inputs, 0, 1)
 
     rows, lanes = width // 4, model // 2
     shares = (o_weight, up_weight.T, down_weight)
@@ -375,11 +385,10 @@
     q, kn, vn, q_long, kn_long, vn_long = call(
         qkv_kernel,
         at,
-        (short_inputs, long_inputs, attn_gain, query_scale, q_weight.T, k_weight.T, v_weight.T),
+        (short_inputs, long_rows_in, attn_gain, query_scale, q_weight.T, k_weight.T, v_weight.T),
         (shape((steps, count, width), BF16),) * 3 + (shape((steps, GROUP, width), BF16),) * 3,
         specs={
             0: pl.BlockSpec((1, count, model), lambda i, at: (i, 0, 0)),
-            1: pl.BlockSpec((1, long_count, model), lambda i, at: (i, 0, 0)),
             4: in_hbm,
             5: in_hbm,
             6: in_hbm,
@@ -393,7 +402,7 @@
 
     part_shape = shape((n, width + 64), F32)
     (part,) = call(functools.partial(long_kernel, heads), at, (q_long, long_keys, long_values, long_len), (part_shape,), name="long_partial")
-    (part,) = call(functools.partial(pair_kernel, heads, width), at, (part, swap(part, "seq", 1)), (part_shape,), name="long_pair")
+    (part,) = call(functools.partial(pair_kernel, heads, width), at, (part, swap(part, "seq", 1), units[0]), (part_shape,), specs={2: in_hbm}, name="long_pair")
     parts = [part] + [swap(part, "seq", 2 * i) for i in range(1, seq // 2)]
 
     block = count // 2
@@ -408,7 +417,7 @@
         specs={0: fresh_rows, 1: fresh_rows, 2: fresh_rows, 3: cache_rows, 4: cache_rows, 6: in_hbm},
         out_specs={0: fresh_rows},
         grid=(count // block,),
-        limit=60,
+        limit=50,
         name="short_attention",
     )
     att_sent = call(
@@ -446,11 +455,10 @@
     outs = call(
         functools.partial(mlp_kernel, tp),
         at,
-        (short_inputs, long_inputs, mlp_gain, *received, *shares, *pieces),
+        (short_inputs, long_rows_in, mlp_gain, *received, *shares, *pieces),
         (packed,) * tp,
         specs={
             0: pl.BlockSpec((1, count, model), lambda _, at: (at[1], 0, 0)),
-            1: pl.BlockSpec((1, long_count, model), lambda _, at: (at[1], 0, 0)),
             **{3 + tp + i: in_hbm for i in range(3 + len(pieces))},
         },
         scratch=(
@@ -464,15 +472,14 @@
         name="feed_forward",
     )
     outs = [outs[0]] + [swap(outs[k], "tp", k) for k in range(1, tp)]
-    return tuple(
-        call(
-            functools.partial(place_kernel, tp),
-            at,
-            outs,
-            (shape((steps, count, width), BF16), shape((steps, long_count, width), BF16)),
-            name="place_outputs",
-        )
-    )
+    short_out, long_out = call(
+        functools.partial(place_kernel, tp),
+        at,
+        outs,
+        (shape((steps, count, width), BF16), shape((long_count, steps, width), BF16)),
+        name="place_outputs",
+    )
+    return short_out, jnp.swapaxes(long_out, 0, 1)
 
 
 def solution(mesh):

time: 117 us -> 111 us (0.949)
  waiting for transfers between devices: 53.7 us -> 50.8 us
  local copies, waits for them, and re-layouts: 6.53 us -> 4.46 us
    ppermute x22, waiting for transfers between devices: 53.7 us -> 50.8 us  [swap(): return lax.ppermute(value, axis, [(i, i ^ k) for i in range(size)])]
    unnamed x39 -> x36, local copies, waits for them, and re-layouts: 5.9 us -> 4.46 us
  transfers between devices with their start and end apart: 22 -> 22, of which waited for: 11 -> 10; matrix products, arithmetic and copies ran while one was open for 1% -> 0% of each run, Pallas kernels for 19% -> 20%
where the time goes in v3:
time: 111 us; the launch traced here: 110 us
  waiting for transfers between devices  50.8 us (46%)
  Pallas kernels  33.5 us (30%)
  starting transfers between devices  19.8 us (18%)
  local copies, waits for them, and re-layouts  4.46 us (4%)
    ppermute x22, waiting for transfers between devices, swap(): return lax.ppermute(value, axis, [(i, i ^ k) for i in range(size)])  50.8 us
    pallas_call x10, Pallas kernels, call(): pl.pallas_call(kernel, grid_spec=pltpu.PrefetchScalarGridSpec(num_scalar_...  33.5 us
    ppermute x22, starting transfers between devices, swap(): return lax.ppermute(value, axis, [(i, i ^ k) for i in range(size)])  19.8 us
    unnamed x36, local copies, waits for them, and re-layouts  4.46 us
  transfers between devices with their start and end apart: 22, of which 10 were waited for; matrix products, arithmetic and copies ran while one was open for 0% of the time, Pallas kernels for 20%

profile of v3, /device:TPU:8, one launch (start us, length us, event | category | flops | bytes accessed | tf_op | source)
XLA Modules:
  0.0 110.1 jit_solution(13988324917160211993)
XLA Ops:
  0.6 0.6 pad_add_fusion.at_ref
  1.2 2.5 %pack_weights.1 = bf16[3,80,640]{2,1,0:T(8,128)(2,1)} custom-call(s32[2]{0:T(128)} %pad_add_fusion.at_ref, bf16[320,1280]{1,0:T(8,128)(2,1)} %refs_4_.1, bf16[320,1280]{1,0:T(8,128)(2,1)} %bitcast.8, bf16[320,1280]{1,0:T(8,128)(2,1)} %refs_6_.1), custom_call_target="tpu_custom_call" | custom-call | bytes 1024 | tf_op jit(solution)/shard_map/pack_weights/pallas_call | solution.py:321
  3.8 3.1 %collective-permute-start.9 = (bf16[3,80,640]{2,1,0:T(8,128)(2,1)}, bf16[3,80,640]{2,1,0:T(8,128)(2,1)S(1)}, u32[]{:S(2)}, u32[]{:S(2)}) collective-permute-start(bf16[3,80,640]{2,1,0:T(8,128)(2,1)} %pack_weights.1), channel_id=1, source_target_pairs={{0,3},{1,2},{2,1},{3,0},{4,7},{5,6},{6,5},{7,4},{8,11},{9,10},{10,... | collective-permute-start | bytes 921608 | tf_op jit(solution)/shard_map/ppermute | solution.py:312
  6.9 1.2 %collective-permute-start.8 = (bf16[3,80,640]{2,1,0:T(8,128)(2,1)}, bf16[3,80,640]{2,1,0:T(8,128)(2,1)S(1)}, u32[]{:S(2)}, u32[]{:S(2)}) collective-permute-start(bf16[3,80,640]{2,1,0:T(8,128)(2,1)} %pack_weights.1), channel_id=1, source_target_pairs={{0,2},{1,3},{2,0},{3,1},{4,6},{5,7},{6,4},{7,5},{8,10},{9,11},{10,... | collective-permute-start | bytes 921608 | tf_op jit(solution)/shard_map/ppermute | solution.py:312
  8.2 10.3 %qkv.1 = (bf16[4,320,320]{2,1,0:T(8,128)(2,1)}, bf16[4,320,320]{2,1,0:T(8,128)(2,1)}, bf16[4,320,320]{2,1,0:T(8,128)(2,1)}, bf16[4,16,320]{2,1,0:T(8,128)(2,1)},...) custom-call(s32[2]{0:T(128)} %pad_add_fusion.at_ref, bf16[4,320,1280]{2,1,0:T(8,128)(2,1)} %x_ref.3, ...), custom_call_target="tpu_custom_call" | custom-call | bytes 1024 | tf_op jit(solution)/shard_map/qkv/pallas_call | solution.py:321
  18.5 0.8 copy-done.8
  19.3 1.1 %long_partial.1.mine_ref = f32[64,384]{1,0:T(8,128)S(1)} custom-call(s32[2]{0:T(128)S(1)} %copy-done.12, bf16[4,16,320]{2,1,0:T(8,128)(2,1)S(1)} %copy-done.8, bf16[12,16,320]{2,1,0:T(8,128)(2,1)S(1)} %copy-done.10, bf16[12,16,320]{2,1,0:T(8,128)(2,1)S(1)} %copy-done.11, s32[12]{0:T(128)S(1)} %copy-done.17), custom_call_target="tpu_custom_call" | custom-call | bytes 1024 | tf_op jit(solution)/shard_map/long_partial/pallas_call | solution.py:321
  20.5 0.1 collective-permute-start
  20.5 1.3 %collective-permute-done.other_ref = f32[64,384]{1,0:T(8,128)S(1)} collective-permute-done((f32[64,384]{1,0:T(8,128)S(1)}, f32[64,384]{1,0:T(8,128)S(1)}, u32[]{:S(2)}, u32[]{:S(2)}) %collective-permute-start) | collective-permute-done | bytes 98336 | tf_op jit(solution)/shard_map/ppermute | solution.py:312
  21.8 1.0 long_pair.1.refs_0_
  22.8 2.5 %collective-permute-start.4 = (f32[64,384]{1,0:T(8,128)S(1)}, f32[64,384]{1,0:T(8,128)S(1)}, u32[]{:S(2)}, u32[]{:S(2)}) collective-permute-start(f32[64,384]{1,0:T(8,128)S(1)} %long_pair.1.refs_0_), channel_id=1, source_target_pairs={{0,24},{4,28},{8,16},{12,20},{16,8},{20,12},{24,0},{28,4},{1,25},{... | collective-permute-start | bytes 294920 | tf_op jit(solution)/shard_map/ppermute | solution.py:312
  25.2 0.5 collective-permute-start.3
  25.7 0.5 collective-permute-start.2
  26.3 1.2 %copy-done.4 = bf16[4,320,320]{2,1,0:T(8,128)(2,1)S(1)} copy-done((bf16[4,320,320]{2,1,0:T(8,128)(2,1)S(1)}, bf16[4,320,320]{2,1,0:T(8,128)(2,1)}, u32[]{:S(2)}) %copy-start.4) | copy-done | bytes 819224
  27.5 1.2 %copy-done.5 = bf16[4,320,320]{2,1,0:T(8,128)(2,1)S(1)} copy-done((bf16[4,320,320]{2,1,0:T(8,128)(2,1)S(1)}, bf16[4,320,320]{2,1,0:T(8,128)(2,1)}, u32[]{:S(2)}) %copy-start.5) | copy-done | bytes 819224
  28.7 1.2 %copy-done.6 = bf16[4,320,320]{2,1,0:T(8,128)(2,1)S(1)} copy-done((bf16[4,320,320]{2,1,0:T(8,128)(2,1)S(1)}, bf16[4,320,320]{2,1,0:T(8,128)(2,1)}, u32[]{:S(2)}) %copy-start.6) | copy-done | bytes 819224
  29.9 7.0 %short_attention.1.att_ref.refs_3_ = bf16[4,320,320]{2,1,0:T(8,128)(2,1)S(1)} custom-call(s32[2]{0:T(128)S(1)} %copy-done.12, bf16[4,320,320]{2,1,0:T(8,128)(2,1)S(1)} %copy-done.4, bf16[4,320,320]{2,1,0:T(8,128)(2,1)S(1)} %copy-done.5, bf16[4,320,320]{2,1,0:T(8,128)(2,1)S(1)} %copy-done.6, bf16[320,16,320]{2,1,0:T(8,128)(2,1)} %k_ref.3, ...), custom_call_target="tpu_custom_call" | custom-call | bytes 1024 | tf_op jit(solution)/shard_map/short_attention/pallas_call | solution.py:321
  36.9 0.0 copy-start
  36.9 0.0 copy-start.1
  36.9 0.0 copy-start.2
  36.9 0.0 copy-start.3
  37.0 0.0 copy-start.7
  37.0 0.0 copy-start.15
  37.0 0.6 stack_weights.1.refs_7_
  37.7 1.6 %collective-permute-start.13 = (bf16[9,80,640]{2,1,0:T(8,128)(2,1)S(1)}, bf16[9,80,640]{2,1,0:T(8,128)(2,1)S(1)}, u32[]{:S(2)}, u32[]{:S(2)}) collective-permute-start(bf16[9,80,640]{2,1,0:T(8,128)(2,1)S(1)} %stack_weights.1.refs_7_), channel_id=1, source_target_pairs={{0,16},{4,20},{8,24},{12,28},{16,0},{20,4},{24,8},{28,12},{1,17},{... | collective-permute-start | bytes 2764808 | tf_op jit(solution)/shard_map/ppermute | solution.py:312
  39.2 1.5 %collective-permute-start.11 = (bf16[9,80,640]{2,1,0:T(8,128)(2,1)S(1)}, bf16[9,80,640]{2,1,0:T(8,128)(2,1)S(1)}, u32[]{:S(2)}, u32[]{:S(2)}) collective-permute-start(bf16[9,80,640]{2,1,0:T(8,128)(2,1)S(1)} %stack_weights.1.refs_7_), channel_id=1, source_target_pairs={{0,8},{4,12},{8,0},{12,4},{16,24},{20,28},{24,16},{28,20},{1,9},{5... | collective-permute-start | bytes 2764808 | tf_op jit(solution)/shard_map/ppermute | solution.py:312
  40.7 2.1 %send_attended.1 = (bf16[168,640]{1,0:T(8,128)(2,1)S(1)}, bf16[168,640]{1,0:T(8,128)(2,1)S(1)}, bf16[168,640]{1,0:T(8,128)(2,1)S(1)}, bf16[168,640]{1,0:T(8,128)(2,1)S(1)}) custom-call(s32[2]{0:T(128)S(1)} %copy-done.12, bf16[4,320,320]{2,1,0:T(8,128)(2,1)S(1)} %short_attention.1.att_ref.refs_3_, bf16[4,16,320]{2,1,0:T(8,128)(2,1)S(1)} %copy-done.9, ...), custom_call_target="tpu_custom_call" | custom-call | bytes 1024 | tf_op jit(solution)/shard_map/send_attended/pallas_call | solution.py:321
  42.9 0.3 collective-permute-start.5
  43.2 2.8 %collective-permute-start.6 = (bf16[168,640]{1,0:T(8,128)(2,1)S(1)}, bf16[168,640]{1,0:T(8,128)(2,1)S(1)}, u32[]{:S(2)}, u32[]{:S(2)}) collective-permute-start(bf16[168,640]{1,0:T(8,128)(2,1)S(1)} %get-tuple-element.28), channel_id=1, source_target_pairs={{0,2},{1,3},{2,0},{3,1},{4,6},{5,7},{6,4},{7,5},{8,10},{9,11},{10,... | collective-permute-start | bytes 645128 | tf_op jit(solution)/shard_map/ppermute | solution.py:312
  46.0 0.5 collective-permute-start.7
  46.4 4.7 %collective-permute-done.5.refs_0_.refs_1_ = bf16[168,640]{1,0:T(8,128)(2,1)S(1)} collective-permute-done((bf16[168,640]{1,0:T(8,128)(2,1)S(1)}, bf16[168,640]{1,0:T(8,128)(2,1)S(1)}, u32[]{:S(2)}, u32[]{:S(2)}) %collective-permute-start.5) | collective-permute-done | bytes 215072 | tf_op jit(solution)/shard_map/ppermute | solution.py:312
  51.2 9.0 %collective-permute-done.6.refs_1_.refs_2_ = bf16[168,640]{1,0:T(8,128)(2,1)S(1)} collective-permute-done((bf16[168,640]{1,0:T(8,128)(2,1)S(1)}, bf16[168,640]{1,0:T(8,128)(2,1)S(1)}, u32[]{:S(2)}, u32[]{:S(2)}) %collective-permute-start.6) | collective-permute-done | bytes 215072 | tf_op jit(solution)/shard_map/ppermute | solution.py:312
  60.2 3.7 %collective-permute-done.7.refs_2_.refs_3_ = bf16[168,640]{1,0:T(8,128)(2,1)S(1)} collective-permute-done((bf16[168,640]{1,0:T(8,128)(2,1)S(1)}, bf16[168,640]{1,0:T(8,128)(2,1)S(1)}, u32[]{:S(2)}, u32[]{:S(2)}) %collective-permute-start.7) | collective-permute-done | bytes 215072 | tf_op jit(solution)/shard_map/ppermute | solution.py:312
  63.9 0.6 cut_weights.1
  64.6 0.6 collective-permute-start.15
  65.2 0.5 collective-permute-start.14
  65.7 0.5 collective-permute-start.17
  66.2 9.5 %collective-permute-done.15.refs_13_ = bf16[5,80,640]{2,1,0:T(8,128)(2,1)S(1)} collective-permute-done((bf16[5,80,640]{2,1,0:T(8,128)(2,1)S(1)}, bf16[5,80,640]{2,1,0:T(8,128)(2,1)S(1)}, u32[]{:S(2)}, u32[]{:S(2)}) %collective-permute-start.15) | collective-permute-done | bytes 512032 | tf_op jit(solution)/shard_map/ppermute | solution.py:312
  75.7 1.9 %collective-permute-done.17.refs_15_ = bf16[4,80,640]{2,1,0:T(8,128)(2,1)S(1)} collective-permute-done((bf16[4,80,640]{2,1,0:T(8,128)(2,1)S(1)}, bf16[4,80,640]{2,1,0:T(8,128)(2,1)S(1)}, u32[]{:S(2)}, u32[]{:S(2)}) %collective-permute-start.17) | collective-permute-done | bytes 409632 | tf_op jit(solution)/shard_map/ppermute | solution.py:312
  77.6 1.7 %collective-permute-done.18.refs_16_ = bf16[4,80,640]{2,1,0:T(8,128)(2,1)S(1)} collective-permute-done((bf16[4,80,640]{2,1,0:T(8,128)(2,1)S(1)}, bf16[4,80,640]{2,1,0:T(8,128)(2,1)S(1)}, u32[]{:S(2)}, u32[]{:S(2)}) %collective-permute-start.18) | collective-permute-done | bytes 409632 | tf_op jit(solution)/shard_map/ppermute | solution.py:312
  79.4 6.5 %feed_forward.1 = (bf16[168,640]{1,0:T(8,128)(2,1)S(1)}, bf16[168,640]{1,0:T(8,128)(2,1)S(1)}, bf16[168,640]{1,0:T(8,128)(2,1)S(1)}, bf16[168,640]{1,0:T(8,128)(2,1)S(1)}) custom-call(s32[2]{0:T(128)S(1)} %copy-done.12, bf16[4,320,1280]{2,1,0:T(8,128)(2,1)S(1)} %copy-done, bf16[12,4,1280]{2,1,0:T(4,128)(2,1)S(1)} %bitcast.11, f32[1280]{0:T(1024)S(1)} %copy-done.15, ...), custom_call_target="tpu_custom_call" | custom-call | flops 3303014400 | bytes 1024 | tf_op jit(solution)/shard_map/feed_forward/pallas_call | solution.py:321
  85.9 0.1 collective-permute-start.19
  86.0 3.0 %collective-permute-start.20 = (bf16[168,640]{1,0:T(8,128)(2,1)S(1)}, bf16[168,640]{1,0:T(8,128)(2,1)S(1)}, u32[]{:S(2)}, u32[]{:S(2)}) collective-permute-start(bf16[168,640]{1,0:T(8,128)(2,1)S(1)} %get-tuple-element.34), channel_id=1, source_target_pairs={{0,2},{1,3},{2,0},{3,1},{4,6},{5,7},{6,4},{7,5},{8,10},{9,11},{10,... | collective-permute-start | bytes 645128 | tf_op jit(solution)/shard_map/ppermute | solution.py:312
  89.0 0.4 collective-permute-start.21
  89.5 5.7 %collective-permute-done.19.refs_1_ = bf16[168,640]{1,0:T(8,128)(2,1)S(1)} collective-permute-done((bf16[168,640]{1,0:T(8,128)(2,1)S(1)}, bf16[168,640]{1,0:T(8,128)(2,1)S(1)}, u32[]{:S(2)}, u32[]{:S(2)}) %collective-permute-start.19) | collective-permute-done | bytes 215072 | tf_op jit(solution)/shard_map/ppermute | solution.py:312
  95.1 8.8 %collective-permute-done.20.refs_2_ = bf16[168,640]{1,0:T(8,128)(2,1)S(1)} collective-permute-done((bf16[168,640]{1,0:T(8,128)(2,1)S(1)}, bf16[168,640]{1,0:T(8,128)(2,1)S(1)}, u32[]{:S(2)}, u32[]{:S(2)}) %collective-permute-start.20) | collective-permute-done | bytes 215072 | tf_op jit(solution)/shard_map/ppermute | solution.py:312
  103.9 4.4 %collective-permute-done.21.refs_3_ = bf16[168,640]{1,0:T(8,128)(2,1)S(1)} collective-permute-done((bf16[168,640]{1,0:T(8,128)(2,1)S(1)}, bf16[168,640]{1,0:T(8,128)(2,1)S(1)}, u32[]{:S(2)}, u32[]{:S(2)}) %collective-permute-start.21) | collective-permute-done | bytes 215072 | tf_op jit(solution)/shard_map/ppermute | solution.py:312
  108.4 1.7 %place_outputs.1 = (bf16[4,320,320]{2,1,0:T(8,128)(2,1)}, bf16[12,4,320]{2,1,0:T(4,128)(2,1)}) custom-call(s32[2]{0:T(128)S(1)} %copy-done.12, bf16[168,640]{1,0:T(8,128)(2,1)S(1)} %get-tuple-element.32.refs_0_, bf16[168,640]{1,0:T(8,128)(2,1)S(1)} %collective-permute-done.19.refs_1_, bf16[168,640]{1,0:T(8,128)(2,1)S(1)} %collective-permute-done.20.refs_2_, ...), custom_call_target="tpu_custom_call" | custom-call | bytes 1024 | tf_op jit(solution)/shard_map/place_outputs/pallas_call | solution.py:321
  (43 shorter events, 0.1 us)
Async XLA Ops:
  1.2 17.3 %copy-start.10 = (bf16[12,16,320]{2,1,0:T(8,128)(2,1)S(1)}, bf16[12,16,320]{2,1,0:T(8,128)(2,1)}, u32[]{:S(2)}) copy-start(bf16[12,16,320]{2,1,0:T(8,128)(2,1)} %k_ref.2) | copy-start | bytes 368644
  1.2 17.3 %copy-start.11 = (bf16[12,16,320]{2,1,0:T(8,128)(2,1)S(1)}, bf16[12,16,320]{2,1,0:T(8,128)(2,1)}, u32[]{:S(2)}) copy-start(bf16[12,16,320]{2,1,0:T(8,128)(2,1)} %v_ref.2) | copy-start | bytes 368644
  1.2 17.3 %copy-start.12 = (s32[2]{0:T(128)S(1)}, s32[2]{0:T(128)}, u32[]{:S(2)}) copy-start(s32[2]{0:T(128)} %pad_add_fusion.at_ref) | copy-start | bytes 28
  1.2 17.3 %copy-start.17 = (s32[12]{0:T(128)S(1)}, s32[12]{0:T(128)}, u32[]{:S(2)}) copy-start(s32[12]{0:T(128)} %len_ref.2) | copy-start | bytes 148
  3.8 22.5 %copy-start.16 = (s32[320]{0:T(512)S(1)}, s32[320]{0:T(512)}, u32[]{:S(2)}) copy-start(s32[320]{0:T(512)} %len_ref.3) | copy-start | bytes 3844
  3.8 18.0 %collective-permute-start.1 = (bf16[3,80,640]{2,1,0:T(8,128)(2,1)}, bf16[3,80,640]{2,1,0:T(8,128)(2,1)S(1)}, u32[]{:S(2)}, u32[]{:S(2)}) collective-permute-start(bf16[3,80,640]{2,1,0:T(8,128)(2,1)} %pack_weights.1), channel_id=1, source_target_pairs={{0,1},{1,0},{2,3},{3,2},{4,5},{5,4},{6,7},{7,6},{8,9},{9,8},{10,11... | collective-permute-start | bytes 921608 | tf_op jit(solution)/shard_map/ppermute | solution.py:312
  3.8 33.2 %collective-permute-start.9 = (bf16[3,80,640]{2,1,0:T(8,128)(2,1)}, bf16[3,80,640]{2,1,0:T(8,128)(2,1)S(1)}, u32[]{:S(2)}, u32[]{:S(2)}) collective-permute-start(bf16[3,80,640]{2,1,0:T(8,128)(2,1)} %pack_weights.1), channel_id=1, source_target_pairs={{0,3},{1,2},{2,1},{3,0},{4,7},{5,6},{6,5},{7,4},{8,11},{9,10},{10,... | collective-permute-start | bytes 921608 | tf_op jit(solution)/shard_map/ppermute | solution.py:312
  6.9 30.1 %collective-permute-start.8 = (bf16[3,80,640]{2,1,0:T(8,128)(2,1)}, bf16[3,80,640]{2,1,0:T(8,128)(2,1)S(1)}, u32[]{:S(2)}, u32[]{:S(2)}) collective-permute-start(bf16[3,80,640]{2,1,0:T(8,128)(2,1)} %pack_weights.1), channel_id=1, source_target_pairs={{0,2},{1,3},{2,0},{3,1},{4,6},{5,7},{6,4},{7,5},{8,10},{9,11},{10,... | collective-permute-start | bytes 921608 | tf_op jit(solution)/shard_map/ppermute | solution.py:312
  18.5 0.8 copy-start.8
  20.5 1.4 %collective-permute-start = (f32[64,384]{1,0:T(8,128)S(1)}, f32[64,384]{1,0:T(8,128)S(1)}, u32[]{:S(2)}, u32[]{:S(2)}) collective-permute-start(f32[64,384]{1,0:T(8,128)S(1)} %long_partial.1.mine_ref), channel_id=1, source_target_pairs={{0,4},{4,0},{8,12},{12,8},{16,20},{20,16},{24,28},{28,24},{1,5},{5... | collective-permute-start | bytes 294920 | tf_op jit(solution)/shard_map/ppermute | solution.py:312
  22.8 14.2 %collective-permute-start.4 = (f32[64,384]{1,0:T(8,128)S(1)}, f32[64,384]{1,0:T(8,128)S(1)}, u32[]{:S(2)}, u32[]{:S(2)}) collective-permute-start(f32[64,384]{1,0:T(8,128)S(1)} %long_pair.1.refs_0_), channel_id=1, source_target_pairs={{0,24},{4,28},{8,16},{12,20},{16,8},{20,12},{24,0},{28,4},{1,25},{... | collective-permute-start | bytes 294920 | tf_op jit(solution)/shard_map/ppermute | solution.py:312
  25.2 11.8 %collective-permute-start.3 = (f32[64,384]{1,0:T(8,128)S(1)}, f32[64,384]{1,0:T(8,128)S(1)}, u32[]{:S(2)}, u32[]{:S(2)}) collective-permute-start(f32[64,384]{1,0:T(8,128)S(1)} %long_pair.1.refs_0_), channel_id=1, source_target_pairs={{0,16},{4,20},{8,24},{12,28},{16,0},{20,4},{24,8},{28,12},{1,17},{... | collective-permute-start | bytes 294920 | tf_op jit(solution)/shard_map/ppermute | solution.py:312
  25.7 11.3 %collective-permute-start.2 = (f32[64,384]{1,0:T(8,128)S(1)}, f32[64,384]{1,0:T(8,128)S(1)}, u32[]{:S(2)}, u32[]{:S(2)}) collective-permute-start(f32[64,384]{1,0:T(8,128)S(1)} %long_pair.1.refs_0_), channel_id=1, source_target_pairs={{0,8},{4,12},{8,0},{12,4},{16,24},{20,28},{24,16},{28,20},{1,9},{5... | collective-permute-start | bytes 294920 | tf_op jit(solution)/shard_map/ppermute | solution.py:312
  26.3 1.2 %copy-start.4 = (bf16[4,320,320]{2,1,0:T(8,128)(2,1)S(1)}, bf16[4,320,320]{2,1,0:T(8,128)(2,1)}, u32[]{:S(2)}) copy-start(bf16[4,320,320]{2,1,0:T(8,128)(2,1)} %get-tuple-element.20.q_ref) | copy-start | bytes 2457604
  27.5 1.2 %copy-start.5 = (bf16[4,320,320]{2,1,0:T(8,128)(2,1)S(1)}, bf16[4,320,320]{2,1,0:T(8,128)(2,1)}, u32[]{:S(2)}) copy-start(bf16[4,320,320]{2,1,0:T(8,128)(2,1)} %get-tuple-element.21.kn_ref) | copy-start | bytes 2457604
  28.7 1.2 %copy-start.6 = (bf16[4,320,320]{2,1,0:T(8,128)(2,1)S(1)}, bf16[4,320,320]{2,1,0:T(8,128)(2,1)}, u32[]{:S(2)}) copy-start(bf16[4,320,320]{2,1,0:T(8,128)(2,1)} %get-tuple-element.22.vn_ref) | copy-start | bytes 2457604
  29.9 10.8 %copy-start.9 = (bf16[4,16,320]{2,1,0:T(8,128)(2,1)S(1)}, bf16[4,16,320]{2,1,0:T(8,128)(2,1)}, u32[]{:S(2)}) copy-start(bf16[4,16,320]{2,1,0:T(8,128)(2,1)} %get-tuple-element.23.q_ref.ql_ref) | copy-start | bytes 122884
  29.9 10.8 %copy-start.13 = (bf16[4,16,320]{2,1,0:T(8,128)(2,1)S(1)}, bf16[4,16,320]{2,1,0:T(8,128)(2,1)}, u32[]{:S(2)}) copy-start(bf16[4,16,320]{2,1,0:T(8,128)(2,1)} %get-tuple-element.24.knl_ref) | copy-start | bytes 122884
  29.9 10.8 %copy-start.14 = (bf16[4,16,320]{2,1,0:T(8,128)(2,1)S(1)}, bf16[4,16,320]{2,1,0:T(8,128)(2,1)}, u32[]{:S(2)}) copy-start(bf16[4,16,320]{2,1,0:T(8,128)(2,1)} %get-tuple-element.25.vnl_ref) | copy-start | bytes 122884
  36.9 42.4 %copy-start = (bf16[4,320,1280]{2,1,0:T(8,128)(2,1)S(1)}, bf16[4,320,1280]{2,1,0:T(8,128)(2,1)}, u32[]{:S(2)}) copy-start(bf16[4,320,1280]{2,1,0:T(8,128)(2,1)} %x_ref.3) | copy-start | bytes 9830404
  36.9 42.4 %copy-start.1 = (bf16[320,1280]{1,0:T(8,128)(2,1)S(1)}, bf16[320,1280]{1,0:T(8,128)(2,1)}, u32[]{:S(2)}) copy-start(bf16[320,1280]{1,0:T(8,128)(2,1)} %refs_4_.1) | copy-start | bytes 2457604
  36.9 42.4 %copy-start.2 = (bf16[1280,320]{0,1:T(8,128)(2,1)S(1)}, bf16[1280,320]{0,1:T(8,128)(2,1)}, u32[]{:S(2)}) copy-start(bf16[1280,320]{0,1:T(8,128)(2,1)} %param.32) | copy-start | bytes 2457604
  36.9 42.4 %copy-start.3 = (bf16[320,1280]{1,0:T(8,128)(2,1)S(1)}, bf16[320,1280]{1,0:T(8,128)(2,1)}, u32[]{:S(2)}) copy-start(bf16[320,1280]{1,0:T(8,128)(2,1)} %refs_6_.1) | copy-start | bytes 2457604
  37.0 42.4 %copy-start.7 = (bf16[4,12,1280]{2,0,1:T(4,128)(2,1)S(1)}, bf16[4,12,1280]{2,0,1:T(4,128)(2,1)}, u32[]{:S(2)}) copy-start(bf16[4,12,1280]{2,0,1:T(4,128)(2,1)} %param.18) | copy-start | bytes 368644
  37.0 42.4 %copy-start.15 = (f32[1280]{0:T(1024)S(1)}, f32[1280]{0:T(1024)}, u32[]{:S(2)}) copy-start(f32[1280]{0:T(1024)} %gain_ref.3) | copy-start | bytes 15364
  37.7 26.3 %collective-permute-start.13 = (bf16[9,80,640]{2,1,0:T(8,128)(2,1)S(1)}, bf16[9,80,640]{2,1,0:T(8,128)(2,1)S(1)}, u32[]{:S(2)}, u32[]{:S(2)}) collective-permute-start(bf16[9,80,640]{2,1,0:T(8,128)(2,1)S(1)} %stack_weights.1.refs_7_), channel_id=1, source_target_pairs={{0,16},{4,20},{8,24},{12,28},{16,0},{20,4},{24,8},{28,12},{1,17},{... | collective-permute-start | bytes 2764808 | tf_op jit(solution)/shard_map/ppermute | solution.py:312
  39.2 24.7 %collective-permute-start.11 = (bf16[9,80,640]{2,1,0:T(8,128)(2,1)S(1)}, bf16[9,80,640]{2,1,0:T(8,128)(2,1)S(1)}, u32[]{:S(2)}, u32[]{:S(2)}) collective-permute-start(bf16[9,80,640]{2,1,0:T(8,128)(2,1)S(1)} %stack_weights.1.refs_7_), channel_id=1, source_target_pairs={{0,8},{4,12},{8,0},{12,4},{16,24},{20,28},{24,16},{28,20},{1,9},{5... | collective-permute-start | bytes 2764808 | tf_op jit(solution)/shard_map/ppermute | solution.py:312
  42.9 8.3 %collective-permute-start.5 = (bf16[168,640]{1,0:T(8,128)(2,1)S(1)}, bf16[168,640]{1,0:T(8,128)(2,1)S(1)}, u32[]{:S(2)}, u32[]{:S(2)}) collective-permute-start(bf16[168,640]{1,0:T(8,128)(2,1)S(1)} %get-tuple-element.27), channel_id=1, source_target_pairs={{0,1},{1,0},{2,3},{3,2},{4,5},{5,4},{6,7},{7,6},{8,9},{9,8},{10,11... | collective-permute-start | bytes 645128 | tf_op jit(solution)/shard_map/ppermute | solution.py:312
  43.2 17.0 %collective-permute-start.6 = (bf16[168,640]{1,0:T(8,128)(2,1)S(1)}, bf16[168,640]{1,0:T(8,128)(2,1)S(1)}, u32[]{:S(2)}, u32[]{:S(2)}) collective-permute-start(bf16[168,640]{1,0:T(8,128)(2,1)S(1)} %get-tuple-element.28), channel_id=1, source_target_pairs={{0,2},{1,3},{2,0},{3,1},{4,6},{5,7},{6,4},{7,5},{8,10},{9,11},{10,... | collective-permute-start | bytes 645128 | tf_op jit(solution)/shard_map/ppermute | solution.py:312
  46.0 18.0 %collective-permute-start.7 = (bf16[168,640]{1,0:T(8,128)(2,1)S(1)}, bf16[168,640]{1,0:T(8,128)(2,1)S(1)}, u32[]{:S(2)}, u32[]{:S(2)}) collective-permute-start(bf16[168,640]{1,0:T(8,128)(2,1)S(1)} %get-tuple-element.29), channel_id=1, source_target_pairs={{0,3},{1,2},{2,1},{3,0},{4,7},{5,6},{6,5},{7,4},{8,11},{9,10},{10,... | collective-permute-start | bytes 645128 | tf_op jit(solution)/shard_map/ppermute | solution.py:312
  64.6 11.1 %collective-permute-start.15 = (bf16[5,80,640]{2,1,0:T(8,128)(2,1)S(1)}, bf16[5,80,640]{2,1,0:T(8,128)(2,1)S(1)}, u32[]{:S(2)}, u32[]{:S(2)}) collective-permute-start(bf16[5,80,640]{2,1,0:T(8,128)(2,1)S(1)} %get-tuple-element.30), channel_id=1, source_target_pairs={{0,8},{4,12},{8,0},{12,4},{16,24},{20,28},{24,16},{28,20},{1,9},{5... | collective-permute-start | bytes 1536008 | tf_op jit(solution)/shard_map/ppermute | solution.py:312
  65.2 12.4 %collective-permute-start.10 = (bf16[9,80,640]{2,1,0:T(8,128)(2,1)S(1)}, bf16[9,80,640]{2,1,0:T(8,128)(2,1)S(1)}, u32[]{:S(2)}, u32[]{:S(2)}) collective-permute-start(bf16[9,80,640]{2,1,0:T(8,128)(2,1)S(1)} %stack_weights.1.refs_7_), channel_id=1, source_target_pairs={{0,4},{4,0},{8,12},{12,8},{16,20},{20,16},{24,28},{28,24},{1,5},{5... | collective-permute-start | bytes 2764808 | tf_op jit(solution)/shard_map/ppermute | solution.py:312
  65.2 14.1 %collective-permute-start.14 = (bf16[9,80,640]{2,1,0:T(8,128)(2,1)S(1)}, bf16[9,80,640]{2,1,0:T(8,128)(2,1)S(1)}, u32[]{:S(2)}, u32[]{:S(2)}) collective-permute-start(bf16[9,80,640]{2,1,0:T(8,128)(2,1)S(1)} %collective-permute-done.13.y_ref.refs_11_), channel_id=1, source_target_pairs={{0,4},{4,0},{8,12},{12,8},{16,20},{20,16},{24,28},{28,24},{1,5},{5... | collective-permute-start | bytes 2764808 | tf_op jit(solution)/shard_map/ppermute | solution.py:312
  65.7 13.6 %collective-permute-start.12 = (bf16[9,80,640]{2,1,0:T(8,128)(2,1)S(1)}, bf16[9,80,640]{2,1,0:T(8,128)(2,1)S(1)}, u32[]{:S(2)}, u32[]{:S(2)}) collective-permute-start(bf16[9,80,640]{2,1,0:T(8,128)(2,1)S(1)} %collective-permute-done.11.x_ref.refs_9_), channel_id=1, source_target_pairs={{0,4},{4,0},{8,12},{12,8},{16,20},{20,16},{24,28},{28,24},{1,5},{5... | collective-permute-start | bytes 2764808 | tf_op jit(solution)/shard_map/ppermute | solution.py:312
  65.7 11.9 %collective-permute-start.17 = (bf16[4,80,640]{2,1,0:T(8,128)(2,1)S(1)}, bf16[4,80,640]{2,1,0:T(8,128)(2,1)S(1)}, u32[]{:S(2)}, u32[]{:S(2)}) collective-permute-start(bf16[4,80,640]{2,1,0:T(8,128)(2,1)S(1)} %get-tuple-element.31), channel_id=1, source_target_pairs={{0,16},{4,20},{8,24},{12,28},{16,0},{20,4},{24,8},{28,12},{1,17},{... | collective-permute-start | bytes 1228808 | tf_op jit(solution)/shard_map/ppermute | solution.py:312
  75.7 3.7 %collective-permute-start.16 = (bf16[5,80,640]{2,1,0:T(8,128)(2,1)S(1)}, bf16[5,80,640]{2,1,0:T(8,128)(2,1)S(1)}, u32[]{:S(2)}, u32[]{:S(2)}) collective-permute-start(bf16[5,80,640]{2,1,0:T(8,128)(2,1)S(1)} %collective-permute-done.15.refs_13_), channel_id=1, source_target_pairs={{0,4},{4,0},{8,12},{12,8},{16,20},{20,16},{24,28},{28,24},{1,5},{5... | collective-permute-start | bytes 1536008 | tf_op jit(solution)/shard_map/ppermute | solution.py:312
  77.6 1.7 %collective-permute-start.18 = (bf16[4,80,640]{2,1,0:T(8,128)(2,1)S(1)}, bf16[4,80,640]{2,1,0:T(8,128)(2,1)S(1)}, u32[]{:S(2)}, u32[]{:S(2)}) collective-permute-start(bf16[4,80,640]{2,1,0:T(8,128)(2,1)S(1)} %collective-permute-done.17.refs_15_), channel_id=1, source_target_pairs={{0,4},{4,0},{8,12},{12,8},{16,20},{20,16},{24,28},{28,24},{1,5},{5... | collective-permute-start | bytes 1228808 | tf_op jit(solution)/shard_map/ppermute | solution.py:312
  85.9 9.2 %collective-permute-start.19 = (bf16[168,640]{1,0:T(8,128)(2,1)S(1)}, bf16[168,640]{1,0:T(8,128)(2,1)S(1)}, u32[]{:S(2)}, u32[]{:S(2)}) collective-permute-start(bf16[168,640]{1,0:T(8,128)(2,1)S(1)} %get-tuple-element.33), channel_id=1, source_target_pairs={{0,1},{1,0},{2,3},{3,2},{4,5},{5,4},{6,7},{7,6},{8,9},{9,8},{10,11... | collective-permute-start | bytes 645128 | tf_op jit(solution)/shard_map/ppermute | solution.py:312
  86.0 18.0 %collective-permute-start.20 = (bf16[168,640]{1,0:T(8,128)(2,1)S(1)}, bf16[168,640]{1,0:T(8,128)(2,1)S(1)}, u32[]{:S(2)}, u32[]{:S(2)}) collective-permute-start(bf16[168,640]{1,0:T(8,128)(2,1)S(1)} %get-tuple-element.34), channel_id=1, source_target_pairs={{0,2},{1,3},{2,0},{3,1},{4,6},{5,7},{6,4},{7,5},{8,10},{9,11},{10,... | collective-permute-start | bytes 645128 | tf_op jit(solution)/shard_map/ppermute | solution.py:312
  89.0 19.4 %collective-permute-start.21 = (bf16[168,640]{1,0:T(8,128)(2,1)S(1)}, bf16[168,640]{1,0:T(8,128)(2,1)S(1)}, u32[]{:S(2)}, u32[]{:S(2)}) collective-permute-start(bf16[168,640]{1,0:T(8,128)(2,1)S(1)} %get-tuple-element.35), channel_id=1, source_target_pairs={{0,3},{1,2},{2,1},{3,0},{4,7},{5,6},{6,5},{7,4},{8,11},{9,10},{10,... | collective-permute-start | bytes 645128 | tf_op jit(solution)/shard_map/ppermute | solution.py:312

commit v4 on v3

--- a/solution.py
+++ b/solution.py
@@ -79,7 +79,7 @@
     return jnp.concatenate([scale_ref[h : h + 1, :] for h in range(scale_ref.shape[0])], axis=1)
 
 
-def qkv_kernel(at_ref, x_ref, xl_ref, gain_ref, scale_ref, qw_ref, kw_ref, vw_ref, q_ref, kn_ref, vn_ref, ql_ref, knl_ref, vnl_ref, w_ref, rows_ref, sem):
+def qkv_kernel(at_ref, x_ref, xl_ref, gain_ref, scale_ref, qw_ref, kw_ref, vw_ref, q_ref, kn_ref, vn_ref, ql_ref, knl_ref, vnl_ref, w_ref, rows_ref, long_ref, sem):
     heads, head_dim = scale_ref.shape
     width = heads * head_dim
     short, count = x_ref.shape[1], xl_ref.shape[0]
@@ -89,12 +89,14 @@
         copies = [pltpu.make_async_copy(ref, w_ref.at[pl.ds(i * width, width), :], sem.at[i]) for i, ref in enumerate((qw_ref, kw_ref, vw_ref))]
         for copy in copies:
             copy.start()
-        rows_ref[short:, :] = jnp.zeros((GROUP, rows_ref.shape[1]), F32)
+        long_ref[...] = jnp.zeros_like(long_ref)
+        for step in range(xl_ref.shape[1]):
+            long_ref[step, :count, :] = xl_ref[:, step, :].astype(F32)
         for copy in copies:
             copy.wait()
 
     rows_ref[:short, :] = x_ref[0].astype(F32)
-    rows_ref[short : short + count, :] = step_rows_of(xl_ref[...], pl.program_id(0))
+    rows_ref[short:, :] = long_ref[pl.program_id(0)]
     normed = rms_scale(rows_ref[...], gain_ref[...][None])
     product = dot_t(normed, w_ref[...])
     queries = (product[:, :width] * scale_lanes(scale_ref) * head_dim**-0.5).astype(BF16)
@@ -395,7 +397,12 @@
         },
         out_specs={0: step_rows, 1: step_rows, 2: step_rows, 3: long_rows, 4: long_rows, 5: long_rows},
         grid=(steps,),
-        scratch=(pltpu.VMEM((3 * width, model), BF16), pltpu.VMEM((count + GROUP, model), F32), pltpu.SemaphoreType.DMA((3,))),
+        scratch=(
+            pltpu.VMEM((3 * width, model), BF16),
+            pltpu.VMEM((count + GROUP, model), F32),
+            pltpu.VMEM((steps, GROUP, model), F32),
+            pltpu.SemaphoreType.DMA((3,)),
+        ),
         limit=60,
         name="qkv",
     )

time: 111 us -> 110 us (level)
  transfers between devices with their start and end apart: 22 -> 22, of which waited for: 10 -> 10; matrix products, arithmetic and copies ran while one was open for 0% -> 0% of each run, Pallas kernels for 20% -> 19%
where the time goes in v4:
time: 110 us; the launch traced here: 109 us
  waiting for transfers between devices  50.9 us (46%)
  Pallas kernels  32.9 us (30%)
  starting transfers between devices  19.8 us (18%)
  local copies, waits for them, and re-layouts  4.46 us (4%)
    ppermute x22, waiting for transfers between devices, swap(): return lax.ppermute(value, axis, [(i, i ^ k) for i in range(size)])  50.9 us
    pallas_call x10, Pallas kernels, call(): pl.pallas_call(kernel, grid_spec=pltpu.PrefetchScalarGridSpec(num_scalar_...  32.9 us
    ppermute x22, starting transfers between devices, swap(): return lax.ppermute(value, axis, [(i, i ^ k) for i in range(size)])  19.8 us
    unnamed x36, local copies, waits for them, and re-layouts  4.46 us
  transfers between devices with their start and end apart: 22, of which 10 were waited for; matrix products, arithmetic and copies ran while one was open for 0% of the time, Pallas kernels for 19%

profile of v4, /device:TPU:8, one launch (start us, length us, event | category | flops | bytes accessed | tf_op | source)
XLA Modules:
  0.0 109.5 jit_solution(9941430243824237511)
XLA Ops:
  0.6 0.6 pad_add_fusion.at_ref
  1.2 2.5 %pack_weights.1 = bf16[3,80,640]{2,1,0:T(8,128)(2,1)} custom-call(s32[2]{0:T(128)} %pad_add_fusion.at_ref, bf16[320,1280]{1,0:T(8,128)(2,1)} %refs_4_.1, bf16[320,1280]{1,0:T(8,128)(2,1)} %bitcast.8, bf16[320,1280]{1,0:T(8,128)(2,1)} %refs_6_.1), custom_call_target="tpu_custom_call" | custom-call | bytes 1024 | tf_op jit(solution)/shard_map/pack_weights/pallas_call | solution.py:323
  3.8 3.1 %collective-permute-start.9 = (bf16[3,80,640]{2,1,0:T(8,128)(2,1)}, bf16[3,80,640]{2,1,0:T(8,128)(2,1)S(1)}, u32[]{:S(2)}, u32[]{:S(2)}) collective-permute-start(bf16[3,80,640]{2,1,0:T(8,128)(2,1)} %pack_weights.1), channel_id=1, source_target_pairs={{0,3},{1,2},{2,1},{3,0},{4,7},{5,6},{6,5},{7,4},{8,11},{9,10},{10,... | collective-permute-start | bytes 921608 | tf_op jit(solution)/shard_map/ppermute | solution.py:314
  6.9 1.2 %collective-permute-start.8 = (bf16[3,80,640]{2,1,0:T(8,128)(2,1)}, bf16[3,80,640]{2,1,0:T(8,128)(2,1)S(1)}, u32[]{:S(2)}, u32[]{:S(2)}) collective-permute-start(bf16[3,80,640]{2,1,0:T(8,128)(2,1)} %pack_weights.1), channel_id=1, source_target_pairs={{0,2},{1,3},{2,0},{3,1},{4,6},{5,7},{6,4},{7,5},{8,10},{9,11},{10,... | collective-permute-start | bytes 921608 | tf_op jit(solution)/shard_map/ppermute | solution.py:314
  8.2 9.7 %qkv.1 = (bf16[4,320,320]{2,1,0:T(8,128)(2,1)}, bf16[4,320,320]{2,1,0:T(8,128)(2,1)}, bf16[4,320,320]{2,1,0:T(8,128)(2,1)}, bf16[4,16,320]{2,1,0:T(8,128)(2,1)},...) custom-call(s32[2]{0:T(128)} %pad_add_fusion.at_ref, bf16[4,320,1280]{2,1,0:T(8,128)(2,1)} %x_ref.3, ...), custom_call_target="tpu_custom_call" | custom-call | bytes 1024 | tf_op jit(solution)/shard_map/qkv/pallas_call | solution.py:323
  17.9 0.8 copy-done.8
  18.7 1.1 %long_partial.1.mine_ref = f32[64,384]{1,0:T(8,128)S(1)} custom-call(s32[2]{0:T(128)S(1)} %copy-done.12, bf16[4,16,320]{2,1,0:T(8,128)(2,1)S(1)} %copy-done.8, bf16[12,16,320]{2,1,0:T(8,128)(2,1)S(1)} %copy-done.10, bf16[12,16,320]{2,1,0:T(8,128)(2,1)S(1)} %copy-done.11, s32[12]{0:T(128)S(1)} %copy-done.17), custom_call_target="tpu_custom_call" | custom-call | bytes 1024 | tf_op jit(solution)/shard_map/long_partial/pallas_call | solution.py:323
  19.8 0.1 collective-permute-start
  19.9 1.3 %collective-permute-done.other_ref = f32[64,384]{1,0:T(8,128)S(1)} collective-permute-done((f32[64,384]{1,0:T(8,128)S(1)}, f32[64,384]{1,0:T(8,128)S(1)}, u32[]{:S(2)}, u32[]{:S(2)}) %collective-permute-start) | collective-permute-done | bytes 98336 | tf_op jit(solution)/shard_map/ppermute | solution.py:314
  21.2 1.0 long_pair.1.refs_0_
  22.1 2.5 %collective-permute-start.4 = (f32[64,384]{1,0:T(8,128)S(1)}, f32[64,384]{1,0:T(8,128)S(1)}, u32[]{:S(2)}, u32[]{:S(2)}) collective-permute-start(f32[64,384]{1,0:T(8,128)S(1)} %long_pair.1.refs_0_), channel_id=1, source_target_pairs={{0,24},{4,28},{8,16},{12,20},{16,8},{20,12},{24,0},{28,4},{1,25},{... | collective-permute-start | bytes 294920 | tf_op jit(solution)/shard_map/ppermute | solution.py:314
  24.6 0.5 collective-permute-start.3
  25.1 0.5 collective-permute-start.2
  25.6 1.2 %copy-done.4 = bf16[4,320,320]{2,1,0:T(8,128)(2,1)S(1)} copy-done((bf16[4,320,320]{2,1,0:T(8,128)(2,1)S(1)}, bf16[4,320,320]{2,1,0:T(8,128)(2,1)}, u32[]{:S(2)}) %copy-start.4) | copy-done | bytes 819224
  26.8 1.2 %copy-done.5 = bf16[4,320,320]{2,1,0:T(8,128)(2,1)S(1)} copy-done((bf16[4,320,320]{2,1,0:T(8,128)(2,1)S(1)}, bf16[4,320,320]{2,1,0:T(8,128)(2,1)}, u32[]{:S(2)}) %copy-start.5) | copy-done | bytes 819224
  28.0 1.2 %copy-done.6 = bf16[4,320,320]{2,1,0:T(8,128)(2,1)S(1)} copy-done((bf16[4,320,320]{2,1,0:T(8,128)(2,1)S(1)}, bf16[4,320,320]{2,1,0:T(8,128)(2,1)}, u32[]{:S(2)}) %copy-start.6) | copy-done | bytes 819224
  29.3 7.0 %short_attention.1.att_ref.refs_3_ = bf16[4,320,320]{2,1,0:T(8,128)(2,1)S(1)} custom-call(s32[2]{0:T(128)S(1)} %copy-done.12, bf16[4,320,320]{2,1,0:T(8,128)(2,1)S(1)} %copy-done.4, bf16[4,320,320]{2,1,0:T(8,128)(2,1)S(1)} %copy-done.5, bf16[4,320,320]{2,1,0:T(8,128)(2,1)S(1)} %copy-done.6, bf16[320,16,320]{2,1,0:T(8,128)(2,1)} %k_ref.3, ...), custom_call_target="tpu_custom_call" | custom-call | bytes 1024 | tf_op jit(solution)/shard_map/short_attention/pallas_call | solution.py:323
  36.3 0.0 copy-start
  36.3 0.0 copy-start.1
  36.3 0.0 copy-start.2
  36.3 0.0 copy-start.3
  36.3 0.0 copy-start.7
  36.3 0.0 copy-start.15
  36.4 0.6 stack_weights.1.refs_7_
  37.0 1.6 %collective-permute-start.13 = (bf16[9,80,640]{2,1,0:T(8,128)(2,1)S(1)}, bf16[9,80,640]{2,1,0:T(8,128)(2,1)S(1)}, u32[]{:S(2)}, u32[]{:S(2)}) collective-permute-start(bf16[9,80,640]{2,1,0:T(8,128)(2,1)S(1)} %stack_weights.1.refs_7_), channel_id=1, source_target_pairs={{0,16},{4,20},{8,24},{12,28},{16,0},{20,4},{24,8},{28,12},{1,17},{... | collective-permute-start | bytes 2764808 | tf_op jit(solution)/shard_map/ppermute | solution.py:314
  38.6 1.5 %collective-permute-start.11 = (bf16[9,80,640]{2,1,0:T(8,128)(2,1)S(1)}, bf16[9,80,640]{2,1,0:T(8,128)(2,1)S(1)}, u32[]{:S(2)}, u32[]{:S(2)}) collective-permute-start(bf16[9,80,640]{2,1,0:T(8,128)(2,1)S(1)} %stack_weights.1.refs_7_), channel_id=1, source_target_pairs={{0,8},{4,12},{8,0},{12,4},{16,24},{20,28},{24,16},{28,20},{1,9},{5... | collective-permute-start | bytes 2764808 | tf_op jit(solution)/shard_map/ppermute | solution.py:314
  40.1 2.1 %send_attended.1 = (bf16[168,640]{1,0:T(8,128)(2,1)S(1)}, bf16[168,640]{1,0:T(8,128)(2,1)S(1)}, bf16[168,640]{1,0:T(8,128)(2,1)S(1)}, bf16[168,640]{1,0:T(8,128)(2,1)S(1)}) custom-call(s32[2]{0:T(128)S(1)} %copy-done.12, bf16[4,320,320]{2,1,0:T(8,128)(2,1)S(1)} %short_attention.1.att_ref.refs_3_, bf16[4,16,320]{2,1,0:T(8,128)(2,1)S(1)} %copy-done.9, ...), custom_call_target="tpu_custom_call" | custom-call | bytes 1024 | tf_op jit(solution)/shard_map/send_attended/pallas_call | solution.py:323
  42.2 0.3 collective-permute-start.5
  42.5 2.8 %collective-permute-start.6 = (bf16[168,640]{1,0:T(8,128)(2,1)S(1)}, bf16[168,640]{1,0:T(8,128)(2,1)S(1)}, u32[]{:S(2)}, u32[]{:S(2)}) collective-permute-start(bf16[168,640]{1,0:T(8,128)(2,1)S(1)} %get-tuple-element.28), channel_id=1, source_target_pairs={{0,2},{1,3},{2,0},{3,1},{4,6},{5,7},{6,4},{7,5},{8,10},{9,11},{10,... | collective-permute-start | bytes 645128 | tf_op jit(solution)/shard_map/ppermute | solution.py:314
  45.3 0.4 collective-permute-start.7
  45.8 4.7 %collective-permute-done.5.refs_0_.refs_1_ = bf16[168,640]{1,0:T(8,128)(2,1)S(1)} collective-permute-done((bf16[168,640]{1,0:T(8,128)(2,1)S(1)}, bf16[168,640]{1,0:T(8,128)(2,1)S(1)}, u32[]{:S(2)}, u32[]{:S(2)}) %collective-permute-start.5) | collective-permute-done | bytes 215072 | tf_op jit(solution)/shard_map/ppermute | solution.py:314
  50.5 9.0 %collective-permute-done.6.refs_1_.refs_2_ = bf16[168,640]{1,0:T(8,128)(2,1)S(1)} collective-permute-done((bf16[168,640]{1,0:T(8,128)(2,1)S(1)}, bf16[168,640]{1,0:T(8,128)(2,1)S(1)}, u32[]{:S(2)}, u32[]{:S(2)}) %collective-permute-start.6) | collective-permute-done | bytes 215072 | tf_op jit(solution)/shard_map/ppermute | solution.py:314
  59.6 3.7 %collective-permute-done.7.refs_2_.refs_3_ = bf16[168,640]{1,0:T(8,128)(2,1)S(1)} collective-permute-done((bf16[168,640]{1,0:T(8,128)(2,1)S(1)}, bf16[168,640]{1,0:T(8,128)(2,1)S(1)}, u32[]{:S(2)}, u32[]{:S(2)}) %collective-permute-start.7) | collective-permute-done | bytes 215072 | tf_op jit(solution)/shard_map/ppermute | solution.py:314
  63.3 0.6 cut_weights.1
  63.9 0.6 collective-permute-start.15
  64.5 0.5 collective-permute-start.14
  65.0 0.5 collective-permute-start.17
  65.5 9.5 %collective-permute-done.15.refs_13_ = bf16[5,80,640]{2,1,0:T(8,128)(2,1)S(1)} collective-permute-done((bf16[5,80,640]{2,1,0:T(8,128)(2,1)S(1)}, bf16[5,80,640]{2,1,0:T(8,128)(2,1)S(1)}, u32[]{:S(2)}, u32[]{:S(2)}) %collective-permute-start.15) | collective-permute-done | bytes 512032 | tf_op jit(solution)/shard_map/ppermute | solution.py:314
  75.0 1.9 %collective-permute-done.17.refs_15_ = bf16[4,80,640]{2,1,0:T(8,128)(2,1)S(1)} collective-permute-done((bf16[4,80,640]{2,1,0:T(8,128)(2,1)S(1)}, bf16[4,80,640]{2,1,0:T(8,128)(2,1)S(1)}, u32[]{:S(2)}, u32[]{:S(2)}) %collective-permute-start.17) | collective-permute-done | bytes 409632 | tf_op jit(solution)/shard_map/ppermute | solution.py:314
  76.9 1.7 %collective-permute-done.18.refs_16_ = bf16[4,80,640]{2,1,0:T(8,128)(2,1)S(1)} collective-permute-done((bf16[4,80,640]{2,1,0:T(8,128)(2,1)S(1)}, bf16[4,80,640]{2,1,0:T(8,128)(2,1)S(1)}, u32[]{:S(2)}, u32[]{:S(2)}) %collective-permute-start.18) | collective-permute-done | bytes 409632 | tf_op jit(solution)/shard_map/ppermute | solution.py:314
  78.7 6.5 %feed_forward.1 = (bf16[168,640]{1,0:T(8,128)(2,1)S(1)}, bf16[168,640]{1,0:T(8,128)(2,1)S(1)}, bf16[168,640]{1,0:T(8,128)(2,1)S(1)}, bf16[168,640]{1,0:T(8,128)(2,1)S(1)}) custom-call(s32[2]{0:T(128)S(1)} %copy-done.12, bf16[4,320,1280]{2,1,0:T(8,128)(2,1)S(1)} %copy-done, bf16[12,4,1280]{2,1,0:T(4,128)(2,1)S(1)} %bitcast.11, f32[1280]{0:T(1024)S(1)} %copy-done.15, ...), custom_call_target="tpu_custom_call" | custom-call | flops 3303014400 | bytes 1024 | tf_op jit(solution)/shard_map/feed_forward/pallas_call | solution.py:323
  85.2 0.1 collective-permute-start.19
  85.3 3.0 %collective-permute-start.20 = (bf16[168,640]{1,0:T(8,128)(2,1)S(1)}, bf16[168,640]{1,0:T(8,128)(2,1)S(1)}, u32[]{:S(2)}, u32[]{:S(2)}) collective-permute-start(bf16[168,640]{1,0:T(8,128)(2,1)S(1)} %get-tuple-element.34), channel_id=1, source_target_pairs={{0,2},{1,3},{2,0},{3,1},{4,6},{5,7},{6,4},{7,5},{8,10},{9,11},{10,... | collective-permute-start | bytes 645128 | tf_op jit(solution)/shard_map/ppermute | solution.py:314
  88.4 0.4 collective-permute-start.21
  88.8 5.7 %collective-permute-done.19.refs_1_ = bf16[168,640]{1,0:T(8,128)(2,1)S(1)} collective-permute-done((bf16[168,640]{1,0:T(8,128)(2,1)S(1)}, bf16[168,640]{1,0:T(8,128)(2,1)S(1)}, u32[]{:S(2)}, u32[]{:S(2)}) %collective-permute-start.19) | collective-permute-done | bytes 215072 | tf_op jit(solution)/shard_map/ppermute | solution.py:314
  94.5 8.8 %collective-permute-done.20.refs_2_ = bf16[168,640]{1,0:T(8,128)(2,1)S(1)} collective-permute-done((bf16[168,640]{1,0:T(8,128)(2,1)S(1)}, bf16[168,640]{1,0:T(8,128)(2,1)S(1)}, u32[]{:S(2)}, u32[]{:S(2)}) %collective-permute-start.20) | collective-permute-done | bytes 215072 | tf_op jit(solution)/shard_map/ppermute | solution.py:314
  103.3 4.4 %collective-permute-done.21.refs_3_ = bf16[168,640]{1,0:T(8,128)(2,1)S(1)} collective-permute-done((bf16[168,640]{1,0:T(8,128)(2,1)S(1)}, bf16[168,640]{1,0:T(8,128)(2,1)S(1)}, u32[]{:S(2)}, u32[]{:S(2)}) %collective-permute-start.21) | collective-permute-done | bytes 215072 | tf_op jit(solution)/shard_map/ppermute | solution.py:314
  107.7 1.7 %place_outputs.1 = (bf16[4,320,320]{2,1,0:T(8,128)(2,1)}, bf16[12,4,320]{2,1,0:T(4,128)(2,1)}) custom-call(s32[2]{0:T(128)S(1)} %copy-done.12, bf16[168,640]{1,0:T(8,128)(2,1)S(1)} %get-tuple-element.32.refs_0_, bf16[168,640]{1,0:T(8,128)(2,1)S(1)} %collective-permute-done.19.refs_1_, bf16[168,640]{1,0:T(8,128)(2,1)S(1)} %collective-permute-done.20.refs_2_, ...), custom_call_target="tpu_custom_call" | custom-call | bytes 1024 | tf_op jit(solution)/shard_map/place_outputs/pallas_call | solution.py:323
  (43 shorter events, 0.1 us)
Async XLA Ops:
  1.2 16.6 %copy-start.10 = (bf16[12,16,320]{2,1,0:T(8,128)(2,1)S(1)}, bf16[12,16,320]{2,1,0:T(8,128)(2,1)}, u32[]{:S(2)}) copy-start(bf16[12,16,320]{2,1,0:T(8,128)(2,1)} %k_ref.2) | copy-start | bytes 368644
  1.2 16.6 %copy-start.11 = (bf16[12,16,320]{2,1,0:T(8,128)(2,1)S(1)}, bf16[12,16,320]{2,1,0:T(8,128)(2,1)}, u32[]{:S(2)}) copy-start(bf16[12,16,320]{2,1,0:T(8,128)(2,1)} %v_ref.2) | copy-start | bytes 368644
  1.2 16.6 %copy-start.12 = (s32[2]{0:T(128)S(1)}, s32[2]{0:T(128)}, u32[]{:S(2)}) copy-start(s32[2]{0:T(128)} %pad_add_fusion.at_ref) | copy-start | bytes 28
  1.2 16.6 %copy-start.17 = (s32[12]{0:T(128)S(1)}, s32[12]{0:T(128)}, u32[]{:S(2)}) copy-start(s32[12]{0:T(128)} %len_ref.2) | copy-start | bytes 148
  3.8 21.9 %copy-start.16 = (s32[320]{0:T(512)S(1)}, s32[320]{0:T(512)}, u32[]{:S(2)}) copy-start(s32[320]{0:T(512)} %len_ref.3) | copy-start | bytes 3844
  3.8 17.4 %collective-permute-start.1 = (bf16[3,80,640]{2,1,0:T(8,128)(2,1)}, bf16[3,80,640]{2,1,0:T(8,128)(2,1)S(1)}, u32[]{:S(2)}, u32[]{:S(2)}) collective-permute-start(bf16[3,80,640]{2,1,0:T(8,128)(2,1)} %pack_weights.1), channel_id=1, source_target_pairs={{0,1},{1,0},{2,3},{3,2},{4,5},{5,4},{6,7},{7,6},{8,9},{9,8},{10,11... | collective-permute-start | bytes 921608 | tf_op jit(solution)/shard_map/ppermute | solution.py:314
  3.8 32.5 %collective-permute-start.9 = (bf16[3,80,640]{2,1,0:T(8,128)(2,1)}, bf16[3,80,640]{2,1,0:T(8,128)(2,1)S(1)}, u32[]{:S(2)}, u32[]{:S(2)}) collective-permute-start(bf16[3,80,640]{2,1,0:T(8,128)(2,1)} %pack_weights.1), channel_id=1, source_target_pairs={{0,3},{1,2},{2,1},{3,0},{4,7},{5,6},{6,5},{7,4},{8,11},{9,10},{10,... | collective-permute-start | bytes 921608 | tf_op jit(solution)/shard_map/ppermute | solution.py:314
  6.9 29.4 %collective-permute-start.8 = (bf16[3,80,640]{2,1,0:T(8,128)(2,1)}, bf16[3,80,640]{2,1,0:T(8,128)(2,1)S(1)}, u32[]{:S(2)}, u32[]{:S(2)}) collective-permute-start(bf16[3,80,640]{2,1,0:T(8,128)(2,1)} %pack_weights.1), channel_id=1, source_target_pairs={{0,2},{1,3},{2,0},{3,1},{4,6},{5,7},{6,4},{7,5},{8,10},{9,11},{10,... | collective-permute-start | bytes 921608 | tf_op jit(solution)/shard_map/ppermute | solution.py:314
  17.9 0.8 copy-start.8
  19.8 1.4 %collective-permute-start = (f32[64,384]{1,0:T(8,128)S(1)}, f32[64,384]{1,0:T(8,128)S(1)}, u32[]{:S(2)}, u32[]{:S(2)}) collective-permute-start(f32[64,384]{1,0:T(8,128)S(1)} %long_partial.1.mine_ref), channel_id=1, source_target_pairs={{0,4},{4,0},{8,12},{12,8},{16,20},{20,16},{24,28},{28,24},{1,5},{5... | collective-permute-start | bytes 294920 | tf_op jit(solution)/shard_map/ppermute | solution.py:314
  22.1 14.2 %collective-permute-start.4 = (f32[64,384]{1,0:T(8,128)S(1)}, f32[64,384]{1,0:T(8,128)S(1)}, u32[]{:S(2)}, u32[]{:S(2)}) collective-permute-start(f32[64,384]{1,0:T(8,128)S(1)} %long_pair.1.refs_0_), channel_id=1, source_target_pairs={{0,24},{4,28},{8,16},{12,20},{16,8},{20,12},{24,0},{28,4},{1,25},{... | collective-permute-start | bytes 294920 | tf_op jit(solution)/shard_map/ppermute | solution.py:314
  24.6 11.8 %collective-permute-start.3 = (f32[64,384]{1,0:T(8,128)S(1)}, f32[64,384]{1,0:T(8,128)S(1)}, u32[]{:S(2)}, u32[]{:S(2)}) collective-permute-start(f32[64,384]{1,0:T(8,128)S(1)} %long_pair.1.refs_0_), channel_id=1, source_target_pairs={{0,16},{4,20},{8,24},{12,28},{16,0},{20,4},{24,8},{28,12},{1,17},{... | collective-permute-start | bytes 294920 | tf_op jit(solution)/shard_map/ppermute | solution.py:314
  25.1 11.3 %collective-permute-start.2 = (f32[64,384]{1,0:T(8,128)S(1)}, f32[64,384]{1,0:T(8,128)S(1)}, u32[]{:S(2)}, u32[]{:S(2)}) collective-permute-start(f32[64,384]{1,0:T(8,128)S(1)} %long_pair.1.refs_0_), channel_id=1, source_target_pairs={{0,8},{4,12},{8,0},{12,4},{16,24},{20,28},{24,16},{28,20},{1,9},{5... | collective-permute-start | bytes 294920 | tf_op jit(solution)/shard_map/ppermute | solution.py:314
  25.6 1.2 %copy-start.4 = (bf16[4,320,320]{2,1,0:T(8,128)(2,1)S(1)}, bf16[4,320,320]{2,1,0:T(8,128)(2,1)}, u32[]{:S(2)}) copy-start(bf16[4,320,320]{2,1,0:T(8,128)(2,1)} %get-tuple-element.20.q_ref) | copy-start | bytes 2457604
  26.8 1.2 %copy-start.5 = (bf16[4,320,320]{2,1,0:T(8,128)(2,1)S(1)}, bf16[4,320,320]{2,1,0:T(8,128)(2,1)}, u32[]{:S(2)}) copy-start(bf16[4,320,320]{2,1,0:T(8,128)(2,1)} %get-tuple-element.21.kn_ref) | copy-start | bytes 2457604
  28.0 1.2 %copy-start.6 = (bf16[4,320,320]{2,1,0:T(8,128)(2,1)S(1)}, bf16[4,320,320]{2,1,0:T(8,128)(2,1)}, u32[]{:S(2)}) copy-start(bf16[4,320,320]{2,1,0:T(8,128)(2,1)} %get-tuple-element.22.vn_ref) | copy-start | bytes 2457604
  29.2 10.8 %copy-start.9 = (bf16[4,16,320]{2,1,0:T(8,128)(2,1)S(1)}, bf16[4,16,320]{2,1,0:T(8,128)(2,1)}, u32[]{:S(2)}) copy-start(bf16[4,16,320]{2,1,0:T(8,128)(2,1)} %get-tuple-element.23.q_ref.ql_ref) | copy-start | bytes 122884
  29.2 10.8 %copy-start.13 = (bf16[4,16,320]{2,1,0:T(8,128)(2,1)S(1)}, bf16[4,16,320]{2,1,0:T(8,128)(2,1)}, u32[]{:S(2)}) copy-start(bf16[4,16,320]{2,1,0:T(8,128)(2,1)} %get-tuple-element.24.knl_ref) | copy-start | bytes 122884
  29.2 10.8 %copy-start.14 = (bf16[4,16,320]{2,1,0:T(8,128)(2,1)S(1)}, bf16[4,16,320]{2,1,0:T(8,128)(2,1)}, u32[]{:S(2)}) copy-start(bf16[4,16,320]{2,1,0:T(8,128)(2,1)} %get-tuple-element.25.vnl_ref) | copy-start | bytes 122884
  36.3 42.4 %copy-start = (bf16[4,320,1280]{2,1,0:T(8,128)(2,1)S(1)}, bf16[4,320,1280]{2,1,0:T(8,128)(2,1)}, u32[]{:S(2)}) copy-start(bf16[4,320,1280]{2,1,0:T(8,128)(2,1)} %x_ref.3) | copy-start | bytes 9830404
  36.3 42.4 %copy-start.1 = (bf16[320,1280]{1,0:T(8,128)(2,1)S(1)}, bf16[320,1280]{1,0:T(8,128)(2,1)}, u32[]{:S(2)}) copy-start(bf16[320,1280]{1,0:T(8,128)(2,1)} %refs_4_.1) | copy-start | bytes 2457604
  36.3 42.4 %copy-start.2 = (bf16[1280,320]{0,1:T(8,128)(2,1)S(1)}, bf16[1280,320]{0,1:T(8,128)(2,1)}, u32[]{:S(2)}) copy-start(bf16[1280,320]{0,1:T(8,128)(2,1)} %param.32) | copy-start | bytes 2457604
  36.3 42.4 %copy-start.3 = (bf16[320,1280]{1,0:T(8,128)(2,1)S(1)}, bf16[320,1280]{1,0:T(8,128)(2,1)}, u32[]{:S(2)}) copy-start(bf16[320,1280]{1,0:T(8,128)(2,1)} %refs_6_.1) | copy-start | bytes 2457604
  36.3 42.4 %copy-start.7 = (bf16[4,12,1280]{2,0,1:T(4,128)(2,1)S(1)}, bf16[4,12,1280]{2,0,1:T(4,128)(2,1)}, u32[]{:S(2)}) copy-start(bf16[4,12,1280]{2,0,1:T(4,128)(2,1)} %param.18) | copy-start | bytes 368644
  36.3 42.4 %copy-start.15 = (f32[1280]{0:T(1024)S(1)}, f32[1280]{0:T(1024)}, u32[]{:S(2)}) copy-start(f32[1280]{0:T(1024)} %gain_ref.3) | copy-start | bytes 15364
  37.0 26.3 %collective-permute-start.13 = (bf16[9,80,640]{2,1,0:T(8,128)(2,1)S(1)}, bf16[9,80,640]{2,1,0:T(8,128)(2,1)S(1)}, u32[]{:S(2)}, u32[]{:S(2)}) collective-permute-start(bf16[9,80,640]{2,1,0:T(8,128)(2,1)S(1)} %stack_weights.1.refs_7_), channel_id=1, source_target_pairs={{0,16},{4,20},{8,24},{12,28},{16,0},{20,4},{24,8},{28,12},{1,17},{... | collective-permute-start | bytes 2764808 | tf_op jit(solution)/shard_map/ppermute | solution.py:314
  38.6 24.7 %collective-permute-start.11 = (bf16[9,80,640]{2,1,0:T(8,128)(2,1)S(1)}, bf16[9,80,640]{2,1,0:T(8,128)(2,1)S(1)}, u32[]{:S(2)}, u32[]{:S(2)}) collective-permute-start(bf16[9,80,640]{2,1,0:T(8,128)(2,1)S(1)} %stack_weights.1.refs_7_), channel_id=1, source_target_pairs={{0,8},{4,12},{8,0},{12,4},{16,24},{20,28},{24,16},{28,20},{1,9},{5... | collective-permute-start | bytes 2764808 | tf_op jit(solution)/shard_map/ppermute | solution.py:314
  42.2 8.3 %collective-permute-start.5 = (bf16[168,640]{1,0:T(8,128)(2,1)S(1)}, bf16[168,640]{1,0:T(8,128)(2,1)S(1)}, u32[]{:S(2)}, u32[]{:S(2)}) collective-permute-start(bf16[168,640]{1,0:T(8,128)(2,1)S(1)} %get-tuple-element.27), channel_id=1, source_target_pairs={{0,1},{1,0},{2,3},{3,2},{4,5},{5,4},{6,7},{7,6},{8,9},{9,8},{10,11... | collective-permute-start | bytes 645128 | tf_op jit(solution)/shard_map/ppermute | solution.py:314
  42.5 17.0 %collective-permute-start.6 = (bf16[168,640]{1,0:T(8,128)(2,1)S(1)}, bf16[168,640]{1,0:T(8,128)(2,1)S(1)}, u32[]{:S(2)}, u32[]{:S(2)}) collective-permute-start(bf16[168,640]{1,0:T(8,128)(2,1)S(1)} %get-tuple-element.28), channel_id=1, source_target_pairs={{0,2},{1,3},{2,0},{3,1},{4,6},{5,7},{6,4},{7,5},{8,10},{9,11},{10,... | collective-permute-start | bytes 645128 | tf_op jit(solution)/shard_map/ppermute | solution.py:314
  45.3 18.0 %collective-permute-start.7 = (bf16[168,640]{1,0:T(8,128)(2,1)S(1)}, bf16[168,640]{1,0:T(8,128)(2,1)S(1)}, u32[]{:S(2)}, u32[]{:S(2)}) collective-permute-start(bf16[168,640]{1,0:T(8,128)(2,1)S(1)} %get-tuple-element.29), channel_id=1, source_target_pairs={{0,3},{1,2},{2,1},{3,0},{4,7},{5,6},{6,5},{7,4},{8,11},{9,10},{10,... | collective-permute-start | bytes 645128 | tf_op jit(solution)/shard_map/ppermute | solution.py:314
  63.9 11.1 %collective-permute-start.15 = (bf16[5,80,640]{2,1,0:T(8,128)(2,1)S(1)}, bf16[5,80,640]{2,1,0:T(8,128)(2,1)S(1)}, u32[]{:S(2)}, u32[]{:S(2)}) collective-permute-start(bf16[5,80,640]{2,1,0:T(8,128)(2,1)S(1)} %get-tuple-element.30), channel_id=1, source_target_pairs={{0,8},{4,12},{8,0},{12,4},{16,24},{20,28},{24,16},{28,20},{1,9},{5... | collective-permute-start | bytes 1536008 | tf_op jit(solution)/shard_map/ppermute | solution.py:314
  64.5 12.4 %collective-permute-start.10 = (bf16[9,80,640]{2,1,0:T(8,128)(2,1)S(1)}, bf16[9,80,640]{2,1,0:T(8,128)(2,1)S(1)}, u32[]{:S(2)}, u32[]{:S(2)}) collective-permute-start(bf16[9,80,640]{2,1,0:T(8,128)(2,1)S(1)} %stack_weights.1.refs_7_), channel_id=1, source_target_pairs={{0,4},{4,0},{8,12},{12,8},{16,20},{20,16},{24,28},{28,24},{1,5},{5... | collective-permute-start | bytes 2764808 | tf_op jit(solution)/shard_map/ppermute | solution.py:314
  64.5 14.1 %collective-permute-start.14 = (bf16[9,80,640]{2,1,0:T(8,128)(2,1)S(1)}, bf16[9,80,640]{2,1,0:T(8,128)(2,1)S(1)}, u32[]{:S(2)}, u32[]{:S(2)}) collective-permute-start(bf16[9,80,640]{2,1,0:T(8,128)(2,1)S(1)} %collective-permute-done.13.y_ref.refs_11_), channel_id=1, source_target_pairs={{0,4},{4,0},{8,12},{12,8},{16,20},{20,16},{24,28},{28,24},{1,5},{5... | collective-permute-start | bytes 2764808 | tf_op jit(solution)/shard_map/ppermute | solution.py:314
  65.0 13.6 %collective-permute-start.12 = (bf16[9,80,640]{2,1,0:T(8,128)(2,1)S(1)}, bf16[9,80,640]{2,1,0:T(8,128)(2,1)S(1)}, u32[]{:S(2)}, u32[]{:S(2)}) collective-permute-start(bf16[9,80,640]{2,1,0:T(8,128)(2,1)S(1)} %collective-permute-done.11.x_ref.refs_9_), channel_id=1, source_target_pairs={{0,4},{4,0},{8,12},{12,8},{16,20},{20,16},{24,28},{28,24},{1,5},{5... | collective-permute-start | bytes 2764808 | tf_op jit(solution)/shard_map/ppermute | solution.py:314
  65.0 11.9 %collective-permute-start.17 = (bf16[4,80,640]{2,1,0:T(8,128)(2,1)S(1)}, bf16[4,80,640]{2,1,0:T(8,128)(2,1)S(1)}, u32[]{:S(2)}, u32[]{:S(2)}) collective-permute-start(bf16[4,80,640]{2,1,0:T(8,128)(2,1)S(1)} %get-tuple-element.31), channel_id=1, source_target_pairs={{0,16},{4,20},{8,24},{12,28},{16,0},{20,4},{24,8},{28,12},{1,17},{... | collective-permute-start | bytes 1228808 | tf_op jit(solution)/shard_map/ppermute | solution.py:314
  75.0 3.7 %collective-permute-start.16 = (bf16[5,80,640]{2,1,0:T(8,128)(2,1)S(1)}, bf16[5,80,640]{2,1,0:T(8,128)(2,1)S(1)}, u32[]{:S(2)}, u32[]{:S(2)}) collective-permute-start(bf16[5,80,640]{2,1,0:T(8,128)(2,1)S(1)} %collective-permute-done.15.refs_13_), channel_id=1, source_target_pairs={{0,4},{4,0},{8,12},{12,8},{16,20},{20,16},{24,28},{28,24},{1,5},{5... | collective-permute-start | bytes 1536008 | tf_op jit(solution)/shard_map/ppermute | solution.py:314
  76.9 1.7 %collective-permute-start.18 = (bf16[4,80,640]{2,1,0:T(8,128)(2,1)S(1)}, bf16[4,80,640]{2,1,0:T(8,128)(2,1)S(1)}, u32[]{:S(2)}, u32[]{:S(2)}) collective-permute-start(bf16[4,80,640]{2,1,0:T(8,128)(2,1)S(1)} %collective-permute-done.17.refs_15_), channel_id=1, source_target_pairs={{0,4},{4,0},{8,12},{12,8},{16,20},{20,16},{24,28},{28,24},{1,5},{5... | collective-permute-start | bytes 1228808 | tf_op jit(solution)/shard_map/ppermute | solution.py:314
  85.2 9.2 %collective-permute-start.19 = (bf16[168,640]{1,0:T(8,128)(2,1)S(1)}, bf16[168,640]{1,0:T(8,128)(2,1)S(1)}, u32[]{:S(2)}, u32[]{:S(2)}) collective-permute-start(bf16[168,640]{1,0:T(8,128)(2,1)S(1)} %get-tuple-element.33), channel_id=1, source_target_pairs={{0,1},{1,0},{2,3},{3,2},{4,5},{5,4},{6,7},{7,6},{8,9},{9,8},{10,11... | collective-permute-start | bytes 645128 | tf_op jit(solution)/shard_map/ppermute | solution.py:314
  85.3 18.0 %collective-permute-start.20 = (bf16[168,640]{1,0:T(8,128)(2,1)S(1)}, bf16[168,640]{1,0:T(8,128)(2,1)S(1)}, u32[]{:S(2)}, u32[]{:S(2)}) collective-permute-start(bf16[168,640]{1,0:T(8,128)(2,1)S(1)} %get-tuple-element.34), channel_id=1, source_target_pairs={{0,2},{1,3},{2,0},{3,1},{4,6},{5,7},{6,4},{7,5},{8,10},{9,11},{10,... | collective-permute-start | bytes 645128 | tf_op jit(solution)/shard_map/ppermute | solution.py:314
  88.4 19.4 %collective-permute-start.21 = (bf16[168,640]{1,0:T(8,128)(2,1)S(1)}, bf16[168,640]{1,0:T(8,128)(2,1)S(1)}, u32[]{:S(2)}, u32[]{:S(2)}) collective-permute-start(bf16[168,640]{1,0:T(8,128)(2,1)S(1)} %get-tuple-element.35), channel_id=1, source_target_pairs={{0,3},{1,2},{2,1},{3,0},{4,7},{5,6},{6,5},{7,4},{8,11},{9,10},{10,... | collective-permute-start | bytes 645128 | tf_op jit(solution)/shard_map/ppermute | solution.py:314

commit v5 on v4

--- a/solution.py
+++ b/solution.py
@@ -79,7 +79,7 @@
     return jnp.concatenate([scale_ref[h : h + 1, :] for h in range(scale_ref.shape[0])], axis=1)
 
 
-def qkv_kernel(at_ref, x_ref, xl_ref, gain_ref, scale_ref, qw_ref, kw_ref, vw_ref, q_ref, kn_ref, vn_ref, ql_ref, knl_ref, vnl_ref, w_ref, rows_ref, long_ref, sem):
+def qkv_kernel(at_ref, x_ref, xl_ref, gain_ref, scale_ref, qw_ref, kw_ref, vw_ref, fresh_ref, ql_ref, knl_ref, vnl_ref, w_ref, rows_ref, long_ref, sem):
     heads, head_dim = scale_ref.shape
     width = heads * head_dim
     short, count = x_ref.shape[1], xl_ref.shape[0]
@@ -102,9 +102,9 @@
     queries = (product[:, :width] * scale_lanes(scale_ref) * head_dim**-0.5).astype(BF16)
     keys = product[:, width : 2 * width].astype(BF16)
     values = product[:, 2 * width :].astype(BF16)
-    for rows, short_ref, long_ref in ((queries, q_ref, ql_ref), (keys, kn_ref, knl_ref), (values, vn_ref, vnl_ref)):
-        short_ref[0] = rows[:short]
-        long_ref[0] = rows[short:]
+    for i, (rows, long_out) in enumerate(((queries, ql_ref), (keys, knl_ref), (values, vnl_ref))):
+        fresh_ref[i, 0] = rows[:short]
+        long_out[0] = rows[short:]
 
 
 def put_sums(part_ref, row_max, weight_sum, width, heads):
@@ -173,9 +173,9 @@
     return acc / pick_heads(denom, heads, width)
 
 
-def short_kernel(heads, at_ref, q_ref, kn_ref, vn_ref, k_ref, v_ref, len_ref, *refs):
+def short_kernel(heads, at_ref, fresh_ref, k_ref, v_ref, len_ref, *refs):
     att_ref = refs[-1]
-    steps, block, width = q_ref.shape
+    _, steps, block, width = fresh_ref.shape
     slots = k_ref.shape[1]
     few = GROUP // 2
     n = steps * few
@@ -193,7 +193,7 @@
     for g in groups:
         at, lo = slice(g * few, (g + 1) * few), g // 2 * GROUP
         half = g % 2 * few
-        new = [ref[:, lo : lo + GROUP, :].astype(F32)[:, half : half + few, :].reshape(n, width).astype(BF16) for ref in (q_ref, kn_ref, vn_ref)]
+        new = [fresh_ref[j, :, lo : lo + GROUP, :].astype(F32)[:, half : half + few, :].reshape(n, width).astype(BF16) for j in range(3)]
         queries.append(stack_heads(new[0], heads))
         keys.append(jnp.concatenate([k_ref[at].reshape(cached, width), new[1]], axis=0))
         values.append(jnp.concatenate([v_ref[at].reshape(cached, width), new[2]], axis=0))
@@ -284,10 +284,11 @@
     pre = dot_t(normed, w_ref[1])
     hidden = (pre * (0.5 + 0.5 * jnp.tanh(0.5 * pre))).astype(BF16)
     out = mid + dot(hidden, w_ref[2])
+    narrow = out[: 2 * half].astype(BF16)
     for b in range(tp):
-        cols = out[:, b * width : (b + 1) * width]
-        cols_ref[b, :half, :] = jnp.concatenate([cols[:half], cols[half : 2 * half]], axis=1).astype(BF16)
-        tail = cols[2 * half :]
+        cols = narrow[:, b * width : (b + 1) * width]
+        cols_ref[b, :half, :] = jnp.concatenate([cols[:half], cols[half:]], axis=1)
+        tail = out[2 * half :, b * width : (b + 1) * width]
         cols_ref[b, half:, :] = jnp.concatenate([tail[: GROUP // 2], tail[GROUP // 2 :]], axis=1).astype(BF16)
     for k in range(tp):
         outs[k][...] = cols_ref[at_ref[1] ^ k]
@@ -382,20 +383,20 @@
     units = [swap(own, "tp", k) for k in range(1, tp)]
 
     n = steps * GROUP
-    step_rows = pl.BlockSpec((1, count, width), lambda i, at: (i, 0, 0))
+    step_rows = pl.BlockSpec((3, 1, count, width), lambda i, at: (0, i, 0, 0))
     long_rows = pl.BlockSpec((1, GROUP, width), lambda i, at: (i, 0, 0))
-    q, kn, vn, q_long, kn_long, vn_long = call(
+    fresh, q_long, kn_long, vn_long = call(
         qkv_kernel,
         at,
         (short_inputs, long_rows_in, attn_gain, query_scale, q_weight.T, k_weight.T, v_weight.T),
-        (shape((steps, count, width), BF16),) * 3 + (shape((steps, GROUP, width), BF16),) * 3,
+        (shape((3, steps, count, width), BF16),) + (shape((steps, GROUP, width), BF16),) * 3,
         specs={
             0: pl.BlockSpec((1, count, model), lambda i, at: (i, 0, 0)),
             4: in_hbm,
             5: in_hbm,
             6: in_hbm,
         },
-        out_specs={0: step_rows, 1: step_rows, 2: step_rows, 3: long_rows, 4: long_rows, 5: long_rows},
+        out_specs={0: step_rows, 1: long_rows, 2: long_rows, 3: long_rows},
         grid=(steps,),
         scratch=(
             pltpu.VMEM((3 * width, model), BF16),
@@ -419,9 +420,9 @@
     (att,) = call(
         functools.partial(short_kernel, heads),
         at,
-        (q, kn, vn, short_keys, short_values, short_len, part),
+        (fresh, short_keys, short_values, short_len, part),
         (shape((steps, count, width), BF16),),
-        specs={0: fresh_rows, 1: fresh_rows, 2: fresh_rows, 3: cache_rows, 4: cache_rows, 6: in_hbm},
+        specs={0: pl.BlockSpec((3, steps, block, width), lambda i, at: (0, 0, i, 0)), 1: cache_rows, 2: cache_rows, 4: in_hbm},
         out_specs={0: fresh_rows},
         grid=(count // block,),
         limit=50,

time: 110 us -> 108 us (0.982)
  local copies, waits for them, and re-layouts: 4.46 us -> 2.69 us
    unnamed x36 -> x32, local copies, waits for them, and re-layouts: 4.46 us -> 2.69 us
where the time goes in v5:
time: 108 us
  waiting for transfers between devices  50.9 us (47%)
  Pallas kernels  33 us (31%)
  starting transfers between devices  19.7 us (18%)
  local copies, waits for them, and re-layouts  2.69 us (2%)
    ppermute x22, waiting for transfers between devices, swap(): return lax.ppermute(value, axis, [(i, i ^ k) for i in range(size)])  50.9 us
    pallas_call x10, Pallas kernels, call(): pl.pallas_call(kernel, grid_spec=pltpu.PrefetchScalarGridSpec(num_scalar_...  33 us
    ppermute x22, starting transfers between devices, swap(): return lax.ppermute(value, axis, [(i, i ^ k) for i in range(size)])  19.7 us
    unnamed x32, local copies, waits for them, and re-layouts  2.69 us
  transfers between devices with their start and end apart: 22, of which 10 were waited for; matrix products, arithmetic and copies ran while one was open for 0% of the time, Pallas kernels for 19%

profile of v5, /device:TPU:8, one launch (start us, length us, event | category | flops | bytes accessed | tf_op | source)
XLA Modules:
  0.0 107.9 jit_solution(13939097772417442692)
XLA Ops:
  0.6 0.6 pad_add_fusion.at_ref
  1.3 2.5 %pack_weights.1 = bf16[3,80,640]{2,1,0:T(8,128)(2,1)} custom-call(s32[2]{0:T(128)} %pad_add_fusion.at_ref, bf16[320,1280]{1,0:T(8,128)(2,1)} %refs_4_.1, bf16[320,1280]{1,0:T(8,128)(2,1)} %bitcast.8, bf16[320,1280]{1,0:T(8,128)(2,1)} %refs_6_.1), custom_call_target="tpu_custom_call" | custom-call | bytes 1024 | tf_op jit(solution)/shard_map/pack_weights/pallas_call | solution.py:324
  3.8 3.1 %collective-permute-start.9 = (bf16[3,80,640]{2,1,0:T(8,128)(2,1)}, bf16[3,80,640]{2,1,0:T(8,128)(2,1)S(1)}, u32[]{:S(2)}, u32[]{:S(2)}) collective-permute-start(bf16[3,80,640]{2,1,0:T(8,128)(2,1)} %pack_weights.1), channel_id=1, source_target_pairs={{0,3},{1,2},{2,1},{3,0},{4,7},{5,6},{6,5},{7,4},{8,11},{9,10},{10,... | collective-permute-start | bytes 921608 | tf_op jit(solution)/shard_map/ppermute | solution.py:315
  7.0 1.2 %collective-permute-start.8 = (bf16[3,80,640]{2,1,0:T(8,128)(2,1)}, bf16[3,80,640]{2,1,0:T(8,128)(2,1)S(1)}, u32[]{:S(2)}, u32[]{:S(2)}) collective-permute-start(bf16[3,80,640]{2,1,0:T(8,128)(2,1)} %pack_weights.1), channel_id=1, source_target_pairs={{0,2},{1,3},{2,0},{3,1},{4,6},{5,7},{6,4},{7,5},{8,10},{9,11},{10,... | collective-permute-start | bytes 921608 | tf_op jit(solution)/shard_map/ppermute | solution.py:315
  8.2 9.8 %qkv.1 = (bf16[3,4,320,320]{3,2,1,0:T(8,128)(2,1)}, bf16[4,16,320]{2,1,0:T(8,128)(2,1)}, bf16[4,16,320]{2,1,0:T(8,128)(2,1)}, bf16[4,16,320]{2,1,0:T(8,128)(2,1)}) custom-call(s32[2]{0:T(128)} %pad_add_fusion.at_ref, bf16[4,320,1280]{2,1,0:T(8,128)(2,1)} %x_ref.3, bf16[12,4,1280]{2,1,0:T(4,128)(2,1)} %bitcast.10, f32[1280]{0:T(1024)} %gain_ref.2, ...), custom_call_target="tpu_custom_call" | custom-call | bytes 1024 | tf_op jit(solution)/shard_map/qkv/pallas_call | solution.py:324
  18.1 0.8 copy-done.6
  18.9 1.1 %long_partial.1.mine_ref = f32[64,384]{1,0:T(8,128)S(1)} custom-call(s32[2]{0:T(128)S(1)} %copy-done.10, bf16[4,16,320]{2,1,0:T(8,128)(2,1)S(1)} %copy-done.6, bf16[12,16,320]{2,1,0:T(8,128)(2,1)S(1)} %copy-done.8, bf16[12,16,320]{2,1,0:T(8,128)(2,1)S(1)} %copy-done.9, s32[12]{0:T(128)S(1)} %copy-done.15), custom_call_target="tpu_custom_call" | custom-call | bytes 1024 | tf_op jit(solution)/shard_map/long_partial/pallas_call | solution.py:324
  20.0 0.1 collective-permute-start
  20.1 1.3 %collective-permute-done.other_ref = f32[64,384]{1,0:T(8,128)S(1)} collective-permute-done((f32[64,384]{1,0:T(8,128)S(1)}, f32[64,384]{1,0:T(8,128)S(1)}, u32[]{:S(2)}, u32[]{:S(2)}) %collective-permute-start) | collective-permute-done | bytes 98336 | tf_op jit(solution)/shard_map/ppermute | solution.py:315
  21.4 0.0 collective-permute-done.1.after_ref.refs_0_
  21.4 1.0 long_pair.1.refs_0_
  22.3 2.5 %collective-permute-start.4 = (f32[64,384]{1,0:T(8,128)S(1)}, f32[64,384]{1,0:T(8,128)S(1)}, u32[]{:S(2)}, u32[]{:S(2)}) collective-permute-start(f32[64,384]{1,0:T(8,128)S(1)} %long_pair.1.refs_0_), channel_id=1, source_target_pairs={{0,24},{4,28},{8,16},{12,20},{16,8},{20,12},{24,0},{28,4},{1,25},{... | collective-permute-start | bytes 294920 | tf_op jit(solution)/shard_map/ppermute | solution.py:315
  24.8 0.5 collective-permute-start.3
  25.3 0.5 collective-permute-start.2
  25.9 1.8 %copy-done.4 = bf16[3,4,320,320]{3,2,1,0:T(8,128)(2,1)S(1)} copy-done((bf16[3,4,320,320]{3,2,1,0:T(8,128)(2,1)S(1)}, bf16[3,4,320,320]{3,2,1,0:T(8,128)(2,1)}, u32[]{:S(2)}) %copy-start.4) | copy-done | bytes 2457624
  27.7 7.0 %short_attention.1.att_ref.refs_3_ = bf16[4,320,320]{2,1,0:T(8,128)(2,1)S(1)} custom-call(s32[2]{0:T(128)S(1)} %copy-done.10, bf16[3,4,320,320]{3,2,1,0:T(8,128)(2,1)S(1)} %copy-done.4, bf16[320,16,320]{2,1,0:T(8,128)(2,1)} %k_ref.3, bf16[320,16,320]{2,1,0:T(8,128)(2,1)} %v_ref.3, s32[320]{0:T(512)S(1)} %copy-done.14, f32[64,384]{1,0:T(8,128)S(1)} %long_pair.1.refs_0_), custom_call_target="tpu_custom_call" | custom-call | bytes 1024 | tf_op jit(solution)/shard_map/short_attention/pallas_call | solution.py:324
  34.7 0.0 copy-start
  34.7 0.0 copy-start.1
  34.7 0.0 copy-start.2
  34.7 0.0 copy-start.3
  34.7 0.0 copy-start.5
  34.7 0.0 copy-start.13
  34.8 0.0 collective-permute-done.8.refs_1_
  34.8 0.6 stack_weights.1.refs_7_
  35.4 1.6 %collective-permute-start.13 = (bf16[9,80,640]{2,1,0:T(8,128)(2,1)S(1)}, bf16[9,80,640]{2,1,0:T(8,128)(2,1)S(1)}, u32[]{:S(2)}, u32[]{:S(2)}) collective-permute-start(bf16[9,80,640]{2,1,0:T(8,128)(2,1)S(1)} %stack_weights.1.refs_7_), channel_id=1, source_target_pairs={{0,16},{4,20},{8,24},{12,28},{16,0},{20,4},{24,8},{28,12},{1,17},{... | collective-permute-start | bytes 2764808 | tf_op jit(solution)/shard_map/ppermute | solution.py:315
  37.0 1.5 %collective-permute-start.11 = (bf16[9,80,640]{2,1,0:T(8,128)(2,1)S(1)}, bf16[9,80,640]{2,1,0:T(8,128)(2,1)S(1)}, u32[]{:S(2)}, u32[]{:S(2)}) collective-permute-start(bf16[9,80,640]{2,1,0:T(8,128)(2,1)S(1)} %stack_weights.1.refs_7_), channel_id=1, source_target_pairs={{0,8},{4,12},{8,0},{12,4},{16,24},{20,28},{24,16},{28,20},{1,9},{5... | collective-permute-start | bytes 2764808 | tf_op jit(solution)/shard_map/ppermute | solution.py:315
  38.5 2.1 %send_attended.1 = (bf16[168,640]{1,0:T(8,128)(2,1)S(1)}, bf16[168,640]{1,0:T(8,128)(2,1)S(1)}, bf16[168,640]{1,0:T(8,128)(2,1)S(1)}, bf16[168,640]{1,0:T(8,128)(2,1)S(1)}) custom-call(s32[2]{0:T(128)S(1)} %copy-done.10, bf16[4,320,320]{2,1,0:T(8,128)(2,1)S(1)} %short_attention.1.att_ref.refs_3_, bf16[4,16,320]{2,1,0:T(8,128)(2,1)S(1)} %copy-done.7, ...), custom_call_target="tpu_custom_call" | custom-call | bytes 1024 | tf_op jit(solution)/shard_map/send_attended/pallas_call | solution.py:324
  40.7 0.7 collective-permute-start.5
  41.3 2.4 %collective-permute-start.6 = (bf16[168,640]{1,0:T(8,128)(2,1)S(1)}, bf16[168,640]{1,0:T(8,128)(2,1)S(1)}, u32[]{:S(2)}, u32[]{:S(2)}) collective-permute-start(bf16[168,640]{1,0:T(8,128)(2,1)S(1)} %get-tuple-element.24), channel_id=1, source_target_pairs={{0,2},{1,3},{2,0},{3,1},{4,6},{5,7},{6,4},{7,5},{8,10},{9,11},{10,... | collective-permute-start | bytes 645128 | tf_op jit(solution)/shard_map/ppermute | solution.py:315
  43.8 0.4 collective-permute-start.7
  44.2 4.7 %collective-permute-done.5.refs_0_.refs_1_ = bf16[168,640]{1,0:T(8,128)(2,1)S(1)} collective-permute-done((bf16[168,640]{1,0:T(8,128)(2,1)S(1)}, bf16[168,640]{1,0:T(8,128)(2,1)S(1)}, u32[]{:S(2)}, u32[]{:S(2)}) %collective-permute-start.5) | collective-permute-done | bytes 215072 | tf_op jit(solution)/shard_map/ppermute | solution.py:315
  49.0 9.1 %collective-permute-done.6.refs_1_.refs_2_ = bf16[168,640]{1,0:T(8,128)(2,1)S(1)} collective-permute-done((bf16[168,640]{1,0:T(8,128)(2,1)S(1)}, bf16[168,640]{1,0:T(8,128)(2,1)S(1)}, u32[]{:S(2)}, u32[]{:S(2)}) %collective-permute-start.6) | collective-permute-done | bytes 215072 | tf_op jit(solution)/shard_map/ppermute | solution.py:315
  58.0 3.7 %collective-permute-done.7.refs_2_.refs_3_ = bf16[168,640]{1,0:T(8,128)(2,1)S(1)} collective-permute-done((bf16[168,640]{1,0:T(8,128)(2,1)S(1)}, bf16[168,640]{1,0:T(8,128)(2,1)S(1)}, u32[]{:S(2)}, u32[]{:S(2)}) %collective-permute-start.7) | collective-permute-done | bytes 215072 | tf_op jit(solution)/shard_map/ppermute | solution.py:315
  61.8 0.6 cut_weights.1
  62.4 0.6 collective-permute-start.15
  63.0 0.5 collective-permute-start.14
  63.5 0.5 collective-permute-start.17
  64.0 9.5 %collective-permute-done.15.refs_13_ = bf16[5,80,640]{2,1,0:T(8,128)(2,1)S(1)} collective-permute-done((bf16[5,80,640]{2,1,0:T(8,128)(2,1)S(1)}, bf16[5,80,640]{2,1,0:T(8,128)(2,1)S(1)}, u32[]{:S(2)}, u32[]{:S(2)}) %collective-permute-start.15) | collective-permute-done | bytes 512032 | tf_op jit(solution)/shard_map/ppermute | solution.py:315
  73.5 1.9 %collective-permute-done.17.refs_15_ = bf16[4,80,640]{2,1,0:T(8,128)(2,1)S(1)} collective-permute-done((bf16[4,80,640]{2,1,0:T(8,128)(2,1)S(1)}, bf16[4,80,640]{2,1,0:T(8,128)(2,1)S(1)}, u32[]{:S(2)}, u32[]{:S(2)}) %collective-permute-start.17) | collective-permute-done | bytes 409632 | tf_op jit(solution)/shard_map/ppermute | solution.py:315
  75.4 1.7 %collective-permute-done.18.refs_16_ = bf16[4,80,640]{2,1,0:T(8,128)(2,1)S(1)} collective-permute-done((bf16[4,80,640]{2,1,0:T(8,128)(2,1)S(1)}, bf16[4,80,640]{2,1,0:T(8,128)(2,1)S(1)}, u32[]{:S(2)}, u32[]{:S(2)}) %collective-permute-start.18) | collective-permute-done | bytes 409632 | tf_op jit(solution)/shard_map/ppermute | solution.py:315
  77.2 6.5 %feed_forward.1 = (bf16[168,640]{1,0:T(8,128)(2,1)S(1)}, bf16[168,640]{1,0:T(8,128)(2,1)S(1)}, bf16[168,640]{1,0:T(8,128)(2,1)S(1)}, bf16[168,640]{1,0:T(8,128)(2,1)S(1)}) custom-call(s32[2]{0:T(128)S(1)} %copy-done.10, bf16[4,320,1280]{2,1,0:T(8,128)(2,1)S(1)} %copy-done, bf16[12,4,1280]{2,1,0:T(4,128)(2,1)S(1)} %bitcast.11, f32[1280]{0:T(1024)S(1)} %copy-done.13, ...), custom_call_target="tpu_custom_call" | custom-call | flops 3303014400 | bytes 1024 | tf_op jit(solution)/shard_map/feed_forward/pallas_call | solution.py:324
  83.7 0.1 collective-permute-start.19
  83.8 3.1 %collective-permute-start.20 = (bf16[168,640]{1,0:T(8,128)(2,1)S(1)}, bf16[168,640]{1,0:T(8,128)(2,1)S(1)}, u32[]{:S(2)}, u32[]{:S(2)}) collective-permute-start(bf16[168,640]{1,0:T(8,128)(2,1)S(1)} %get-tuple-element.30), channel_id=1, source_target_pairs={{0,2},{1,3},{2,0},{3,1},{4,6},{5,7},{6,4},{7,5},{8,10},{9,11},{10,... | collective-permute-start | bytes 645128 | tf_op jit(solution)/shard_map/ppermute | solution.py:315
  86.8 0.4 collective-permute-start.21
  87.2 5.7 %collective-permute-done.19.refs_1_ = bf16[168,640]{1,0:T(8,128)(2,1)S(1)} collective-permute-done((bf16[168,640]{1,0:T(8,128)(2,1)S(1)}, bf16[168,640]{1,0:T(8,128)(2,1)S(1)}, u32[]{:S(2)}, u32[]{:S(2)}) %collective-permute-start.19) | collective-permute-done | bytes 215072 | tf_op jit(solution)/shard_map/ppermute | solution.py:315
  92.9 8.8 %collective-permute-done.20.refs_2_ = bf16[168,640]{1,0:T(8,128)(2,1)S(1)} collective-permute-done((bf16[168,640]{1,0:T(8,128)(2,1)S(1)}, bf16[168,640]{1,0:T(8,128)(2,1)S(1)}, u32[]{:S(2)}, u32[]{:S(2)}) %collective-permute-start.20) | collective-permute-done | bytes 215072 | tf_op jit(solution)/shard_map/ppermute | solution.py:315
  101.7 4.4 %collective-permute-done.21.refs_3_ = bf16[168,640]{1,0:T(8,128)(2,1)S(1)} collective-permute-done((bf16[168,640]{1,0:T(8,128)(2,1)S(1)}, bf16[168,640]{1,0:T(8,128)(2,1)S(1)}, u32[]{:S(2)}, u32[]{:S(2)}) %collective-permute-start.21) | collective-permute-done | bytes 215072 | tf_op jit(solution)/shard_map/ppermute | solution.py:315
  106.2 1.7 %place_outputs.1 = (bf16[4,320,320]{2,1,0:T(8,128)(2,1)}, bf16[12,4,320]{2,1,0:T(4,128)(2,1)}) custom-call(s32[2]{0:T(128)S(1)} %copy-done.10, bf16[168,640]{1,0:T(8,128)(2,1)S(1)} %get-tuple-element.28.refs_0_, bf16[168,640]{1,0:T(8,128)(2,1)S(1)} %collective-permute-done.19.refs_1_, bf16[168,640]{1,0:T(8,128)(2,1)S(1)} %collective-permute-done.20.refs_2_, ...), custom_call_target="tpu_custom_call" | custom-call | bytes 1024 | tf_op jit(solution)/shard_map/place_outputs/pallas_call | solution.py:324
  (39 shorter events, 0.1 us)
Async XLA Ops:
  1.3 16.8 %copy-start.8 = (bf16[12,16,320]{2,1,0:T(8,128)(2,1)S(1)}, bf16[12,16,320]{2,1,0:T(8,128)(2,1)}, u32[]{:S(2)}) copy-start(bf16[12,16,320]{2,1,0:T(8,128)(2,1)} %k_ref.2) | copy-start | bytes 368644
  1.3 16.8 %copy-start.9 = (bf16[12,16,320]{2,1,0:T(8,128)(2,1)S(1)}, bf16[12,16,320]{2,1,0:T(8,128)(2,1)}, u32[]{:S(2)}) copy-start(bf16[12,16,320]{2,1,0:T(8,128)(2,1)} %v_ref.2) | copy-start | bytes 368644
  1.3 16.8 %copy-start.10 = (s32[2]{0:T(128)S(1)}, s32[2]{0:T(128)}, u32[]{:S(2)}) copy-start(s32[2]{0:T(128)} %pad_add_fusion.at_ref) | copy-start | bytes 28
  1.3 16.8 %copy-start.15 = (s32[12]{0:T(128)S(1)}, s32[12]{0:T(128)}, u32[]{:S(2)}) copy-start(s32[12]{0:T(128)} %len_ref.2) | copy-start | bytes 148
  3.8 22.0 %copy-start.14 = (s32[320]{0:T(512)S(1)}, s32[320]{0:T(512)}, u32[]{:S(2)}) copy-start(s32[320]{0:T(512)} %len_ref.3) | copy-start | bytes 3844
  3.8 17.6 %collective-permute-start.1 = (bf16[3,80,640]{2,1,0:T(8,128)(2,1)}, bf16[3,80,640]{2,1,0:T(8,128)(2,1)S(1)}, u32[]{:S(2)}, u32[]{:S(2)}) collective-permute-start(bf16[3,80,640]{2,1,0:T(8,128)(2,1)} %pack_weights.1), channel_id=1, source_target_pairs={{0,1},{1,0},{2,3},{3,2},{4,5},{5,4},{6,7},{7,6},{8,9},{9,8},{10,11... | collective-permute-start | bytes 921608 | tf_op jit(solution)/shard_map/ppermute | solution.py:315
  3.8 30.9 %collective-permute-start.9 = (bf16[3,80,640]{2,1,0:T(8,128)(2,1)}, bf16[3,80,640]{2,1,0:T(8,128)(2,1)S(1)}, u32[]{:S(2)}, u32[]{:S(2)}) collective-permute-start(bf16[3,80,640]{2,1,0:T(8,128)(2,1)} %pack_weights.1), channel_id=1, source_target_pairs={{0,3},{1,2},{2,1},{3,0},{4,7},{5,6},{6,5},{7,4},{8,11},{9,10},{10,... | collective-permute-start | bytes 921608 | tf_op jit(solution)/shard_map/ppermute | solution.py:315
  7.0 27.8 %collective-permute-start.8 = (bf16[3,80,640]{2,1,0:T(8,128)(2,1)}, bf16[3,80,640]{2,1,0:T(8,128)(2,1)S(1)}, u32[]{:S(2)}, u32[]{:S(2)}) collective-permute-start(bf16[3,80,640]{2,1,0:T(8,128)(2,1)} %pack_weights.1), channel_id=1, source_target_pairs={{0,2},{1,3},{2,0},{3,1},{4,6},{5,7},{6,4},{7,5},{8,10},{9,11},{10,... | collective-permute-start | bytes 921608 | tf_op jit(solution)/shard_map/ppermute | solution.py:315
  18.1 0.8 copy-start.6
  20.0 1.4 %collective-permute-start = (f32[64,384]{1,0:T(8,128)S(1)}, f32[64,384]{1,0:T(8,128)S(1)}, u32[]{:S(2)}, u32[]{:S(2)}) collective-permute-start(f32[64,384]{1,0:T(8,128)S(1)} %long_partial.1.mine_ref), channel_id=1, source_target_pairs={{0,4},{4,0},{8,12},{12,8},{16,20},{20,16},{24,28},{28,24},{1,5},{5... | collective-permute-start | bytes 294920 | tf_op jit(solution)/shard_map/ppermute | solution.py:315
  22.3 12.4 %collective-permute-start.4 = (f32[64,384]{1,0:T(8,128)S(1)}, f32[64,384]{1,0:T(8,128)S(1)}, u32[]{:S(2)}, u32[]{:S(2)}) collective-permute-start(f32[64,384]{1,0:T(8,128)S(1)} %long_pair.1.refs_0_), channel_id=1, source_target_pairs={{0,24},{4,28},{8,16},{12,20},{16,8},{20,12},{24,0},{28,4},{1,25},{... | collective-permute-start | bytes 294920 | tf_op jit(solution)/shard_map/ppermute | solution.py:315
  24.8 10.0 %collective-permute-start.3 = (f32[64,384]{1,0:T(8,128)S(1)}, f32[64,384]{1,0:T(8,128)S(1)}, u32[]{:S(2)}, u32[]{:S(2)}) collective-permute-start(f32[64,384]{1,0:T(8,128)S(1)} %long_pair.1.refs_0_), channel_id=1, source_target_pairs={{0,16},{4,20},{8,24},{12,28},{16,0},{20,4},{24,8},{28,12},{1,17},{... | collective-permute-start | bytes 294920 | tf_op jit(solution)/shard_map/ppermute | solution.py:315
  25.3 9.5 %collective-permute-start.2 = (f32[64,384]{1,0:T(8,128)S(1)}, f32[64,384]{1,0:T(8,128)S(1)}, u32[]{:S(2)}, u32[]{:S(2)}) collective-permute-start(f32[64,384]{1,0:T(8,128)S(1)} %long_pair.1.refs_0_), channel_id=1, source_target_pairs={{0,8},{4,12},{8,0},{12,4},{16,24},{20,28},{24,16},{28,20},{1,9},{5... | collective-permute-start | bytes 294920 | tf_op jit(solution)/shard_map/ppermute | solution.py:315
  25.8 1.8 %copy-start.4 = (bf16[3,4,320,320]{3,2,1,0:T(8,128)(2,1)S(1)}, bf16[3,4,320,320]{3,2,1,0:T(8,128)(2,1)}, u32[]{:S(2)}) copy-start(bf16[3,4,320,320]{3,2,1,0:T(8,128)(2,1)} %get-tuple-element.18.fresh_ref) | copy-start | bytes 7372804
  27.7 10.8 %copy-start.7 = (bf16[4,16,320]{2,1,0:T(8,128)(2,1)S(1)}, bf16[4,16,320]{2,1,0:T(8,128)(2,1)}, u32[]{:S(2)}) copy-start(bf16[4,16,320]{2,1,0:T(8,128)(2,1)} %get-tuple-element.19.q_ref.ql_ref) | copy-start | bytes 122884
  27.7 10.8 %copy-start.11 = (bf16[4,16,320]{2,1,0:T(8,128)(2,1)S(1)}, bf16[4,16,320]{2,1,0:T(8,128)(2,1)}, u32[]{:S(2)}) copy-start(bf16[4,16,320]{2,1,0:T(8,128)(2,1)} %get-tuple-element.20.knl_ref) | copy-start | bytes 122884
  27.7 10.8 %copy-start.12 = (bf16[4,16,320]{2,1,0:T(8,128)(2,1)S(1)}, bf16[4,16,320]{2,1,0:T(8,128)(2,1)}, u32[]{:S(2)}) copy-start(bf16[4,16,320]{2,1,0:T(8,128)(2,1)} %get-tuple-element.21.vnl_ref) | copy-start | bytes 122884
  34.7 42.4 %copy-start = (bf16[4,320,1280]{2,1,0:T(8,128)(2,1)S(1)}, bf16[4,320,1280]{2,1,0:T(8,128)(2,1)}, u32[]{:S(2)}) copy-start(bf16[4,320,1280]{2,1,0:T(8,128)(2,1)} %x_ref.3) | copy-start | bytes 9830404
  34.7 42.4 %copy-start.1 = (bf16[320,1280]{1,0:T(8,128)(2,1)S(1)}, bf16[320,1280]{1,0:T(8,128)(2,1)}, u32[]{:S(2)}) copy-start(bf16[320,1280]{1,0:T(8,128)(2,1)} %refs_4_.1) | copy-start | bytes 2457604
  34.7 42.4 %copy-start.2 = (bf16[1280,320]{0,1:T(8,128)(2,1)S(1)}, bf16[1280,320]{0,1:T(8,128)(2,1)}, u32[]{:S(2)}) copy-start(bf16[1280,320]{0,1:T(8,128)(2,1)} %param.32) | copy-start | bytes 2457604
  34.7 42.4 %copy-start.3 = (bf16[320,1280]{1,0:T(8,128)(2,1)S(1)}, bf16[320,1280]{1,0:T(8,128)(2,1)}, u32[]{:S(2)}) copy-start(bf16[320,1280]{1,0:T(8,128)(2,1)} %refs_6_.1) | copy-start | bytes 2457604
  34.7 42.4 %copy-start.5 = (bf16[4,12,1280]{2,0,1:T(4,128)(2,1)S(1)}, bf16[4,12,1280]{2,0,1:T(4,128)(2,1)}, u32[]{:S(2)}) copy-start(bf16[4,12,1280]{2,0,1:T(4,128)(2,1)} %param.18) | copy-start | bytes 368644
  34.7 42.4 %copy-start.13 = (f32[1280]{0:T(1024)S(1)}, f32[1280]{0:T(1024)}, u32[]{:S(2)}) copy-start(f32[1280]{0:T(1024)} %gain_ref.3) | copy-start | bytes 15364
  35.4 26.3 %collective-permute-start.13 = (bf16[9,80,640]{2,1,0:T(8,128)(2,1)S(1)}, bf16[9,80,640]{2,1,0:T(8,128)(2,1)S(1)}, u32[]{:S(2)}, u32[]{:S(2)}) collective-permute-start(bf16[9,80,640]{2,1,0:T(8,128)(2,1)S(1)} %stack_weights.1.refs_7_), channel_id=1, source_target_pairs={{0,16},{4,20},{8,24},{12,28},{16,0},{20,4},{24,8},{28,12},{1,17},{... | collective-permute-start | bytes 2764808 | tf_op jit(solution)/shard_map/ppermute | solution.py:315
  37.0 24.7 %collective-permute-start.11 = (bf16[9,80,640]{2,1,0:T(8,128)(2,1)S(1)}, bf16[9,80,640]{2,1,0:T(8,128)(2,1)S(1)}, u32[]{:S(2)}, u32[]{:S(2)}) collective-permute-start(bf16[9,80,640]{2,1,0:T(8,128)(2,1)S(1)} %stack_weights.1.refs_7_), channel_id=1, source_target_pairs={{0,8},{4,12},{8,0},{12,4},{16,24},{20,28},{24,16},{28,20},{1,9},{5... | collective-permute-start | bytes 2764808 | tf_op jit(solution)/shard_map/ppermute | solution.py:315
  40.7 8.3 %collective-permute-start.5 = (bf16[168,640]{1,0:T(8,128)(2,1)S(1)}, bf16[168,640]{1,0:T(8,128)(2,1)S(1)}, u32[]{:S(2)}, u32[]{:S(2)}) collective-permute-start(bf16[168,640]{1,0:T(8,128)(2,1)S(1)} %get-tuple-element.23), channel_id=1, source_target_pairs={{0,1},{1,0},{2,3},{3,2},{4,5},{5,4},{6,7},{7,6},{8,9},{9,8},{10,11... | collective-permute-start | bytes 645128 | tf_op jit(solution)/shard_map/ppermute | solution.py:315
  41.3 16.7 %collective-permute-start.6 = (bf16[168,640]{1,0:T(8,128)(2,1)S(1)}, bf16[168,640]{1,0:T(8,128)(2,1)S(1)}, u32[]{:S(2)}, u32[]{:S(2)}) collective-permute-start(bf16[168,640]{1,0:T(8,128)(2,1)S(1)} %get-tuple-element.24), channel_id=1, source_target_pairs={{0,2},{1,3},{2,0},{3,1},{4,6},{5,7},{6,4},{7,5},{8,10},{9,11},{10,... | collective-permute-start | bytes 645128 | tf_op jit(solution)/shard_map/ppermute | solution.py:315
  43.8 18.0 %collective-permute-start.7 = (bf16[168,640]{1,0:T(8,128)(2,1)S(1)}, bf16[168,640]{1,0:T(8,128)(2,1)S(1)}, u32[]{:S(2)}, u32[]{:S(2)}) collective-permute-start(bf16[168,640]{1,0:T(8,128)(2,1)S(1)} %get-tuple-element.25), channel_id=1, source_target_pairs={{0,3},{1,2},{2,1},{3,0},{4,7},{5,6},{6,5},{7,4},{8,11},{9,10},{10,... | collective-permute-start | bytes 645128 | tf_op jit(solution)/shard_map/ppermute | solution.py:315
  62.4 11.1 %collective-permute-start.15 = (bf16[5,80,640]{2,1,0:T(8,128)(2,1)S(1)}, bf16[5,80,640]{2,1,0:T(8,128)(2,1)S(1)}, u32[]{:S(2)}, u32[]{:S(2)}) collective-permute-start(bf16[5,80,640]{2,1,0:T(8,128)(2,1)S(1)} %get-tuple-element.26), channel_id=1, source_target_pairs={{0,8},{4,12},{8,0},{12,4},{16,24},{20,28},{24,16},{28,20},{1,9},{5... | collective-permute-start | bytes 1536008 | tf_op jit(solution)/shard_map/ppermute | solution.py:315
  63.0 12.4 %collective-permute-start.10 = (bf16[9,80,640]{2,1,0:T(8,128)(2,1)S(1)}, bf16[9,80,640]{2,1,0:T(8,128)(2,1)S(1)}, u32[]{:S(2)}, u32[]{:S(2)}) collective-permute-start(bf16[9,80,640]{2,1,0:T(8,128)(2,1)S(1)} %stack_weights.1.refs_7_), channel_id=1, source_target_pairs={{0,4},{4,0},{8,12},{12,8},{16,20},{20,16},{24,28},{28,24},{1,5},{5... | collective-permute-start | bytes 2764808 | tf_op jit(solution)/shard_map/ppermute | solution.py:315
  63.0 14.1 %collective-permute-start.14 = (bf16[9,80,640]{2,1,0:T(8,128)(2,1)S(1)}, bf16[9,80,640]{2,1,0:T(8,128)(2,1)S(1)}, u32[]{:S(2)}, u32[]{:S(2)}) collective-permute-start(bf16[9,80,640]{2,1,0:T(8,128)(2,1)S(1)} %collective-permute-done.13.y_ref.refs_11_), channel_id=1, source_target_pairs={{0,4},{4,0},{8,12},{12,8},{16,20},{20,16},{24,28},{28,24},{1,5},{5... | collective-permute-start | bytes 2764808 | tf_op jit(solution)/shard_map/ppermute | solution.py:315
  63.5 13.6 %collective-permute-start.12 = (bf16[9,80,640]{2,1,0:T(8,128)(2,1)S(1)}, bf16[9,80,640]{2,1,0:T(8,128)(2,1)S(1)}, u32[]{:S(2)}, u32[]{:S(2)}) collective-permute-start(bf16[9,80,640]{2,1,0:T(8,128)(2,1)S(1)} %collective-permute-done.11.x_ref.refs_9_), channel_id=1, source_target_pairs={{0,4},{4,0},{8,12},{12,8},{16,20},{20,16},{24,28},{28,24},{1,5},{5... | collective-permute-start | bytes 2764808 | tf_op jit(solution)/shard_map/ppermute | solution.py:315
  63.5 11.9 %collective-permute-start.17 = (bf16[4,80,640]{2,1,0:T(8,128)(2,1)S(1)}, bf16[4,80,640]{2,1,0:T(8,128)(2,1)S(1)}, u32[]{:S(2)}, u32[]{:S(2)}) collective-permute-start(bf16[4,80,640]{2,1,0:T(8,128)(2,1)S(1)} %get-tuple-element.27), channel_id=1, source_target_pairs={{0,16},{4,20},{8,24},{12,28},{16,0},{20,4},{24,8},{28,12},{1,17},{... | collective-permute-start | bytes 1228808 | tf_op jit(solution)/shard_map/ppermute | solution.py:315
  73.5 3.6 %collective-permute-start.16 = (bf16[5,80,640]{2,1,0:T(8,128)(2,1)S(1)}, bf16[5,80,640]{2,1,0:T(8,128)(2,1)S(1)}, u32[]{:S(2)}, u32[]{:S(2)}) collective-permute-start(bf16[5,80,640]{2,1,0:T(8,128)(2,1)S(1)} %collective-permute-done.15.refs_13_), channel_id=1, source_target_pairs={{0,4},{4,0},{8,12},{12,8},{16,20},{20,16},{24,28},{28,24},{1,5},{5... | collective-permute-start | bytes 1536008 | tf_op jit(solution)/shard_map/ppermute | solution.py:315
  75.4 1.7 %collective-permute-start.18 = (bf16[4,80,640]{2,1,0:T(8,128)(2,1)S(1)}, bf16[4,80,640]{2,1,0:T(8,128)(2,1)S(1)}, u32[]{:S(2)}, u32[]{:S(2)}) collective-permute-start(bf16[4,80,640]{2,1,0:T(8,128)(2,1)S(1)} %collective-permute-done.17.refs_15_), channel_id=1, source_target_pairs={{0,4},{4,0},{8,12},{12,8},{16,20},{20,16},{24,28},{28,24},{1,5},{5... | collective-permute-start | bytes 1228808 | tf_op jit(solution)/shard_map/ppermute | solution.py:315
  83.7 9.2 %collective-permute-start.19 = (bf16[168,640]{1,0:T(8,128)(2,1)S(1)}, bf16[168,640]{1,0:T(8,128)(2,1)S(1)}, u32[]{:S(2)}, u32[]{:S(2)}) collective-permute-start(bf16[168,640]{1,0:T(8,128)(2,1)S(1)} %get-tuple-element.29), channel_id=1, source_target_pairs={{0,1},{1,0},{2,3},{3,2},{4,5},{5,4},{6,7},{7,6},{8,9},{9,8},{10,11... | collective-permute-start | bytes 645128 | tf_op jit(solution)/shard_map/ppermute | solution.py:315
  83.8 18.0 %collective-permute-start.20 = (bf16[168,640]{1,0:T(8,128)(2,1)S(1)}, bf16[168,640]{1,0:T(8,128)(2,1)S(1)}, u32[]{:S(2)}, u32[]{:S(2)}) collective-permute-start(bf16[168,640]{1,0:T(8,128)(2,1)S(1)} %get-tuple-element.30), channel_id=1, source_target_pairs={{0,2},{1,3},{2,0},{3,1},{4,6},{5,7},{6,4},{7,5},{8,10},{9,11},{10,... | collective-permute-start | bytes 645128 | tf_op jit(solution)/shard_map/ppermute | solution.py:315
  86.8 19.3 %collective-permute-start.21 = (bf16[168,640]{1,0:T(8,128)(2,1)S(1)}, bf16[168,640]{1,0:T(8,128)(2,1)S(1)}, u32[]{:S(2)}, u32[]{:S(2)}) collective-permute-start(bf16[168,640]{1,0:T(8,128)(2,1)S(1)} %get-tuple-element.31), channel_id=1, source_target_pairs={{0,3},{1,2},{2,1},{3,0},{4,7},{5,6},{6,5},{7,4},{8,11},{9,10},{10,... | collective-permute-start | bytes 645128 | tf_op jit(solution)/shard_map/ppermute | solution.py:315

commit v6 on v5

--- a/solution.py
+++ b/solution.py
@@ -225,7 +225,7 @@
         rows = att_ref[at_ref[1] ^ k]
         mine = long_ref[at_ref[1] ^ k]
         outs[k][:half, :] = jnp.concatenate([rows[:half], rows[half:]], axis=1)
-        outs[k][half:, :] = jnp.concatenate([mine[: GROUP // 2], mine[GROUP // 2 :]], axis=1).astype(BF16)
+        outs[k][half:, :] = jnp.concatenate([mine, jnp.zeros_like(mine)], axis=1).astype(BF16)
 
 
 def pack_kernel(at_ref, o_ref, up_ref, down_ref, out_ref):
@@ -272,9 +272,7 @@
     x = jnp.concatenate([x_ref[0].astype(F32), xs_ref[...]], axis=0)
 
     def rows_of(piece):
-        tail = piece[half:].astype(F32)
-        tail = jnp.concatenate([tail[:, :width], tail[:, width:]], axis=0).astype(BF16)
-        return jnp.concatenate([piece[:half, :width], piece[:half, width:], tail], axis=0)
+        return jnp.concatenate([piece[:half, :width], piece[:half, width:], piece[half:, :width]], axis=0)
 
     attended = jnp.concatenate([rows_of(piece[...]) for piece in atts], axis=1)
     for copy in copies:
@@ -289,7 +287,7 @@
         cols = narrow[:, b * width : (b + 1) * width]
         cols_ref[b, :half, :] = jnp.concatenate([cols[:half], cols[half:]], axis=1)
         tail = out[2 * half :, b * width : (b + 1) * width]
-        cols_ref[b, half:, :] = jnp.concatenate([tail[: GROUP // 2], tail[GROUP // 2 :]], axis=1).astype(BF16)
+        cols_ref[b, half:, :] = jnp.concatenate([tail, jnp.zeros_like(tail)], axis=1).astype(BF16)
     for k in range(tp):
         outs[k][...] = cols_ref[at_ref[1] ^ k]
 
@@ -304,8 +302,7 @@
         step = at_ref[1] ^ k
         short_ref[step, :half, :] = pieces[k][:half, :width]
         short_ref[step, half:, :] = pieces[k][:half, width:]
-        tail = pieces[k][half:, :].astype(F32)
-        tail = jnp.concatenate([tail[:, :width], tail[:, width:]], axis=0)[:count]
+        tail = pieces[k][half:, :width].astype(F32)[:count]
         longs = jnp.where(at == step, tail[:, None, :], longs)
     long_ref[...] = longs.astype(BF16)
 
@@ -414,7 +411,7 @@
     parts = [part] + [swap(part, "seq", 2 * i) for i in range(1, seq // 2)]
 
     block = count // 2
-    packed = shape((count // 2 + GROUP // 2, 2 * width), BF16)
+    packed = shape((count // 2 + GROUP, 2 * width), BF16)
     fresh_rows = pl.BlockSpec((steps, block, width), lambda i, at: (0, i, 0))
     cache_rows = pl.BlockSpec((block, slots, width), lambda i, at: (i, 0, 0))
     (att,) = call(

time: 108 us -> 110 us (1.019)
  waiting for transfers between devices: 50.9 us -> 52.6 us
    ppermute x22, waiting for transfers between devices: 50.9 us -> 52.6 us  [swap(): return lax.ppermute(value, axis, [(i, i ^ k) for i in range(size)])]
where the time goes in v6:
time: 110 us
  waiting for transfers between devices  52.6 us (48%)
  Pallas kernels  33 us (30%)
  starting transfers between devices  19.7 us (18%)
  local copies, waits for them, and re-layouts  2.69 us (2%)
    ppermute x22, waiting for transfers between devices, swap(): return lax.ppermute(value, axis, [(i, i ^ k) for i in range(size)])  52.6 us
    pallas_call x10, Pallas kernels, call(): pl.pallas_call(kernel, grid_spec=pltpu.PrefetchScalarGridSpec(num_scalar_...  33 us
    ppermute x22, starting transfers between devices, swap(): return lax.ppermute(value, axis, [(i, i ^ k) for i in range(size)])  19.7 us
    unnamed x32, local copies, waits for them, and re-layouts  2.69 us
  transfers between devices with their start and end apart: 22, of which 10 were waited for; matrix products, arithmetic and copies ran while one was open for 0% of the time, Pallas kernels for 19%

profile of v6, /device:TPU:8, one launch (start us, length us, event | category | flops | bytes accessed | tf_op | source)
XLA Modules:
  0.0 109.6 jit_solution(18071182255045952083)
XLA Ops:
  0.6 0.6 pad_add_fusion.at_ref
  1.3 2.5 %pack_weights.1 = bf16[3,80,640]{2,1,0:T(8,128)(2,1)} custom-call(s32[2]{0:T(128)} %pad_add_fusion.at_ref, bf16[320,1280]{1,0:T(8,128)(2,1)} %refs_4_.1, bf16[320,1280]{1,0:T(8,128)(2,1)} %bitcast.8, bf16[320,1280]{1,0:T(8,128)(2,1)} %refs_6_.1), custom_call_target="tpu_custom_call" | custom-call | bytes 1024 | tf_op jit(solution)/shard_map/pack_weights/pallas_call | solution.py:321
  3.8 0.0 collective-permute-start.1
  3.8 3.1 %collective-permute-start.9 = (bf16[3,80,640]{2,1,0:T(8,128)(2,1)}, bf16[3,80,640]{2,1,0:T(8,128)(2,1)S(1)}, u32[]{:S(2)}, u32[]{:S(2)}) collective-permute-start(bf16[3,80,640]{2,1,0:T(8,128)(2,1)} %pack_weights.1), channel_id=1, source_target_pairs={{0,3},{1,2},{2,1},{3,0},{4,7},{5,6},{6,5},{7,4},{8,11},{9,10},{10,... | collective-permute-start | bytes 921608 | tf_op jit(solution)/shard_map/ppermute | solution.py:312
  7.0 1.2 %collective-permute-start.8 = (bf16[3,80,640]{2,1,0:T(8,128)(2,1)}, bf16[3,80,640]{2,1,0:T(8,128)(2,1)S(1)}, u32[]{:S(2)}, u32[]{:S(2)}) collective-permute-start(bf16[3,80,640]{2,1,0:T(8,128)(2,1)} %pack_weights.1), channel_id=1, source_target_pairs={{0,2},{1,3},{2,0},{3,1},{4,6},{5,7},{6,4},{7,5},{8,10},{9,11},{10,... | collective-permute-start | bytes 921608 | tf_op jit(solution)/shard_map/ppermute | solution.py:312
  8.2 9.8 %qkv.1 = (bf16[3,4,320,320]{3,2,1,0:T(8,128)(2,1)}, bf16[4,16,320]{2,1,0:T(8,128)(2,1)}, bf16[4,16,320]{2,1,0:T(8,128)(2,1)}, bf16[4,16,320]{2,1,0:T(8,128)(2,1)}) custom-call(s32[2]{0:T(128)} %pad_add_fusion.at_ref, bf16[4,320,1280]{2,1,0:T(8,128)(2,1)} %x_ref.3, bf16[12,4,1280]{2,1,0:T(4,128)(2,1)} %bitcast.10, f32[1280]{0:T(1024)} %gain_ref.2, ...), custom_call_target="tpu_custom_call" | custom-call | bytes 1024 | tf_op jit(solution)/shard_map/qkv/pallas_call | solution.py:321
  18.1 0.8 copy-done.6
  18.9 1.1 %long_partial.1.mine_ref = f32[64,384]{1,0:T(8,128)S(1)} custom-call(s32[2]{0:T(128)S(1)} %copy-done.10, bf16[4,16,320]{2,1,0:T(8,128)(2,1)S(1)} %copy-done.6, bf16[12,16,320]{2,1,0:T(8,128)(2,1)S(1)} %copy-done.8, bf16[12,16,320]{2,1,0:T(8,128)(2,1)S(1)} %copy-done.9, s32[12]{0:T(128)S(1)} %copy-done.15), custom_call_target="tpu_custom_call" | custom-call | bytes 1024 | tf_op jit(solution)/shard_map/long_partial/pallas_call | solution.py:321
  20.0 0.1 collective-permute-start
  20.1 1.3 %collective-permute-done.other_ref = f32[64,384]{1,0:T(8,128)S(1)} collective-permute-done((f32[64,384]{1,0:T(8,128)S(1)}, f32[64,384]{1,0:T(8,128)S(1)}, u32[]{:S(2)}, u32[]{:S(2)}) %collective-permute-start) | collective-permute-done | bytes 98336 | tf_op jit(solution)/shard_map/ppermute | solution.py:312
  21.4 1.0 long_pair.1.refs_0_
  22.3 2.5 %collective-permute-start.4 = (f32[64,384]{1,0:T(8,128)S(1)}, f32[64,384]{1,0:T(8,128)S(1)}, u32[]{:S(2)}, u32[]{:S(2)}) collective-permute-start(f32[64,384]{1,0:T(8,128)S(1)} %long_pair.1.refs_0_), channel_id=1, source_target_pairs={{0,24},{4,28},{8,16},{12,20},{16,8},{20,12},{24,0},{28,4},{1,25},{... | collective-permute-start | bytes 294920 | tf_op jit(solution)/shard_map/ppermute | solution.py:312
  24.8 0.5 collective-permute-start.3
  25.3 0.5 collective-permute-start.2
  25.9 1.8 %copy-done.4 = bf16[3,4,320,320]{3,2,1,0:T(8,128)(2,1)S(1)} copy-done((bf16[3,4,320,320]{3,2,1,0:T(8,128)(2,1)S(1)}, bf16[3,4,320,320]{3,2,1,0:T(8,128)(2,1)}, u32[]{:S(2)}) %copy-start.4) | copy-done | bytes 2457624
  27.7 7.0 %short_attention.1.att_ref.refs_3_ = bf16[4,320,320]{2,1,0:T(8,128)(2,1)S(1)} custom-call(s32[2]{0:T(128)S(1)} %copy-done.10, bf16[3,4,320,320]{3,2,1,0:T(8,128)(2,1)S(1)} %copy-done.4, bf16[320,16,320]{2,1,0:T(8,128)(2,1)} %k_ref.3, bf16[320,16,320]{2,1,0:T(8,128)(2,1)} %v_ref.3, s32[320]{0:T(512)S(1)} %copy-done.14, f32[64,384]{1,0:T(8,128)S(1)} %long_pair.1.refs_0_), custom_call_target="tpu_custom_call" | custom-call | bytes 1024 | tf_op jit(solution)/shard_map/short_attention/pallas_call | solution.py:321
  34.7 0.0 copy-start
  34.7 0.0 copy-start.1
  34.7 0.0 copy-start.2
  34.7 0.0 copy-start.3
  34.7 0.0 copy-start.5
  34.7 0.0 copy-start.13
  34.8 0.0 collective-permute-done.9.refs_2_
  34.8 0.6 stack_weights.1.refs_7_
  35.4 1.6 %collective-permute-start.13 = (bf16[9,80,640]{2,1,0:T(8,128)(2,1)S(1)}, bf16[9,80,640]{2,1,0:T(8,128)(2,1)S(1)}, u32[]{:S(2)}, u32[]{:S(2)}) collective-permute-start(bf16[9,80,640]{2,1,0:T(8,128)(2,1)S(1)} %stack_weights.1.refs_7_), channel_id=1, source_target_pairs={{0,16},{4,20},{8,24},{12,28},{16,0},{20,4},{24,8},{28,12},{1,17},{... | collective-permute-start | bytes 2764808 | tf_op jit(solution)/shard_map/ppermute | solution.py:312
  37.0 1.5 %collective-permute-start.11 = (bf16[9,80,640]{2,1,0:T(8,128)(2,1)S(1)}, bf16[9,80,640]{2,1,0:T(8,128)(2,1)S(1)}, u32[]{:S(2)}, u32[]{:S(2)}) collective-permute-start(bf16[9,80,640]{2,1,0:T(8,128)(2,1)S(1)} %stack_weights.1.refs_7_), channel_id=1, source_target_pairs={{0,8},{4,12},{8,0},{12,4},{16,24},{20,28},{24,16},{28,20},{1,9},{5... | collective-permute-start | bytes 2764808 | tf_op jit(solution)/shard_map/ppermute | solution.py:312
  38.5 2.1 %send_attended.1 = (bf16[176,640]{1,0:T(8,128)(2,1)S(1)}, bf16[176,640]{1,0:T(8,128)(2,1)S(1)}, bf16[176,640]{1,0:T(8,128)(2,1)S(1)}, bf16[176,640]{1,0:T(8,128)(2,1)S(1)}) custom-call(s32[2]{0:T(128)S(1)} %copy-done.10, bf16[4,320,320]{2,1,0:T(8,128)(2,1)S(1)} %short_attention.1.att_ref.refs_3_, bf16[4,16,320]{2,1,0:T(8,128)(2,1)S(1)} %copy-done.7, ...), custom_call_target="tpu_custom_call" | custom-call | bytes 1024 | tf_op jit(solution)/shard_map/send_attended/pallas_call | solution.py:321
  40.6 0.7 collective-permute-start.5
  41.3 2.4 %collective-permute-start.6 = (bf16[176,640]{1,0:T(8,128)(2,1)S(1)}, bf16[176,640]{1,0:T(8,128)(2,1)S(1)}, u32[]{:S(2)}, u32[]{:S(2)}) collective-permute-start(bf16[176,640]{1,0:T(8,128)(2,1)S(1)} %get-tuple-element.24), channel_id=1, source_target_pairs={{0,2},{1,3},{2,0},{3,1},{4,6},{5,7},{6,4},{7,5},{8,10},{9,11},{10,... | collective-permute-start | bytes 675848 | tf_op jit(solution)/shard_map/ppermute | solution.py:312
  43.7 0.4 collective-permute-start.7
  44.2 5.0 %collective-permute-done.5.refs_0_.refs_1_ = bf16[176,640]{1,0:T(8,128)(2,1)S(1)} collective-permute-done((bf16[176,640]{1,0:T(8,128)(2,1)S(1)}, bf16[176,640]{1,0:T(8,128)(2,1)S(1)}, u32[]{:S(2)}, u32[]{:S(2)}) %collective-permute-start.5) | collective-permute-done | bytes 225312 | tf_op jit(solution)/shard_map/ppermute | solution.py:312
  49.1 9.6 %collective-permute-done.6.refs_1_.refs_2_ = bf16[176,640]{1,0:T(8,128)(2,1)S(1)} collective-permute-done((bf16[176,640]{1,0:T(8,128)(2,1)S(1)}, bf16[176,640]{1,0:T(8,128)(2,1)S(1)}, u32[]{:S(2)}, u32[]{:S(2)}) %collective-permute-start.6) | collective-permute-done | bytes 225312 | tf_op jit(solution)/shard_map/ppermute | solution.py:312
  58.7 3.8 %collective-permute-done.7.refs_2_.refs_3_ = bf16[176,640]{1,0:T(8,128)(2,1)S(1)} collective-permute-done((bf16[176,640]{1,0:T(8,128)(2,1)S(1)}, bf16[176,640]{1,0:T(8,128)(2,1)S(1)}, u32[]{:S(2)}, u32[]{:S(2)}) %collective-permute-start.7) | collective-permute-done | bytes 225312 | tf_op jit(solution)/shard_map/ppermute | solution.py:312
  62.6 0.6 cut_weights.1
  63.2 0.6 collective-permute-start.15
  63.8 0.5 collective-permute-start.14
  64.3 0.5 collective-permute-start.17
  64.8 9.4 %collective-permute-done.15.refs_13_ = bf16[5,80,640]{2,1,0:T(8,128)(2,1)S(1)} collective-permute-done((bf16[5,80,640]{2,1,0:T(8,128)(2,1)S(1)}, bf16[5,80,640]{2,1,0:T(8,128)(2,1)S(1)}, u32[]{:S(2)}, u32[]{:S(2)}) %collective-permute-start.15) | collective-permute-done | bytes 512032 | tf_op jit(solution)/shard_map/ppermute | solution.py:312
  74.2 2.0 %collective-permute-done.17.refs_15_ = bf16[4,80,640]{2,1,0:T(8,128)(2,1)S(1)} collective-permute-done((bf16[4,80,640]{2,1,0:T(8,128)(2,1)S(1)}, bf16[4,80,640]{2,1,0:T(8,128)(2,1)S(1)}, u32[]{:S(2)}, u32[]{:S(2)}) %collective-permute-start.17) | collective-permute-done | bytes 409632 | tf_op jit(solution)/shard_map/ppermute | solution.py:312
  76.2 1.7 %collective-permute-done.18.refs_16_ = bf16[4,80,640]{2,1,0:T(8,128)(2,1)S(1)} collective-permute-done((bf16[4,80,640]{2,1,0:T(8,128)(2,1)S(1)}, bf16[4,80,640]{2,1,0:T(8,128)(2,1)S(1)}, u32[]{:S(2)}, u32[]{:S(2)}) %collective-permute-start.18) | collective-permute-done | bytes 409632 | tf_op jit(solution)/shard_map/ppermute | solution.py:312
  78.0 6.5 %feed_forward.1 = (bf16[176,640]{1,0:T(8,128)(2,1)S(1)}, bf16[176,640]{1,0:T(8,128)(2,1)S(1)}, bf16[176,640]{1,0:T(8,128)(2,1)S(1)}, bf16[176,640]{1,0:T(8,128)(2,1)S(1)}) custom-call(s32[2]{0:T(128)S(1)} %copy-done.10, bf16[4,320,1280]{2,1,0:T(8,128)(2,1)S(1)} %copy-done, bf16[12,4,1280]{2,1,0:T(4,128)(2,1)S(1)} %bitcast.11, f32[1280]{0:T(1024)S(1)} %copy-done.13, ...), custom_call_target="tpu_custom_call" | custom-call | flops 3303014400 | bytes 1024 | tf_op jit(solution)/shard_map/feed_forward/pallas_call | solution.py:321
  84.5 0.1 collective-permute-start.19
  84.6 3.0 %collective-permute-start.20 = (bf16[176,640]{1,0:T(8,128)(2,1)S(1)}, bf16[176,640]{1,0:T(8,128)(2,1)S(1)}, u32[]{:S(2)}, u32[]{:S(2)}) collective-permute-start(bf16[176,640]{1,0:T(8,128)(2,1)S(1)} %get-tuple-element.30), channel_id=1, source_target_pairs={{0,2},{1,3},{2,0},{3,1},{4,6},{5,7},{6,4},{7,5},{8,10},{9,11},{10,... | collective-permute-start | bytes 675848 | tf_op jit(solution)/shard_map/ppermute | solution.py:312
  87.6 0.4 collective-permute-start.21
  88.1 6.1 %collective-permute-done.19.refs_1_ = bf16[176,640]{1,0:T(8,128)(2,1)S(1)} collective-permute-done((bf16[176,640]{1,0:T(8,128)(2,1)S(1)}, bf16[176,640]{1,0:T(8,128)(2,1)S(1)}, u32[]{:S(2)}, u32[]{:S(2)}) %collective-permute-start.19) | collective-permute-done | bytes 225312 | tf_op jit(solution)/shard_map/ppermute | solution.py:312
  94.2 9.0 %collective-permute-done.20.refs_2_ = bf16[176,640]{1,0:T(8,128)(2,1)S(1)} collective-permute-done((bf16[176,640]{1,0:T(8,128)(2,1)S(1)}, bf16[176,640]{1,0:T(8,128)(2,1)S(1)}, u32[]{:S(2)}, u32[]{:S(2)}) %collective-permute-start.20) | collective-permute-done | bytes 225312 | tf_op jit(solution)/shard_map/ppermute | solution.py:312
  103.2 4.7 %collective-permute-done.21.refs_3_ = bf16[176,640]{1,0:T(8,128)(2,1)S(1)} collective-permute-done((bf16[176,640]{1,0:T(8,128)(2,1)S(1)}, bf16[176,640]{1,0:T(8,128)(2,1)S(1)}, u32[]{:S(2)}, u32[]{:S(2)}) %collective-permute-start.21) | collective-permute-done | bytes 225312 | tf_op jit(solution)/shard_map/ppermute | solution.py:312
  107.9 1.7 %place_outputs.1 = (bf16[4,320,320]{2,1,0:T(8,128)(2,1)}, bf16[12,4,320]{2,1,0:T(4,128)(2,1)}) custom-call(s32[2]{0:T(128)S(1)} %copy-done.10, bf16[176,640]{1,0:T(8,128)(2,1)S(1)} %get-tuple-element.28.refs_0_, bf16[176,640]{1,0:T(8,128)(2,1)S(1)} %collective-permute-done.19.refs_1_, bf16[176,640]{1,0:T(8,128)(2,1)S(1)} %collective-permute-done.20.refs_2_, ...), custom_call_target="tpu_custom_call" | custom-call | bytes 1024 | tf_op jit(solution)/shard_map/place_outputs/pallas_call | solution.py:321
  (39 shorter events, 0.1 us)
Async XLA Ops:
  1.3 16.8 %copy-start.8 = (bf16[12,16,320]{2,1,0:T(8,128)(2,1)S(1)}, bf16[12,16,320]{2,1,0:T(8,128)(2,1)}, u32[]{:S(2)}) copy-start(bf16[12,16,320]{2,1,0:T(8,128)(2,1)} %k_ref.2) | copy-start | bytes 368644
  1.3 16.8 %copy-start.9 = (bf16[12,16,320]{2,1,0:T(8,128)(2,1)S(1)}, bf16[12,16,320]{2,1,0:T(8,128)(2,1)}, u32[]{:S(2)}) copy-start(bf16[12,16,320]{2,1,0:T(8,128)(2,1)} %v_ref.2) | copy-start | bytes 368644
  1.3 16.8 %copy-start.10 = (s32[2]{0:T(128)S(1)}, s32[2]{0:T(128)}, u32[]{:S(2)}) copy-start(s32[2]{0:T(128)} %pad_add_fusion.at_ref) | copy-start | bytes 28
  1.3 16.8 %copy-start.15 = (s32[12]{0:T(128)S(1)}, s32[12]{0:T(128)}, u32[]{:S(2)}) copy-start(s32[12]{0:T(128)} %len_ref.2) | copy-start | bytes 148
  3.8 22.0 %copy-start.14 = (s32[320]{0:T(512)S(1)}, s32[320]{0:T(512)}, u32[]{:S(2)}) copy-start(s32[320]{0:T(512)} %len_ref.3) | copy-start | bytes 3844
  3.8 17.6 %collective-permute-start.1 = (bf16[3,80,640]{2,1,0:T(8,128)(2,1)}, bf16[3,80,640]{2,1,0:T(8,128)(2,1)S(1)}, u32[]{:S(2)}, u32[]{:S(2)}) collective-permute-start(bf16[3,80,640]{2,1,0:T(8,128)(2,1)} %pack_weights.1), channel_id=1, source_target_pairs={{0,1},{1,0},{2,3},{3,2},{4,5},{5,4},{6,7},{7,6},{8,9},{9,8},{10,11... | collective-permute-start | bytes 921608 | tf_op jit(solution)/shard_map/ppermute | solution.py:312
  3.8 30.9 %collective-permute-start.9 = (bf16[3,80,640]{2,1,0:T(8,128)(2,1)}, bf16[3,80,640]{2,1,0:T(8,128)(2,1)S(1)}, u32[]{:S(2)}, u32[]{:S(2)}) collective-permute-start(bf16[3,80,640]{2,1,0:T(8,128)(2,1)} %pack_weights.1), channel_id=1, source_target_pairs={{0,3},{1,2},{2,1},{3,0},{4,7},{5,6},{6,5},{7,4},{8,11},{9,10},{10,... | collective-permute-start | bytes 921608 | tf_op jit(solution)/shard_map/ppermute | solution.py:312
  7.0 27.8 %collective-permute-start.8 = (bf16[3,80,640]{2,1,0:T(8,128)(2,1)}, bf16[3,80,640]{2,1,0:T(8,128)(2,1)S(1)}, u32[]{:S(2)}, u32[]{:S(2)}) collective-permute-start(bf16[3,80,640]{2,1,0:T(8,128)(2,1)} %pack_weights.1), channel_id=1, source_target_pairs={{0,2},{1,3},{2,0},{3,1},{4,6},{5,7},{6,4},{7,5},{8,10},{9,11},{10,... | collective-permute-start | bytes 921608 | tf_op jit(solution)/shard_map/ppermute | solution.py:312
  18.1 0.8 copy-start.6
  20.0 1.4 %collective-permute-start = (f32[64,384]{1,0:T(8,128)S(1)}, f32[64,384]{1,0:T(8,128)S(1)}, u32[]{:S(2)}, u32[]{:S(2)}) collective-permute-start(f32[64,384]{1,0:T(8,128)S(1)} %long_partial.1.mine_ref), channel_id=1, source_target_pairs={{0,4},{4,0},{8,12},{12,8},{16,20},{20,16},{24,28},{28,24},{1,5},{5... | collective-permute-start | bytes 294920 | tf_op jit(solution)/shard_map/ppermute | solution.py:312
  22.3 12.4 %collective-permute-start.4 = (f32[64,384]{1,0:T(8,128)S(1)}, f32[64,384]{1,0:T(8,128)S(1)}, u32[]{:S(2)}, u32[]{:S(2)}) collective-permute-start(f32[64,384]{1,0:T(8,128)S(1)} %long_pair.1.refs_0_), channel_id=1, source_target_pairs={{0,24},{4,28},{8,16},{12,20},{16,8},{20,12},{24,0},{28,4},{1,25},{... | collective-permute-start | bytes 294920 | tf_op jit(solution)/shard_map/ppermute | solution.py:312
  24.8 10.0 %collective-permute-start.3 = (f32[64,384]{1,0:T(8,128)S(1)}, f32[64,384]{1,0:T(8,128)S(1)}, u32[]{:S(2)}, u32[]{:S(2)}) collective-permute-start(f32[64,384]{1,0:T(8,128)S(1)} %long_pair.1.refs_0_), channel_id=1, source_target_pairs={{0,16},{4,20},{8,24},{12,28},{16,0},{20,4},{24,8},{28,12},{1,17},{... | collective-permute-start | bytes 294920 | tf_op jit(solution)/shard_map/ppermute | solution.py:312
  25.3 9.5 %collective-permute-start.2 = (f32[64,384]{1,0:T(8,128)S(1)}, f32[64,384]{1,0:T(8,128)S(1)}, u32[]{:S(2)}, u32[]{:S(2)}) collective-permute-start(f32[64,384]{1,0:T(8,128)S(1)} %long_pair.1.refs_0_), channel_id=1, source_target_pairs={{0,8},{4,12},{8,0},{12,4},{16,24},{20,28},{24,16},{28,20},{1,9},{5... | collective-permute-start | bytes 294920 | tf_op jit(solution)/shard_map/ppermute | solution.py:312
  25.8 1.8 %copy-start.4 = (bf16[3,4,320,320]{3,2,1,0:T(8,128)(2,1)S(1)}, bf16[3,4,320,320]{3,2,1,0:T(8,128)(2,1)}, u32[]{:S(2)}) copy-start(bf16[3,4,320,320]{3,2,1,0:T(8,128)(2,1)} %get-tuple-element.18.fresh_ref) | copy-start | bytes 7372804
  27.7 10.8 %copy-start.7 = (bf16[4,16,320]{2,1,0:T(8,128)(2,1)S(1)}, bf16[4,16,320]{2,1,0:T(8,128)(2,1)}, u32[]{:S(2)}) copy-start(bf16[4,16,320]{2,1,0:T(8,128)(2,1)} %get-tuple-element.19.q_ref.ql_ref) | copy-start | bytes 122884
  27.7 10.8 %copy-start.11 = (bf16[4,16,320]{2,1,0:T(8,128)(2,1)S(1)}, bf16[4,16,320]{2,1,0:T(8,128)(2,1)}, u32[]{:S(2)}) copy-start(bf16[4,16,320]{2,1,0:T(8,128)(2,1)} %get-tuple-element.20.knl_ref) | copy-start | bytes 122884
  27.7 10.8 %copy-start.12 = (bf16[4,16,320]{2,1,0:T(8,128)(2,1)S(1)}, bf16[4,16,320]{2,1,0:T(8,128)(2,1)}, u32[]{:S(2)}) copy-start(bf16[4,16,320]{2,1,0:T(8,128)(2,1)} %get-tuple-element.21.vnl_ref) | copy-start | bytes 122884
  34.7 43.3 %copy-start = (bf16[4,320,1280]{2,1,0:T(8,128)(2,1)S(1)}, bf16[4,320,1280]{2,1,0:T(8,128)(2,1)}, u32[]{:S(2)}) copy-start(bf16[4,320,1280]{2,1,0:T(8,128)(2,1)} %x_ref.3) | copy-start | bytes 9830404
  34.7 43.3 %copy-start.1 = (bf16[320,1280]{1,0:T(8,128)(2,1)S(1)}, bf16[320,1280]{1,0:T(8,128)(2,1)}, u32[]{:S(2)}) copy-start(bf16[320,1280]{1,0:T(8,128)(2,1)} %refs_4_.1) | copy-start | bytes 2457604
  34.7 43.3 %copy-start.2 = (bf16[1280,320]{0,1:T(8,128)(2,1)S(1)}, bf16[1280,320]{0,1:T(8,128)(2,1)}, u32[]{:S(2)}) copy-start(bf16[1280,320]{0,1:T(8,128)(2,1)} %param.32) | copy-start | bytes 2457604
  34.7 43.3 %copy-start.3 = (bf16[320,1280]{1,0:T(8,128)(2,1)S(1)}, bf16[320,1280]{1,0:T(8,128)(2,1)}, u32[]{:S(2)}) copy-start(bf16[320,1280]{1,0:T(8,128)(2,1)} %refs_6_.1) | copy-start | bytes 2457604
  34.7 43.3 %copy-start.5 = (bf16[4,12,1280]{2,0,1:T(4,128)(2,1)S(1)}, bf16[4,12,1280]{2,0,1:T(4,128)(2,1)}, u32[]{:S(2)}) copy-start(bf16[4,12,1280]{2,0,1:T(4,128)(2,1)} %param.18) | copy-start | bytes 368644
  34.7 43.3 %copy-start.13 = (f32[1280]{0:T(1024)S(1)}, f32[1280]{0:T(1024)}, u32[]{:S(2)}) copy-start(f32[1280]{0:T(1024)} %gain_ref.3) | copy-start | bytes 15364
  35.4 27.1 %collective-permute-start.13 = (bf16[9,80,640]{2,1,0:T(8,128)(2,1)S(1)}, bf16[9,80,640]{2,1,0:T(8,128)(2,1)S(1)}, u32[]{:S(2)}, u32[]{:S(2)}) collective-permute-start(bf16[9,80,640]{2,1,0:T(8,128)(2,1)S(1)} %stack_weights.1.refs_7_), channel_id=1, source_target_pairs={{0,16},{4,20},{8,24},{12,28},{16,0},{20,4},{24,8},{28,12},{1,17},{... | collective-permute-start | bytes 2764808 | tf_op jit(solution)/shard_map/ppermute | solution.py:312
  37.0 25.6 %collective-permute-start.11 = (bf16[9,80,640]{2,1,0:T(8,128)(2,1)S(1)}, bf16[9,80,640]{2,1,0:T(8,128)(2,1)S(1)}, u32[]{:S(2)}, u32[]{:S(2)}) collective-permute-start(bf16[9,80,640]{2,1,0:T(8,128)(2,1)S(1)} %stack_weights.1.refs_7_), channel_id=1, source_target_pairs={{0,8},{4,12},{8,0},{12,4},{16,24},{20,28},{24,16},{28,20},{1,9},{5... | collective-permute-start | bytes 2764808 | tf_op jit(solution)/shard_map/ppermute | solution.py:312
  40.6 8.5 %collective-permute-start.5 = (bf16[176,640]{1,0:T(8,128)(2,1)S(1)}, bf16[176,640]{1,0:T(8,128)(2,1)S(1)}, u32[]{:S(2)}, u32[]{:S(2)}) collective-permute-start(bf16[176,640]{1,0:T(8,128)(2,1)S(1)} %get-tuple-element.23), channel_id=1, source_target_pairs={{0,1},{1,0},{2,3},{3,2},{4,5},{5,4},{6,7},{7,6},{8,9},{9,8},{10,11... | collective-permute-start | bytes 675848 | tf_op jit(solution)/shard_map/ppermute | solution.py:312
  41.3 17.4 %collective-permute-start.6 = (bf16[176,640]{1,0:T(8,128)(2,1)S(1)}, bf16[176,640]{1,0:T(8,128)(2,1)S(1)}, u32[]{:S(2)}, u32[]{:S(2)}) collective-permute-start(bf16[176,640]{1,0:T(8,128)(2,1)S(1)} %get-tuple-element.24), channel_id=1, source_target_pairs={{0,2},{1,3},{2,0},{3,1},{4,6},{5,7},{6,4},{7,5},{8,10},{9,11},{10,... | collective-permute-start | bytes 675848 | tf_op jit(solution)/shard_map/ppermute | solution.py:312
  43.7 18.9 %collective-permute-start.7 = (bf16[176,640]{1,0:T(8,128)(2,1)S(1)}, bf16[176,640]{1,0:T(8,128)(2,1)S(1)}, u32[]{:S(2)}, u32[]{:S(2)}) collective-permute-start(bf16[176,640]{1,0:T(8,128)(2,1)S(1)} %get-tuple-element.25), channel_id=1, source_target_pairs={{0,3},{1,2},{2,1},{3,0},{4,7},{5,6},{6,5},{7,4},{8,11},{9,10},{10,... | collective-permute-start | bytes 675848 | tf_op jit(solution)/shard_map/ppermute | solution.py:312
  63.2 11.0 %collective-permute-start.15 = (bf16[5,80,640]{2,1,0:T(8,128)(2,1)S(1)}, bf16[5,80,640]{2,1,0:T(8,128)(2,1)S(1)}, u32[]{:S(2)}, u32[]{:S(2)}) collective-permute-start(bf16[5,80,640]{2,1,0:T(8,128)(2,1)S(1)} %get-tuple-element.26), channel_id=1, source_target_pairs={{0,8},{4,12},{8,0},{12,4},{16,24},{20,28},{24,16},{28,20},{1,9},{5... | collective-permute-start | bytes 1536008 | tf_op jit(solution)/shard_map/ppermute | solution.py:312
  63.8 12.4 %collective-permute-start.10 = (bf16[9,80,640]{2,1,0:T(8,128)(2,1)S(1)}, bf16[9,80,640]{2,1,0:T(8,128)(2,1)S(1)}, u32[]{:S(2)}, u32[]{:S(2)}) collective-permute-start(bf16[9,80,640]{2,1,0:T(8,128)(2,1)S(1)} %stack_weights.1.refs_7_), channel_id=1, source_target_pairs={{0,4},{4,0},{8,12},{12,8},{16,20},{20,16},{24,28},{28,24},{1,5},{5... | collective-permute-start | bytes 2764808 | tf_op jit(solution)/shard_map/ppermute | solution.py:312
  63.8 14.1 %collective-permute-start.14 = (bf16[9,80,640]{2,1,0:T(8,128)(2,1)S(1)}, bf16[9,80,640]{2,1,0:T(8,128)(2,1)S(1)}, u32[]{:S(2)}, u32[]{:S(2)}) collective-permute-start(bf16[9,80,640]{2,1,0:T(8,128)(2,1)S(1)} %collective-permute-done.13.y_ref.refs_11_), channel_id=1, source_target_pairs={{0,4},{4,0},{8,12},{12,8},{16,20},{20,16},{24,28},{28,24},{1,5},{5... | collective-permute-start | bytes 2764808 | tf_op jit(solution)/shard_map/ppermute | solution.py:312
  64.3 13.6 %collective-permute-start.12 = (bf16[9,80,640]{2,1,0:T(8,128)(2,1)S(1)}, bf16[9,80,640]{2,1,0:T(8,128)(2,1)S(1)}, u32[]{:S(2)}, u32[]{:S(2)}) collective-permute-start(bf16[9,80,640]{2,1,0:T(8,128)(2,1)S(1)} %collective-permute-done.11.x_ref.refs_9_), channel_id=1, source_target_pairs={{0,4},{4,0},{8,12},{12,8},{16,20},{20,16},{24,28},{28,24},{1,5},{5... | collective-permute-start | bytes 2764808 | tf_op jit(solution)/shard_map/ppermute | solution.py:312
  64.3 11.9 %collective-permute-start.17 = (bf16[4,80,640]{2,1,0:T(8,128)(2,1)S(1)}, bf16[4,80,640]{2,1,0:T(8,128)(2,1)S(1)}, u32[]{:S(2)}, u32[]{:S(2)}) collective-permute-start(bf16[4,80,640]{2,1,0:T(8,128)(2,1)S(1)} %get-tuple-element.27), channel_id=1, source_target_pairs={{0,16},{4,20},{8,24},{12,28},{16,0},{20,4},{24,8},{28,12},{1,17},{... | collective-permute-start | bytes 1228808 | tf_op jit(solution)/shard_map/ppermute | solution.py:312
  74.2 3.7 %collective-permute-start.16 = (bf16[5,80,640]{2,1,0:T(8,128)(2,1)S(1)}, bf16[5,80,640]{2,1,0:T(8,128)(2,1)S(1)}, u32[]{:S(2)}, u32[]{:S(2)}) collective-permute-start(bf16[5,80,640]{2,1,0:T(8,128)(2,1)S(1)} %collective-permute-done.15.refs_13_), channel_id=1, source_target_pairs={{0,4},{4,0},{8,12},{12,8},{16,20},{20,16},{24,28},{28,24},{1,5},{5... | collective-permute-start | bytes 1536008 | tf_op jit(solution)/shard_map/ppermute | solution.py:312
  76.2 1.7 %collective-permute-start.18 = (bf16[4,80,640]{2,1,0:T(8,128)(2,1)S(1)}, bf16[4,80,640]{2,1,0:T(8,128)(2,1)S(1)}, u32[]{:S(2)}, u32[]{:S(2)}) collective-permute-start(bf16[4,80,640]{2,1,0:T(8,128)(2,1)S(1)} %collective-permute-done.17.refs_15_), channel_id=1, source_target_pairs={{0,4},{4,0},{8,12},{12,8},{16,20},{20,16},{24,28},{28,24},{1,5},{5... | collective-permute-start | bytes 1228808 | tf_op jit(solution)/shard_map/ppermute | solution.py:312
  84.5 9.7 %collective-permute-start.19 = (bf16[176,640]{1,0:T(8,128)(2,1)S(1)}, bf16[176,640]{1,0:T(8,128)(2,1)S(1)}, u32[]{:S(2)}, u32[]{:S(2)}) collective-permute-start(bf16[176,640]{1,0:T(8,128)(2,1)S(1)} %get-tuple-element.29), channel_id=1, source_target_pairs={{0,1},{1,0},{2,3},{3,2},{4,5},{5,4},{6,7},{7,6},{8,9},{9,8},{10,11... | collective-permute-start | bytes 675848 | tf_op jit(solution)/shard_map/ppermute | solution.py:312
  84.6 18.6 %collective-permute-start.20 = (bf16[176,640]{1,0:T(8,128)(2,1)S(1)}, bf16[176,640]{1,0:T(8,128)(2,1)S(1)}, u32[]{:S(2)}, u32[]{:S(2)}) collective-permute-start(bf16[176,640]{1,0:T(8,128)(2,1)S(1)} %get-tuple-element.30), channel_id=1, source_target_pairs={{0,2},{1,3},{2,0},{3,1},{4,6},{5,7},{6,4},{7,5},{8,10},{9,11},{10,... | collective-permute-start | bytes 675848 | tf_op jit(solution)/shard_map/ppermute | solution.py:312
  87.6 20.2 %collective-permute-start.21 = (bf16[176,640]{1,0:T(8,128)(2,1)S(1)}, bf16[176,640]{1,0:T(8,128)(2,1)S(1)}, u32[]{:S(2)}, u32[]{:S(2)}) collective-permute-start(bf16[176,640]{1,0:T(8,128)(2,1)S(1)} %get-tuple-element.31), channel_id=1, source_target_pairs={{0,3},{1,2},{2,1},{3,0},{4,7},{5,6},{6,5},{7,4},{8,11},{9,10},{10,... | collective-permute-start | bytes 675848 | tf_op jit(solution)/shard_map/ppermute | solution.py:312
